TPU v7x, 128 devices: a whole 4x4x4 slice. The times are simulated.
128 devices in a mesh: dp: 2 (over core), row: 8 (over y_hi, x), col: 8 (over z, y_lo).
Axes of the slice: x: 4, y: 4 (y_hi: 2, y_lo: 2; y = y_hi * 2 + y_lo), z: 4, core: 2. Of those that a mesh axis runs over, the one named last changes fastest.
Arguments:
- block_input: bfloat16 [8192, 2048], P(('dp', 'row'), 'col'), may hold values from -6 to 6
- cotangent: bfloat16 [8192, 2048], P(('dp', 'row'), 'col'), may hold values from -6 to 6
- doc_lengths: int32 [16, 6], P(('dp', 'col')), may hold values from 1 to 384, as said below
- heads_weight: float32 [2048, 6144], P('col', 'row'), may hold values from -0.13258252 to 0.13258252
- heads_first: float32 [2048, 6144], P('col', 'row'), may hold values from -1024 to 1024
- heads_second: float32 [2048, 6144], P('col', 'row'), may hold values from 32768 to 131072
- merge_weight: float32 [2048, 2048], P('row', 'col'), may hold values from -0.13258252 to 0.13258252
- merge_first: float32 [2048, 2048], P('row', 'col'), may hold values from -1024 to 1024
- merge_second: float32 [2048, 2048], P('row', 'col'), may hold values from 32768 to 131072
- expand_weight: float32 [2048, 16384], P('col', 'row'), may hold values from -0.125 to 0.125
- expand_first: float32 [2048, 16384], P('col', 'row'), may hold values from -256 to 256
- expand_second: float32 [2048, 16384], P('col', 'row'), may hold values from 2048 to 8192
- reduce_weight: float32 [8192, 2048], P('row', 'col'), may hold values from -0.06629126 to 0.06629126
- reduce_first: float32 [8192, 2048], P('row', 'col'), may hold values from -512 to 512
- reduce_second: float32 [8192, 2048], P('row', 'col'), may hold values from 8192 to 32768
- norm_gains: float32 [4, 2048], replicated, may hold values from 0.5 to 1.5
- gains_first: float32 [4, 2048], replicated, may hold values from -768 to 768
- gains_second: float32 [4, 2048], replicated, may hold values from 16384 to 65536
Outputs:
- block_output: bfloat16 [8192, 2048], P(('dp', 'row'), 'col')
- input_grad: float32 [8192, 2048], P(('dp', 'row'), 'col')
- heads_grad: float32 [2048, 6144], P('col', 'row')
- heads_mean: float32 [2048, 6144], P('col', 'row')
- heads_square: float32 [2048, 6144], P('col', 'row')
- heads_fresh: float32 [2048, 6144], P('col', 'row')
- heads_copy: bfloat16 [2048, 6144], P('col', 'row')
- merge_grad: float32 [2048, 2048], P('row', 'col')
- merge_mean: float32 [2048, 2048], P('row', 'col')
- merge_square: float32 [2048, 2048], P('row', 'col')
- merge_fresh: float32 [2048, 2048], P('row', 'col')
- merge_copy: bfloat16 [2048, 2048], P('row', 'col')
- expand_grad: float32 [2048, 16384], P('col', 'row')
- expand_mean: float32 [2048, 16384], P('col', 'row')
- expand_square: float32 [2048, 16384], P('col', 'row')
- expand_fresh: float32 [2048, 16384], P('col', 'row')
- expand_copy: bfloat16 [2048, 16384], P('col', 'row')
- reduce_grad: float32 [8192, 2048], P('row', 'col')
- reduce_mean: float32 [8192, 2048], P('row', 'col')
- reduce_square: float32 [8192, 2048], P('row', 'col')
- reduce_fresh: float32 [8192, 2048], P('row', 'col')
- reduce_copy: bfloat16 [8192, 2048], P('row', 'col')
- gains_grad: float32 [4, 2048], replicated
- gains_mean: float32 [4, 2048], replicated
- gains_square: float32 [4, 2048], replicated
- gains_fresh: float32 [4, 2048], replicated
Inputs may be any that keep to these rules, and one draw needn't show every extreme that they name: `doc_lengths`: each row sums to 512; its last entry counts the padding tokens at the sequence's end; exactly one of the other entries is the largest, 384, and the rest together hold 128 tokens.
All inputs are finite; a program needn't handle non-finite values.
Results may differ from a plain program's by a relative error of at most 0.018.
Values may be sent and summed in bfloat16 or wider, within the bound.
A program may use at most 192 MiB of HBM per device.

v0:
```python
import jax
import jax.numpy as jnp
from jax import lax
from jax.sharding import PartitionSpec as P

HD = 128
WINDOW = 256
STEP = 5


EPS = 1e-06
THETA = 500000.0
LR = 0.02
LR_GAIN = 0.2
BETA_ONE = 0.5
BETA_TWO = 0.5
DECAY = 0.1
ADAM_EPS = 1e-08


def positions(lengths, row_count):
    doc_ends = jnp.cumsum(lengths)
    index_ids = jnp.arange(row_count, dtype=jnp.int32)
    passed = doc_ends[None, :] <= index_ids[:, None]
    doc_ids = jnp.sum(passed.astype(jnp.int32), axis=1)
    starts = jnp.sum(jnp.where(passed, lengths[None, :], 0), axis=1)
    live_rows = (doc_ids < lengths.shape[0] - 1).astype(jnp.float32)
    return (doc_ids, index_ids - starts, live_rows)


def rotate(values, places, turn_sign):
    half_dim = values.shape[-1] // 2
    frequency = THETA ** (-2.0 * jnp.arange(half_dim, dtype=jnp.float32) / values.shape[-1])
    angles = places.astype(jnp.float32)[:, None] * frequency[None, :]
    cosine = jnp.cos(angles)[:, None, :]
    sine_part = turn_sign * jnp.sin(angles)[:, None, :]
    first_half = values[..., :half_dim]
    second_half = values[..., half_dim:]
    return jnp.concatenate(
        [
            first_half * cosine - second_half * sine_part,
            second_half * cosine + first_half * sine_part,
        ],
        axis=-1,
    )


def allowed_mask(doc_ids, row_count):
    index_ids = jnp.arange(row_count, dtype=jnp.int32)
    distance = index_ids[:, None] - index_ids[None, :]
    return (doc_ids[:, None] == doc_ids[None, :]) & (distance >= 0) & (distance < WINDOW)


def product(left_side, right_side, flipped):
    if flipped:
        return lax.dot_general(
            left_side, right_side, (((1,), (1,)), ((), ())), preferred_element_type=jnp.float32
        )
    return jnp.dot(left_side, right_side, preferred_element_type=jnp.float32)


def column_total(left_side, right_side):
    return lax.dot_general(
        left_side, right_side, (((0,), (0,)), ((), ())), preferred_element_type=jnp.float32
    )


def across_cols(local_rows, weight, flipped):
    gathered = lax.all_gather(local_rows, "row", axis=0, tiled=True)

    def partial_rows(row_start, row_count):
        return product(gathered, weight, flipped)

    result = lax.psum_scatter(
        partial_rows(
            jnp.int32(0), lax.axis_size("col") * (gathered.shape[0] // lax.axis_size("col"))
        ),
        "col",
        scatter_dimension=0,
        tiled=True,
    )
    return (gathered, result)


def across_rows(local_rows, weight, flipped):
    gathered = lax.all_gather(local_rows, "col", axis=0, tiled=True)

    def partial_rows(row_start, row_count):
        return product(gathered, weight, flipped)

    result = lax.psum_scatter(
        partial_rows(
            jnp.int32(0), lax.axis_size("row") * (gathered.shape[0] // lax.axis_size("row"))
        ),
        "row",
        scatter_dimension=0,
        tiled=True,
    )
    return (gathered, result)


def head_sums(values):
    return lax.psum((values[0], values[1]), "row")


def width_sums(values):
    return lax.psum(values, "col")


def norm_back(grad_hat, hat_vals, rates, dots, model_width):
    return rates * (grad_hat - hat_vals * (dots / model_width)[:, None])


def attend_forward(queries, key_rows, value_rows, allowed, live_rows):
    score_scale = queries.shape[-1] ** (-0.5)
    scores = (
        jnp.einsum("qhd,khd->hqk", queries, key_rows, preferred_element_type=jnp.float32)
        * score_scale
    )
    scores = jnp.where(allowed[None], scores, -1e30)
    highest = jnp.max(scores, axis=-1, keepdims=True)
    weights = jnp.exp(scores - highest)
    totals = jnp.sum(weights, axis=-1, keepdims=True)
    shares = (weights / totals).astype(jnp.bfloat16)
    mixture = jnp.einsum("hqk,khd->qhd", shares, value_rows, preferred_element_type=jnp.float32)
    return (mixture * live_rows[:, None, None], highest + jnp.log(totals))


def attend_backward(queries, key_rows, value_rows, allowed, log_totals, grad_mix):
    score_scale = queries.shape[-1] ** (-0.5)
    scores = (
        jnp.einsum("qhd,khd->hqk", queries, key_rows, preferred_element_type=jnp.float32)
        * score_scale
    )
    scores = jnp.where(allowed[None], scores, -1e30)
    shares = jnp.exp(scores - log_totals)
    grad_shares = jnp.einsum(
        "qhd,khd->hqk", grad_mix, value_rows, preferred_element_type=jnp.float32
    )
    grad_values = jnp.einsum(
        "hqk,qhd->khd", shares.astype(jnp.bfloat16), grad_mix, preferred_element_type=jnp.float32
    )
    center = jnp.sum(shares * grad_shares, axis=-1, keepdims=True)
    grad_scores = (shares * (grad_shares - center)).astype(jnp.bfloat16)
    grad_queries = (
        jnp.einsum("hqk,khd->qhd", grad_scores, key_rows, preferred_element_type=jnp.float32)
        * score_scale
    )
    grad_keys = (
        jnp.einsum("hqk,qhd->khd", grad_scores, queries, preferred_element_type=jnp.float32)
        * score_scale
    )
    return (grad_queries, grad_keys, grad_values)


def adamw(weight, gradient, first_mom, second_mom, step_rate, decay_rate):
    mean_new = BETA_ONE * first_mom + (1.0 - BETA_ONE) * gradient
    square_new = BETA_TWO * second_mom + (1.0 - BETA_TWO) * gradient * gradient
    fix_one = 1.0 - BETA_ONE**STEP
    fix_two = 1.0 - BETA_TWO**STEP
    update = mean_new / fix_one / (jnp.sqrt(square_new / fix_two) + ADAM_EPS) + decay_rate * weight
    return (mean_new, square_new, weight - step_rate * update)


def on_device(
    block_input,
    cotangent,
    doc_lengths,
    heads_weight,
    heads_first,
    heads_second,
    merge_weight,
    merge_first,
    merge_second,
    expand_weight,
    expand_first,
    expand_second,
    reduce_weight,
    reduce_first,
    reduce_second,
    norm_gains,
    gains_first,
    gains_second,
):
    row_at = lax.axis_index("row")
    col_at = lax.axis_index("col")
    col_width = block_input.shape[1]
    model_width = col_width * lax.axis_size("col")
    head_width = merge_weight.shape[0]
    unit_width = reduce_weight.shape[0]
    seq_len = block_input.shape[0] * lax.axis_size("row") // lax.axis_size("col")
    head_count = head_width // HD
    doc_ids, places, live_rows = positions(doc_lengths[0], seq_len)
    allowed = allowed_mask(doc_ids, seq_len)
    heads_low = heads_weight.astype(jnp.bfloat16)
    merge_low = merge_weight.astype(jnp.bfloat16)
    expand_low = expand_weight.astype(jnp.bfloat16)
    reduce_low = reduce_weight.astype(jnp.bfloat16)
    gain_query = lax.dynamic_slice_in_dim(norm_gains[0], row_at * head_width, head_width)
    gain_key = lax.dynamic_slice_in_dim(norm_gains[1], row_at * head_width, head_width)
    gain_merge = lax.dynamic_slice_in_dim(norm_gains[2], col_at * col_width, col_width)
    gain_reduce = lax.dynamic_slice_in_dim(norm_gains[3], col_at * col_width, col_width)
    input_rows, joined_cols = across_cols(block_input, heads_low, False)
    queries = joined_cols[:, :head_width]
    key_rows = joined_cols[:, head_width : 2 * head_width]
    value_rows = joined_cols[:, 2 * head_width :]
    query_sq, key_sq = head_sums(
        (jnp.sum(queries * queries, axis=1), jnp.sum(key_rows * key_rows, axis=1))
    )
    query_rate = lax.rsqrt(query_sq / model_width + EPS)[:, None]
    key_rate = lax.rsqrt(key_sq / model_width + EPS)[:, None]
    query_hat = queries * query_rate
    key_hat = key_rows * key_rate
    query_low = rotate(
        (query_hat * gain_query).reshape(seq_len, head_count, HD), places, 1.0
    ).astype(jnp.bfloat16)
    key_low = rotate((key_hat * gain_key).reshape(seq_len, head_count, HD), places, 1.0).astype(
        jnp.bfloat16
    )
    value_low = value_rows.reshape(seq_len, head_count, HD).astype(jnp.bfloat16)
    mixture, log_totals = attend_forward(query_low, key_low, value_low, allowed, live_rows)
    mixture_low = mixture.reshape(seq_len, head_width).astype(jnp.bfloat16)
    mixture_rows, merged = across_rows(mixture_low, merge_low, False)
    merged_rate = lax.rsqrt(width_sums(jnp.sum(merged * merged, axis=1)) / model_width + EPS)[
        :, None
    ]
    merged_hat = merged * merged_rate
    residual = block_input.astype(jnp.float32) + merged_hat * gain_merge
    residual_rows, gated_cols = across_cols(residual.astype(jnp.bfloat16), expand_low, False)
    gate_vals = gated_cols[:, :unit_width]
    up_vals = gated_cols[:, unit_width:]
    activity = (jax.nn.silu(gate_vals) * up_vals).astype(jnp.bfloat16)
    activity_rows, reduced = across_rows(activity, reduce_low, False)
    reduced_rate = lax.rsqrt(width_sums(jnp.sum(reduced * reduced, axis=1)) / model_width + EPS)[
        :, None
    ]
    reduced_hat = reduced * reduced_rate
    block_output = residual + reduced_hat * gain_reduce
    grad_output = cotangent.astype(jnp.float32)
    reduce_gain_part = jnp.sum(grad_output * reduced_hat, axis=0)
    grad_hat = grad_output * gain_reduce
    grad_reduced = norm_back(
        grad_hat,
        reduced_hat,
        reduced_rate,
        width_sums(jnp.sum(grad_hat * reduced_hat, axis=1)),
        model_width,
    )
    reduced_grad_rows, grad_activity = across_cols(
        grad_reduced.astype(jnp.bfloat16), reduce_low, True
    )
    reduce_grad = column_total(activity_rows, reduced_grad_rows)
    sigmoid_vals = jax.nn.sigmoid(gate_vals)
    grad_gate = grad_activity * up_vals * sigmoid_vals * (1.0 + gate_vals * (1.0 - sigmoid_vals))
    grad_up = grad_activity * jax.nn.silu(gate_vals)
    gated_grad = jnp.concatenate([grad_gate, grad_up], axis=1).astype(jnp.bfloat16)
    gated_grad_rows, grad_branch = across_rows(gated_grad, expand_low, True)
    expand_grad = column_total(residual_rows, gated_grad_rows)
    grad_resid = grad_output + grad_branch
    merge_gain_part = jnp.sum(grad_resid * merged_hat, axis=0)
    merge_hat_grad = grad_resid * gain_merge
    grad_merged = norm_back(
        merge_hat_grad,
        merged_hat,
        merged_rate,
        width_sums(jnp.sum(merge_hat_grad * merged_hat, axis=1)),
        model_width,
    )
    merged_grad_rows, grad_mixture = across_cols(grad_merged.astype(jnp.bfloat16), merge_low, True)
    merge_grad = column_total(mixture_rows, merged_grad_rows)
    grad_mix_low = (
        grad_mixture.astype(jnp.bfloat16).reshape(seq_len, head_count, HD)
        * live_rows.astype(jnp.bfloat16)[:, None, None]
    )
    grad_queries, grad_keys, grad_values = attend_backward(
        query_low, key_low, value_low, allowed, log_totals, grad_mix_low
    )
    query_norm_grad = rotate(grad_queries, places, -1.0).reshape(seq_len, head_width)
    key_norm_grad = rotate(grad_keys, places, -1.0).reshape(seq_len, head_width)
    query_gain_part = jnp.sum(query_norm_grad * query_hat, axis=0)
    key_gain_part = jnp.sum(key_norm_grad * key_hat, axis=0)
    query_hat_grad = query_norm_grad * gain_query
    key_hat_grad = key_norm_grad * gain_key
    query_dot, key_dot = head_sums(
        (jnp.sum(query_hat_grad * query_hat, axis=1), jnp.sum(key_hat_grad * key_hat, axis=1))
    )
    grad_query_rows = norm_back(query_hat_grad, query_hat, query_rate, query_dot, model_width)
    grad_key_rows = norm_back(key_hat_grad, key_hat, key_rate, key_dot, model_width)
    joined_grad = jnp.concatenate(
        [grad_query_rows, grad_key_rows, grad_values.reshape(seq_len, head_width)], axis=1
    ).astype(jnp.bfloat16)
    joined_grad_rows, grad_input_branch = across_rows(joined_grad, heads_low, True)
    heads_grad = column_total(input_rows, joined_grad_rows)
    input_grad = grad_resid + grad_input_branch
    heads_grad, merge_grad, expand_grad, reduce_grad = (
        lax.psum(heads_grad.astype(jnp.bfloat16), "dp").astype(jnp.float32),
        lax.psum(merge_grad.astype(jnp.bfloat16), "dp").astype(jnp.float32),
        lax.psum(expand_grad.astype(jnp.bfloat16), "dp").astype(jnp.float32),
        lax.psum(reduce_grad.astype(jnp.bfloat16), "dp").astype(jnp.float32),
    )
    gain_parts = jnp.zeros((4, model_width), jnp.float32)
    gain_parts = lax.dynamic_update_slice(
        gain_parts, jnp.stack([query_gain_part, key_gain_part]), (jnp.int32(0), row_at * head_width)
    )
    gain_parts = lax.dynamic_update_slice(
        gain_parts,
        jnp.stack([merge_gain_part, reduce_gain_part]),
        (jnp.int32(2), col_at * col_width),
    )
    gains_grad = lax.psum(gain_parts, ("dp", "row", "col"))
    heads_mean, heads_square, heads_fresh = adamw(
        heads_weight, heads_grad, heads_first, heads_second, LR, DECAY
    )
    merge_mean, merge_square, merge_fresh = adamw(
        merge_weight, merge_grad, merge_first, merge_second, LR, DECAY
    )
    expand_mean, expand_square, expand_fresh = adamw(
        expand_weight, expand_grad, expand_first, expand_second, LR, DECAY
    )
    reduce_mean, reduce_square, reduce_fresh = adamw(
        reduce_weight, reduce_grad, reduce_first, reduce_second, LR, DECAY
    )
    gains_mean, gains_square, gains_fresh = adamw(
        norm_gains, gains_grad, gains_first, gains_second, LR_GAIN, 0.0
    )
    return (
        block_output.astype(jnp.bfloat16),
        input_grad,
        heads_grad,
        heads_mean,
        heads_square,
        heads_fresh,
        heads_fresh.astype(jnp.bfloat16),
        merge_grad,
        merge_mean,
        merge_square,
        merge_fresh,
        merge_fresh.astype(jnp.bfloat16),
        expand_grad,
        expand_mean,
        expand_square,
        expand_fresh,
        expand_fresh.astype(jnp.bfloat16),
        reduce_grad,
        reduce_mean,
        reduce_square,
        reduce_fresh,
        reduce_fresh.astype(jnp.bfloat16),
        gains_grad,
        gains_mean,
        gains_square,
        gains_fresh,
    )


def solution(mesh):
    return jax.shard_map(
        on_device,
        mesh=mesh,
        in_specs=(
            P(("dp", "row"), "col"),
            P(("dp", "row"), "col"),
            P(("dp", "col"), None),
            P("col", "row"),
            P("col", "row"),
            P("col", "row"),
            P("row", "col"),
            P("row", "col"),
            P("row", "col"),
            P("col", "row"),
            P("col", "row"),
            P("col", "row"),
            P("row", "col"),
            P("row", "col"),
            P("row", "col"),
            P(),
            P(),
            P(),
        ),
        out_specs=(
            P(("dp", "row"), "col"),
            P(("dp", "row"), "col"),
            P("col", "row"),
            P("col", "row"),
            P("col", "row"),
            P("col", "row"),
            P("col", "row"),
            P("row", "col"),
            P("row", "col"),
            P("row", "col"),
            P("row", "col"),
            P("row", "col"),
            P("col", "row"),
            P("col", "row"),
            P("col", "row"),
            P("col", "row"),
            P("col", "row"),
            P("row", "col"),
            P("row", "col"),
            P("row", "col"),
            P("row", "col"),
            P("row", "col"),
            P(),
            P(),
            P(),
            P(),
        ),
        check_vma=False,
    )
```

profile of v0, /device:TPU:9, one launch (start us, length us, event | category | flops | bytes accessed | tf_op | source)
XLA Modules:
  0.0 2813.6 jit_solution(17385808710673824584)
XLA Ops:
  8.0 57.4 %all-gather.9.cloned.1.call-done = bf16[4096,256]{1,0:T(8,128)(2,1)} async-done(((bf16[512,256]{1,0:T(8,128)(2,1)}), bf16[4096,256]{1,0:T(8,128)(2,1)}) %all-gather.9.cloned.1.call-update) | async-done | bytes 2097168 | tf_op jit(solution)/shard_map/all_gather | solution.py:69
  76.5 246.4 %reduce-scatter.9.cloned.1.call-done = f32[512,768]{1,0:T(8,128)} async-done(((f32[4096,768]{1,0:T(8,128)}), f32[512,768]{1,0:T(8,128)}) %reduce-scatter.9.cloned.1.call-update) | async-done | bytes 1572880 | tf_op jit(solution)/shard_map/reduce_scatter | solution.py:74
  324.3 19.8 all-reduce.1
  351.1 51.5 %all-gather.11.cloned.1.call-done = bf16[4096,256]{0,1:T(8,128)(2,1)} async-done(((bf16[512,256]{0,1:T(8,128)(2,1)}), bf16[4096,256]{0,1:T(8,128)(2,1)}) %all-gather.11.cloned.1.call-update) | async-done | bytes 2097168 | tf_op jit(solution)/shard_map/all_gather | solution.py:86
  407.0 83.9 %reduce-scatter.11.cloned.1.call-done = f32[512,256]{1,0:T(8,128)} async-done(((f32[4096,256]{1,0:T(8,128)}), f32[512,256]{1,0:T(8,128)}) %reduce-scatter.11.cloned.1.call-update) | async-done | bytes 524304 | tf_op jit(solution)/shard_map/reduce_scatter | solution.py:91
  492.1 13.9 psum.93
  508.4 56.6 %all-gather.13.cloned.1.call-done = bf16[4096,256]{1,0:T(8,128)(2,1)} async-done(((bf16[512,256]{1,0:T(8,128)(2,1)}), bf16[4096,256]{1,0:T(8,128)(2,1)}) %all-gather.13.cloned.1.call-update) | async-done | bytes 2097168 | tf_op jit(solution)/shard_map/all_gather | solution.py:69
  565.0 17.8 fusion.26
  582.9 642.3 %reduce-scatter.13.cloned.1.call-done = f32[512,2048]{1,0:T(8,128)} async-done(((f32[4096,2048]{1,0:T(8,128)}), f32[512,2048]{1,0:T(8,128)}) %reduce-scatter.13.cloned.1.call-update) | async-done | bytes 4194320 | tf_op jit(solution)/shard_map/reduce_scatter | solution.py:74
  1229.1 169.5 %all-gather.15.cloned.1.call-done = bf16[4096,1024]{1,0:T(8,128)(2,1)} async-done(((bf16[512,1024]{1,0:T(8,128)(2,1)}), bf16[4096,1024]{1,0:T(8,128)(2,1)}) %all-gather.15.cloned.1.call-update) | async-done | bytes 8388624 | tf_op jit(solution)/shard_map/all_gather | solution.py:86
  1406.3 84.0 %reduce-scatter.15.cloned.1.call-done = f32[512,256]{1,0:T(8,128)} async-done(((f32[4096,256]{1,0:T(8,128)}), f32[512,256]{1,0:T(8,128)}) %reduce-scatter.15.cloned.1.call-update) | async-done | bytes 524304 | tf_op jit(solution)/shard_map/reduce_scatter | solution.py:91
  1491.6 13.8 psum.94
  1506.7 15.4 psum.95
  1524.1 58.3 %all-gather.17.cloned.1.call-done = bf16[4096,256]{1,0:T(8,128)(2,1)} async-done(((bf16[512,256]{1,0:T(8,128)(2,1)}), bf16[4096,256]{1,0:T(8,128)(2,1)}) %all-gather.17.cloned.1.call-update) | async-done | bytes 2097168 | tf_op jit(solution)/shard_map/all_gather | solution.py:69
  1592.3 327.5 %reduce-scatter.17.cloned.1.call-done = f32[512,1024]{1,0:T(8,128)} async-done(((f32[4096,1024]{1,0:T(8,128)}), f32[512,1024]{1,0:T(8,128)}) %reduce-scatter.17.cloned.1.call-update) | async-done | bytes 2097168 | tf_op jit(solution)/shard_map/reduce_scatter | solution.py:74
  1925.6 326.7 %all-gather.19.cloned.1.call-done = bf16[4096,2048]{1,0:T(8,128)(2,1)} async-done(((bf16[512,2048]{1,0:T(8,128)(2,1)}), bf16[4096,2048]{1,0:T(8,128)(2,1)}) %all-gather.19.cloned.1.call-update) | async-done | bytes 16777232 | tf_op jit(solution)/shard_map/all_gather | solution.py:86
  2265.3 83.9 %reduce-scatter.19.cloned.1.call-done = f32[512,256]{1,0:T(8,128)} async-done(((f32[4096,256]{1,0:T(8,128)}), f32[512,256]{1,0:T(8,128)}) %reduce-scatter.19.cloned.1.call-update) | async-done | bytes 524304 | tf_op jit(solution)/shard_map/reduce_scatter | solution.py:91
  2350.5 13.9 psum.96
  2366.7 57.1 %all-gather.21.cloned.1.call-done = bf16[4096,256]{1,0:T(8,128)(2,1)} async-done(((bf16[512,256]{1,0:T(8,128)(2,1)}), bf16[4096,256]{1,0:T(8,128)(2,1)}) %all-gather.21.cloned.1.call-update) | async-done | bytes 2097168 | tf_op jit(solution)/shard_map/all_gather | solution.py:69
  2428.2 91.5 %reduce-scatter.21.cloned.1.call-done = f32[512,256]{1,0:T(8,128)} async-done(((f32[4096,256]{1,0:T(8,128)}), f32[512,256]{1,0:T(8,128)}) %reduce-scatter.21.cloned.1.call-update) | async-done | bytes 524304 | tf_op jit(solution)/shard_map/reduce_scatter | solution.py:74
  2528.4 19.9 all-reduce
  2571.2 111.9 %all-gather.23.cloned.1.call-done = bf16[4096,768]{1,0:T(8,128)(2,1)} async-done(((bf16[512,768]{1,0:T(8,128)(2,1)}), bf16[4096,768]{1,0:T(8,128)(2,1)}) %all-gather.23.cloned.1.call-update) | async-done | bytes 6291472 | tf_op jit(solution)/shard_map/all_gather | solution.py:86
  2699.0 66.1 %psum.103 = f32[4,2048]{1,0:T(4,128)S(1)} all-reduce(f32[4,2048]{1,0:T(4,128)S(1)} %maximum_dynamic-update-slice_fusion.1), channel_id=1, replica_groups=mesh['dp'=2,'row'=8,'col'=8] {'dp','row','col'}, use_global_device_ids=true, to_apply=%region_38.39 | all-reduce | flops 8192 | bytes 65536 | tf_op jit(solution)/shard_map/psum | solution.py:310
  2787.7 16.9 reduce-scatter.23.cloned.1.call-done
  (204 shorter events, 152.7 us)
Async XLA Ops:
  7.2 58.2 %all-gather.9.cloned.1.call-start = ((), (), s32[]{:S(2)}) async-start(), calls=%async_computation.8 | async-start | bytes 2359296 | tf_op jit(solution)/shard_map/all_gather | solution.py:69
  7.9 315.0 %reduce-scatter.9.cloned.1.call-start = ((), (), s32[]{:S(2)}) async-start(), calls=%async_computation.9 | async-start | bytes 14155776 | tf_op jit(solution)/shard_map/reduce_scatter | solution.py:74
  73.5 329.1 %all-gather.11.cloned.1.call-start = ((), (), s32[]{:S(2)}) async-start(), calls=%async_computation.10 | async-start | bytes 2359296 | tf_op jit(solution)/shard_map/all_gather | solution.py:86
  76.5 270.8 %copy-start.16 = (f32[512,64]{1,0:T(8,128)}, f32[512,64]{1,0:T(8,128)S(1)}, u32[]{:S(2)}) copy-start(f32[512,64]{1,0:T(8,128)S(1)} %get-tuple-element.152) | copy-start | bytes 393220
  351.0 139.9 %reduce-scatter.11.cloned.1.call-start = ((), (), s32[]{:S(2)}) async-start(), calls=%async_computation.11 | async-start | bytes 4718592 | tf_op jit(solution)/shard_map/reduce_scatter | solution.py:91
  406.9 99.1 %copy-start.18 = (bf16[512,256]{1,0:T(8,128)(2,1)S(1)}, bf16[512,256]{1,0:T(8,128)(2,1)}, u32[]{:S(2)}) copy-start(bf16[512,256]{1,0:T(8,128)(2,1)} %param.18) | copy-start | bytes 786436
  406.9 158.1 %all-gather.13.cloned.1.call-start = ((), (), s32[]{:S(2)}) async-start(), calls=%async_computation.12 | async-start | bytes 2359296 | tf_op jit(solution)/shard_map/all_gather | solution.py:69
  507.9 717.3 %reduce-scatter.13.cloned.1.call-start = ((), (), s32[]{:S(2)}) async-start(), calls=%async_computation.13 | async-start | bytes 37748736 | tf_op jit(solution)/shard_map/reduce_scatter | solution.py:74
  582.9 815.7 %copy-start.12 = (f32[1024,256]{1,0:T(8,128)S(1)}, f32[1024,256]{1,0:T(8,128)}, u32[]{:S(2)}) copy-start(f32[1024,256]{1,0:T(8,128)} %param.30) | copy-start | bytes 3145732
  582.9 815.7 %all-gather.15.cloned.1.call-start = ((), (), s32[]{:S(2)}) async-start(), calls=%async_computation.14 | async-start | bytes 9437184 | tf_op jit(solution)/shard_map/all_gather | solution.py:86
  1229.0 261.3 %reduce-scatter.15.cloned.1.call-start = ((), (), s32[]{:S(2)}) async-start(), calls=%async_computation.15 | async-start | bytes 4718592 | tf_op jit(solution)/shard_map/reduce_scatter | solution.py:91
  1406.2 99.1 %copy-start.7 = (bf16[512,256]{1,0:T(8,128)(2,1)S(1)}, bf16[512,256]{1,0:T(8,128)(2,1)}, u32[]{:S(2)}) copy-start(bf16[512,256]{1,0:T(8,128)(2,1)} %param.19) | copy-start | bytes 786436
  1406.3 176.1 %all-gather.17.cloned.1.call-start = ((), (), s32[]{:S(2)}) async-start(), calls=%async_computation.16 | async-start | bytes 2359296 | tf_op jit(solution)/shard_map/all_gather | solution.py:69
  1524.1 395.8 %reduce-scatter.17.cloned.1.call-start = ((), (), s32[]{:S(2)}) async-start(), calls=%async_computation.17 | async-start | bytes 18874368 | tf_op jit(solution)/shard_map/reduce_scatter | solution.py:74
  1592.1 660.2 %all-gather.19.cloned.1.call-start = ((), (), s32[]{:S(2)}) async-start(), calls=%async_computation.18 | async-start | bytes 18874368 | tf_op jit(solution)/shard_map/all_gather | solution.py:86
  1925.5 423.7 %reduce-scatter.19.cloned.1.call-start = ((), (), s32[]{:S(2)}) async-start(), calls=%async_computation.19 | async-start | bytes 4718592 | tf_op jit(solution)/shard_map/reduce_scatter | solution.py:91
  2265.2 84.0 %copy-start.3 = (f32[512,256]{1,0:T(8,128)S(1)}, f32[512,256]{1,0:T(8,128)}, u32[]{:S(2)}) copy-start(f32[512,256]{1,0:T(8,128)} %reduce-scatter.11.cloned.1.call-done) | copy-start | bytes 1572868
  2265.2 99.2 %copy-start.4 = (f32[512,256]{1,0:T(8,128)S(1)}, f32[512,256]{1,0:T(8,128)}, u32[]{:S(2)}) copy-start(f32[512,256]{1,0:T(8,128)} %reduce-scatter.15.cloned.1.call-done) | copy-start | bytes 1572868
  2265.2 158.5 %all-gather.21.cloned.1.call-start = ((), (), s32[]{:S(2)}) async-start(), calls=%async_computation.20 | async-start | bytes 2359296 | tf_op jit(solution)/shard_map/all_gather | solution.py:69
  2366.6 153.0 %reduce-scatter.21.cloned.1.call-start = ((), (), s32[]{:S(2)}) async-start(), calls=%async_computation.21 | async-start | bytes 4718592 | tf_op jit(solution)/shard_map/reduce_scatter | solution.py:74
  2428.1 255.0 %all-gather.23.cloned.1.call-start = ((), (), s32[]{:S(2)}) async-start(), calls=%async_computation.22 | async-start | bytes 7077888 | tf_op jit(solution)/shard_map/all_gather | solution.py:86
  2552.8 213.0 %all-reduce.5.cloned.1.call-start = ((), (), s32[]{:S(2)}) async-start(), calls=%async_computation.24 | async-start | bytes 4194304 | tf_op jit(solution)/shard_map/psum | solution.py:296
  2569.8 113.2 %copy-start.2 = (bf16[4096,256]{1,0:T(8,128)(2,1)S(1)}, bf16[4096,256]{1,0:T(8,128)(2,1)}, u32[]{:S(2)}) copy-start(bf16[4096,256]{1,0:T(8,128)(2,1)} %all-gather.9.cloned.1.call-done) | copy-start | bytes 6291460
  2688.4 116.2 %reduce-scatter.23.cloned.1.call-start = ((), (), s32[]{:S(2)}) async-start(), calls=%async_computation.23 | async-start | bytes 4718592 | tf_op jit(solution)/shard_map/reduce_scatter | solution.py:91
  (38 other events, 308.0 us)
Sparse Core Ops, SparseCore 0:
  10.4 54.9 all-gather.8
  73.6 249.2 reduce-scatter.8
  351.1 51.4 all-gather.10
  407.0 83.8 reduce-scatter.10
  508.0 56.9 all-gather.12
  583.0 642.1 reduce-scatter.12
  1229.1 169.3 all-gather.14
  1406.4 83.9 reduce-scatter.14
  1524.2 58.1 all-gather.16
  1592.2 327.5 reduce-scatter.16
  1925.6 326.5 all-gather.18
  2265.3 83.8 reduce-scatter.18
  2366.7 56.9 all-gather.20
  2428.2 91.3 reduce-scatter.20
  2552.9 130.0 all-gather.22
  2688.6 28.5 all-reduce.4
  2720.9 83.7 reduce-scatter.22
where the time goes:
time: 2820 us; the launch traced here: 2810 us
  waiting for transfers between devices  2470 us (88%)
  blocking collectives  163 us (6%)
  matrix products  102 us (4%)
  other arithmetic  46.5 us (2%)
    reduce_scatter x4, waiting for transfers between devices, across_cols(): lax.psum_scatter(partial_rows(jnp.int32(0), lax.axis_size('col') * (gathe...  1310 us
    all_gather x4, waiting for transfers between devices, across_rows(): gathered = lax.all_gather(local_rows, 'col', axis=0, tiled=True)  660 us
    reduce_scatter x4, waiting for transfers between devices, across_rows(): lax.psum_scatter(partial_rows(jnp.int32(0), lax.axis_size('row') * (gathe...  269 us
    all_gather x4, waiting for transfers between devices, across_cols(): gathered = lax.all_gather(local_rows, 'row', axis=0, tiled=True)  229 us
    psum x1, blocking collectives, on_device(): gains_grad = lax.psum(gain_parts, ('dp', 'row', 'col'))  66.1 us
    psum x4, blocking collectives, width_sums(): return lax.psum(values, 'col')  56.9 us
  transfers between devices with their start and end apart: 17, of which 16 were waited for; matrix products, arithmetic and copies ran while one was open for 2% of the time, Pallas kernels for 0%

commit v1 on v0

--- a/solution.py
+++ b/solution.py
@@ -1,6 +1,10 @@
+import functools
+
 import jax
 import jax.numpy as jnp
 from jax import lax
+from jax.experimental import pallas as pl
+from jax.experimental.pallas import tpu as pltpu
 from jax.sharding import PartitionSpec as P
 
 HD = 128
@@ -16,6 +20,13 @@
 BETA_TWO = 0.5
 DECAY = 0.1
 ADAM_EPS = 1e-08
+
+BF16 = jnp.bfloat16
+F32 = jnp.float32
+MESH = pl.DeviceIdType.MESH
+ANY = pl.BlockSpec(memory_space=pl.ANY)
+VMEM = pl.BlockSpec(memory_space=pltpu.VMEM)
+DMA = pltpu.SemaphoreType.DMA
 
 
 def positions(lengths, row_count):
@@ -65,48 +76,6 @@
     )
 
 
-def across_cols(local_rows, weight, flipped):
-    gathered = lax.all_gather(local_rows, "row", axis=0, tiled=True)
-
-    def partial_rows(row_start, row_count):
-        return product(gathered, weight, flipped)
-
-    result = lax.psum_scatter(
-        partial_rows(
-            jnp.int32(0), lax.axis_size("col") * (gathered.shape[0] // lax.axis_size("col"))
-        ),
-        "col",
-        scatter_dimension=0,
-        tiled=True,
-    )
-    return (gathered, result)
-
-
-def across_rows(local_rows, weight, flipped):
-    gathered = lax.all_gather(local_rows, "col", axis=0, tiled=True)
-
-    def partial_rows(row_start, row_count):
-        return product(gathered, weight, flipped)
-
-    result = lax.psum_scatter(
-        partial_rows(
-            jnp.int32(0), lax.axis_size("row") * (gathered.shape[0] // lax.axis_size("row"))
-        ),
-        "row",
-        scatter_dimension=0,
-        tiled=True,
-    )
-    return (gathered, result)
-
-
-def head_sums(values):
-    return lax.psum((values[0], values[1]), "row")
-
-
-def width_sums(values):
-    return lax.psum(values, "col")
-
-
 def norm_back(grad_hat, hat_vals, rates, dots, model_width):
     return rates * (grad_hat - hat_vals * (dots / model_width)[:, None])
 
@@ -160,6 +129,567 @@
     fix_two = 1.0 - BETA_TWO**STEP
     update = mean_new / fix_one / (jnp.sqrt(square_new / fix_two) + ADAM_EPS) + decay_rate * weight
     return (mean_new, square_new, weight - step_rate * update)
+
+
+def here():
+    return lax.axis_index("dp"), lax.axis_index("row"), lax.axis_index("col")
+
+
+def row_peer(row, d):
+    return (row // 4 + d // 4) % 2 * 4 + (row % 4 + d % 4) % 4
+
+
+def z_peer(col, d):
+    return (col // 2 + d) % 4 * 2 + col % 2
+
+
+def z_source(col, d):
+    return (col // 2 + 4 - d) % 4 * 2 + col % 2
+
+
+def y_peer(col):
+    return col // 2 * 2 + 1 - col % 2
+
+
+def remote(source, target, sent, arrived, **where):
+    return pltpu.make_async_remote_copy(
+        src_ref=source,
+        dst_ref=target,
+        send_sem=sent,
+        recv_sem=arrived,
+        device_id=where,
+        device_id_type=MESH,
+    )
+
+
+def meet(rows=False, cols=False, weights=False, spread_in=False, spread_out=False):
+    dp, row, col = here()
+    barrier = pltpu.get_barrier_semaphore()
+    count = 0
+
+    def greet(**where):
+        pl.semaphore_signal(barrier, inc=1, device_id=where, device_id_type=MESH)
+
+    if rows:
+        for d in range(1, 8):
+            greet(row=row_peer(row, d))
+        count = count + 7
+    if cols:
+        for d in range(1, 8):
+            greet(col=(col + d) % 8)
+        count = count + 7
+    if weights:
+        greet(col=y_peer(col))
+        for d in range(1, 4):
+            greet(col=z_peer(col, d))
+        greet(dp=1 - dp)
+        count = count + 5
+    for wanted, inward in ((spread_in, True), (spread_out, False)):
+        if wanted:
+            for k in range(8):
+                at_row, at_col = (col, k) if inward else (k, row)
+
+                @pl.when(jnp.logical_not((at_row == row) & (at_col == col)))
+                def _():
+                    greet(row=at_row, col=at_col)
+
+            count = count + 8 - (row == col).astype(jnp.int32)
+    pl.semaphore_wait(barrier, count)
+
+
+class Spread:
+    def __init__(self, inward, source, target, sent, arrived):
+        dp, row, col = here()
+        self.row, self.col, self.inward = row, col, inward
+        self.copies = []
+        for k in range(8):
+            to_row, to_col = (k, row) if inward else (col, k)
+            mine = (row == to_row) & (col == to_col)
+            copy = remote(
+                source(k),
+                target(col if inward else row),
+                sent.at[k],
+                arrived.at[col if inward else row],
+                row=to_row,
+                col=to_col,
+            )
+            waiter = remote(source(k), target(k), sent.at[k], arrived.at[k], row=to_row, col=to_col)
+            local = pltpu.make_async_copy(
+                source(k), target(col if inward else row), sent.at[k]
+            )
+            self.copies.append((mine, copy, waiter, local))
+
+    def start(self):
+        for mine, copy, _, local in self.copies:
+            pl.when(jnp.logical_not(mine))(copy.start)
+            pl.when(mine)(local.start)
+
+    def wait(self):
+        for k, (mine, copy, waiter, local) in enumerate(self.copies):
+            from_row, from_col = (self.col, k) if self.inward else (k, self.row)
+            me = (from_row == self.row) & (from_col == self.col)
+            pl.when(jnp.logical_not(me))(waiter.wait_recv)
+            pl.when(jnp.logical_not(mine))(copy.wait_send)
+            pl.when(mine)(local.wait)
+
+
+class RowScatter:
+    def __init__(self, part, arrived_rows, sent, arrived):
+        dp, self.row, col = here()
+        self.part, self.arrived_rows = part, arrived_rows
+        self.count = arrived_rows.shape[1]
+        self.copies = [
+            remote(
+                part.at[self.block(row_peer(self.row, d))],
+                arrived_rows.at[d - 1],
+                sent.at[d - 1],
+                arrived.at[d - 1],
+                row=row_peer(self.row, d),
+            )
+            for d in range(1, 8)
+        ]
+
+    def block(self, k):
+        return pl.ds(pl.multiple_of(k * self.count, self.count), self.count)
+
+    def start(self):
+        for copy in self.copies:
+            copy.start()
+
+    def total(self):
+        for copy in self.copies:
+            copy.wait_recv()
+        total = self.part[self.block(self.row)].astype(F32)
+        for d in range(7):
+            total = total + self.arrived_rows[d].astype(F32)
+        return total
+
+    def finish(self):
+        for copy in self.copies:
+            copy.wait_send()
+
+
+class RowGather:
+    def __init__(self, rows, whole, sent, arrived):
+        dp, row, col = here()
+        count = rows.shape[0]
+        block = pl.ds(pl.multiple_of(row * count, count), count)
+        self.copies = [
+            remote(rows, whole.at[block], sent.at[d - 1], arrived.at[d - 1], row=row_peer(row, d))
+            for d in range(1, 8)
+        ]
+        self.local = pltpu.make_async_copy(rows, whole.at[block], sent.at[7])
+
+    def start(self):
+        for copy in self.copies:
+            copy.start()
+        self.local.start()
+
+    def wait(self):
+        for copy in self.copies:
+            copy.wait()
+        self.local.wait()
+
+
+def half_of(kind, ref, c, h):
+    if kind == "tall":
+        count = ref.shape[0] // 16
+        return ref.at[pl.ds(pl.multiple_of((2 * c + h) * count, count), count)]
+    count, width = ref.shape[0] // 2, ref.shape[1] // 8
+    return ref.at[
+        pl.ds(pl.multiple_of(h * count, count), count), pl.ds(pl.multiple_of(c * width, width), width)
+    ]
+
+
+def half_shard(ref, h):
+    count = ref.shape[0] // 2
+    return ref.at[pl.ds(pl.multiple_of(h * count, count), count)]
+
+
+class WeightGather:
+    def __init__(self, kind, shard, whole, sent, arrived):
+        dp, _, col = here()
+        self.kind, self.whole, self.sent, self.arrived = kind, whole, sent, arrived
+        self.dp, self.col = dp, col
+        near = y_peer(col)
+        mine = half_shard(shard, dp)
+        self.local = [
+            pltpu.make_async_copy(half_shard(shard, h), self.half(col, h), sent.at[14 + h])
+            for h in range(2)
+        ]
+        self.first = [remote(mine, self.half(col, dp), sent.at[0], arrived.at[0], col=near)] + [
+            remote(mine, self.half(col, dp), sent.at[d], arrived.at[d], col=z_peer(col, d))
+            for d in range(1, 4)
+        ]
+        self.second = [
+            remote(
+                self.half(near, dp), self.half(near, dp), sent.at[3 + d], arrived.at[3 + d],
+                col=z_peer(col, d),
+            )
+            for d in range(1, 4)
+        ]
+        blocks = (
+            [near]
+            + [z_source(col, d) for d in range(1, 4)]
+            + [y_peer(z_source(col, d)) for d in range(1, 4)]
+        )
+        self.across = [
+            remote(self.half(b, dp), self.half(b, dp), sent.at[7 + i], arrived.at[7 + i], dp=1 - dp)
+            for i, b in enumerate(blocks)
+        ]
+
+    def half(self, c, h):
+        return half_of(self.kind, self.whole, c, h)
+
+    def start(self):
+        for copy in self.first + self.local:
+            copy.start()
+
+    def relay(self):
+        self.first[0].wait_recv()
+        for copy in self.second:
+            copy.start()
+        self.across[0].start()
+
+    def share(self):
+        for i in range(1, 4):
+            self.first[i].wait_recv()
+            self.across[i].start()
+        for i in range(3):
+            self.second[i].wait_recv()
+            self.across[4 + i].start()
+
+    def wait(self):
+        for copy in self.across:
+            copy.wait()
+        for copy in self.first + self.second:
+            copy.wait_send()
+        for copy in self.local:
+            copy.wait()
+
+
+def gather_sems(n):
+    return [DMA((n, 16)), DMA((n, 14))]
+
+
+class GradScatter:
+    def __init__(self, kind, part, out, own, other, far, near, sent, arrived):
+        dp, _, col = here()
+        self.dp, self.col = dp, col
+        self.own, self.other, self.far, self.near = own, other, far, near
+        self.load = [
+            pltpu.make_async_copy(half_of(kind, part, c, dp), own.at[c], sent.at[8 + c])
+            for c in range(8)
+        ]
+        self.core = [
+            remote(half_of(kind, part, c, 1 - dp), other.at[c], sent.at[c], arrived.at[c], dp=1 - dp)
+            for c in range(8)
+        ]
+        self.zs = [
+            remote(
+                own.at[pl.ds(z_peer(col, d) // 2 * 2, 2)], far.at[d - 1], sent.at[15 + d],
+                arrived.at[7 + d], col=z_peer(col, d),
+            )
+            for d in range(1, 4)
+        ]
+        self.ys = remote(near.at[0], near.at[1], sent.at[19], arrived.at[11], col=y_peer(col))
+        self.last = remote(
+            near.at[0], half_shard(out, dp), sent.at[20], arrived.at[12], dp=1 - dp
+        )
+        self.keep = pltpu.make_async_copy(near.at[0], half_shard(out, dp), sent.at[21])
+
+    def start(self):
+        for copy in self.load + self.core:
+            copy.start()
+
+    def each(self, rows, body):
+        @pl.loop(0, rows // 16)
+        def _(i):
+            body(pl.ds(pl.multiple_of(i * 16, 16), 16))
+
+    def over_z(self):
+        for c in range(8):
+            self.load[c].wait()
+            self.core[c].wait_recv()
+        rows = self.own.shape[1]
+
+        @pl.loop(0, 8)
+        def _(c):
+            def add(at):
+                self.own[c, at] = (self.own[c, at].astype(F32) + self.other[c, at].astype(F32)).astype(BF16)
+
+            self.each(rows, add)
+
+        for copy in self.zs:
+            copy.start()
+
+    def over_y(self):
+        for copy in self.zs:
+            copy.wait_recv()
+        rows = self.own.shape[1]
+        yl = self.col % 2
+
+        def total(at, c, k):
+            sums = self.own[c, at].astype(F32)
+            for d in range(3):
+                sums = sums + self.far[d, k, at].astype(F32)
+            return sums.astype(BF16)
+
+        def add(at):
+            self.near[0, at] = total(at, y_peer(self.col), 1 - yl)
+
+        self.each(rows, add)
+        self.ys.start()
+        for copy in self.zs:
+            copy.wait_send()
+
+        def keep(at):
+            self.own[self.col, at] = total(at, self.col, yl)
+
+        self.each(rows, keep)
+
+    def over_core(self):
+        self.ys.wait()
+        rows = self.own.shape[1]
+
+        def add(at):
+            self.near[0, at] = (self.own[self.col, at].astype(F32) + self.near[1, at].astype(F32)).astype(BF16)
+
+        self.each(rows, add)
+        self.last.start()
+        self.keep.start()
+
+    def wait(self):
+        for copy in self.core:
+            copy.wait_send()
+        self.last.wait()
+        self.keep.wait()
+
+
+def grad_scratch(rows, width):
+    return [
+        pltpu.VMEM((8, rows, width), BF16),
+        pltpu.VMEM((8, rows, width), BF16),
+        pltpu.VMEM((3, 2, rows, width), BF16),
+        pltpu.VMEM((2, rows, width), BF16),
+        DMA((22,)),
+        DMA((13,)),
+    ]
+
+
+def mean_rate(values):
+    return lax.rsqrt(jnp.mean(values * values, axis=-1, keepdims=True) + EPS)
+
+
+def call(kernel, name, number, outs, ins, in_specs, out_specs, scratch):
+    return pl.pallas_call(
+        kernel,
+        name=name,
+        out_shape=outs,
+        in_specs=in_specs,
+        out_specs=out_specs,
+        scratch_shapes=scratch,
+        compiler_params=pltpu.CompilerParams(
+            collective_id=number, has_side_effects=True, vmem_limit_bytes=56 * 2**20
+        ),
+    )(*ins)
+
+
+def struct(shape, kind):
+    return jax.ShapeDtypeStruct(shape, kind)
+
+
+def cols(ref, k, width):
+    return ref.at[:, pl.ds(pl.multiple_of(k * width, width), width)]
+
+
+def rows_of(ref, k, count):
+    return ref.at[pl.ds(pl.multiple_of(k * count, count), count)]
+
+
+def bring_kernel(x, g, heads, merge, xs, gs, heads_all, merge_all, xsent, xcame, gsent, gcame, wsent, wcame):
+    meet(weights=True, spread_in=True)
+    spread_x = Spread(True, lambda k: x, lambda k: cols(xs, k, 256), xsent, xcame)
+    spread_g = Spread(True, lambda k: rows_of(g, k, 64), lambda k: cols(gs, k, 256), gsent, gcame)
+    gathers = [
+        WeightGather("tall", heads, heads_all, wsent.at[0], wcame.at[0]),
+        WeightGather("wide", merge, merge_all, wsent.at[1], wcame.at[1]),
+    ]
+    spread_x.start()
+    for gather in gathers:
+        gather.start()
+    spread_g.start()
+    for gather in gathers:
+        gather.relay()
+    for gather in gathers:
+        gather.share()
+    spread_x.wait()
+    spread_g.wait()
+    for gather in gathers:
+        gather.wait()
+
+
+def sums_kernel(part, out, came, sent, arrived):
+    dp, row, col = here()
+    meet(rows=True)
+    copies = [
+        remote(part, came.at[d - 1], sent.at[d - 1], arrived.at[d - 1], row=row_peer(row, d))
+        for d in range(1, 8)
+    ]
+    for copy in copies:
+        copy.start()
+    total = part[...]
+    for d, copy in enumerate(copies):
+        copy.wait_recv()
+        total = total + came[d]
+    out[...] = total
+    for copy in copies:
+        copy.wait_send()
+
+
+def merged_kernel(
+    part, x, gain, expand, reduce, merged, residual, rows_all, expand_all, reduce_all,
+    came, mine, ssent, scame, gsent, gcame, wsent, wcame,
+):
+    meet(rows=True, weights=True)
+    scatter = RowScatter(part, came, ssent, scame)
+    gather = RowGather(mine, rows_all, gsent, gcame)
+    weights = [
+        WeightGather("tall", expand, expand_all, wsent.at[0], wcame.at[0]),
+        WeightGather("wide", reduce, reduce_all, wsent.at[1], wcame.at[1]),
+    ]
+    scatter.start()
+    for weight in weights:
+        weight.start()
+    for weight in weights:
+        weight.relay()
+    total = scatter.total()
+    merged[...] = total
+    result = x[...].astype(F32) + total * mean_rate(total) * gain[...]
+    residual[...] = result
+    mine[...] = result.astype(BF16)
+    gather.start()
+    for weight in weights:
+        weight.share()
+    scatter.finish()
+    gather.wait()
+    for weight in weights:
+        weight.wait()
+
+
+def back_of(grad, values, gain):
+    rate = mean_rate(values)
+    hat = values * rate
+    grad_hat = grad * gain
+    dots = jnp.mean(grad_hat * hat, axis=-1, keepdims=True)
+    return hat, rate * (grad_hat - hat * dots)
+
+
+def reduced_kernel(
+    part, residual, g, gain, out, rows_all, gain_part,
+    came, mine, done, ssent, scame, gsent, gcame, osent, ocame,
+):
+    meet(rows=True, spread_out=True)
+    scatter = RowScatter(part, came, ssent, scame)
+    gather = RowGather(mine, rows_all, gsent, gcame)
+    spread = Spread(False, lambda k: cols(done, k, 256), lambda k: rows_of(out, k, 64), osent, ocame)
+    scatter.start()
+    total = scatter.total()
+    grad = g[...].astype(F32)
+    hat, back = back_of(grad, total, gain[...])
+    mine[...] = back.astype(BF16)
+    gather.start()
+    done[...] = (residual[...] + hat * gain[...]).astype(BF16)
+    spread.start()
+    gain_part[...] = jnp.sum(grad * hat, axis=0, keepdims=True)
+    scatter.finish()
+    gather.wait()
+    spread.wait()
+
+
+def branch_kernel(
+    part, g, merged, gain, expand_part, grad_resid, rows_all, gain_part, expand_grad,
+    came, mine, ssent, scame, gsent, gcame, *grad_refs,
+):
+    meet(rows=True, weights=True)
+    scatter = RowScatter(part, came, ssent, scame)
+    gather = RowGather(mine, rows_all, gsent, gcame)
+    expand = GradScatter("tall", expand_part, expand_grad, *grad_refs)
+    scatter.start()
+    expand.start()
+    expand.over_z()
+    grad = g[...].astype(F32) + scatter.total()
+    grad_resid[...] = grad
+    hat, back = back_of(grad, merged[...], gain[...])
+    mine[...] = back.astype(BF16)
+    gather.start()
+    gain_part[...] = jnp.sum(grad * hat, axis=0, keepdims=True)
+    scatter.finish()
+    expand.over_y()
+    expand.over_core()
+    gather.wait()
+    expand.wait()
+
+
+def last_kernel(
+    part, grad_resid, gains, heads_part, merge_part, reduce_part,
+    input_grad, gains_grad, heads_grad, merge_grad, reduce_grad,
+    came, done, grow, gcol, gcore, gsum, ssent, scame, osent, ocame, gsent, gcame, *grad_refs,
+):
+    dp, row, col = here()
+    meet(rows=True, cols=True, weights=True, spread_out=True)
+    scatter = RowScatter(part, came, ssent, scame)
+    spread = Spread(False, lambda k: cols(done, k, 256), lambda k: rows_of(input_grad, k, 64), osent, ocame)
+    grads = [
+        GradScatter("wide", reduce_part, reduce_grad, *grad_refs[:6]),
+        GradScatter("tall", heads_part, heads_grad, *grad_refs[6:12]),
+        GradScatter("wide", merge_part, merge_grad, *grad_refs[12:]),
+    ]
+    row_sums = [
+        remote(gains, grow.at[row], gsent.at[d - 1], gcame.at[d - 1], row=row_peer(row, d))
+        for d in range(1, 8)
+    ]
+    col_sums = [
+        remote(gsum.at[0], gcol.at[col], gsent.at[6 + d], gcame.at[6 + d], col=(col + d) % 8)
+        for d in range(1, 8)
+    ]
+    core_sum = remote(gsum.at[1], gcore, gsent.at[14], gcame.at[14], dp=1 - dp)
+    for copy in row_sums:
+        copy.start()
+    scatter.start()
+    for grad in grads:
+        grad.start()
+    grow[row] = gains[...]
+    for grad in grads:
+        grad.over_z()
+    for copy in row_sums:
+        copy.wait()
+    total = grow[0]
+    for k in range(1, 8):
+        total = total + grow[k]
+    gsum[0] = total
+    for copy in col_sums:
+        copy.start()
+    gcol[col] = total
+    done[...] = grad_resid[...] + scatter.total()
+    spread.start()
+    for copy in col_sums:
+        copy.wait()
+    total = gcol[0]
+    for k in range(1, 8):
+        total = total + gcol[k]
+    gsum[1] = total
+    core_sum.start()
+    for grad in grads:
+        grad.over_y()
+    for grad in grads:
+        grad.over_core()
+    core_sum.wait()
+    gains_grad[...] = total + gcore[...]
+    scatter.finish()
+    spread.wait()
+    for grad in grads:
+        grad.wait()
 
 
 def on_device(
@@ -183,29 +713,53 @@
     gains_second,
 ):
     row_at = lax.axis_index("row")
-    col_at = lax.axis_index("col")
     col_width = block_input.shape[1]
     model_width = col_width * lax.axis_size("col")
     head_width = merge_weight.shape[0]
     unit_width = reduce_weight.shape[0]
     seq_len = block_input.shape[0] * lax.axis_size("row") // lax.axis_size("col")
+    share = seq_len // lax.axis_size("row")
     head_count = head_width // HD
     doc_ids, places, live_rows = positions(doc_lengths[0], seq_len)
     allowed = allowed_mask(doc_ids, seq_len)
-    heads_low = heads_weight.astype(jnp.bfloat16)
-    merge_low = merge_weight.astype(jnp.bfloat16)
-    expand_low = expand_weight.astype(jnp.bfloat16)
-    reduce_low = reduce_weight.astype(jnp.bfloat16)
     gain_query = lax.dynamic_slice_in_dim(norm_gains[0], row_at * head_width, head_width)
     gain_key = lax.dynamic_slice_in_dim(norm_gains[1], row_at * head_width, head_width)
-    gain_merge = lax.dynamic_slice_in_dim(norm_gains[2], col_at * col_width, col_width)
-    gain_reduce = lax.dynamic_slice_in_dim(norm_gains[3], col_at * col_width, col_width)
-    input_rows, joined_cols = across_cols(block_input, heads_low, False)
+    gain_merge, gain_reduce = norm_gains[2:3], norm_gains[3:4]
+    rows_shape = struct((seq_len, model_width), BF16)
+    mine_f32 = struct((share, model_width), F32)
+    line = struct((1, model_width), F32)
+    row_scratch = [
+        pltpu.VMEM((7, share, model_width), BF16),
+        pltpu.VMEM((share, model_width), BF16),
+        DMA((7,)),
+        DMA((7,)),
+        DMA((8,)),
+        DMA((7,)),
+    ]
+
+    input_rows, cot_share, heads_low, merge_low = call(
+        bring_kernel, "bring", 1,
+        [rows_shape, struct((share, model_width), BF16), struct((model_width, 3 * head_width), BF16),
+         struct((head_width, model_width), BF16)],
+        [block_input, cotangent, heads_weight.astype(BF16), merge_weight.astype(BF16)],
+        [ANY] * 4, [ANY] * 4,
+        [DMA((8,)), DMA((8,)), DMA((8,)), DMA((8,))] + gather_sems(2),
+    )
+    joined_cols = product(input_rows, heads_low, False)
     queries = joined_cols[:, :head_width]
     key_rows = joined_cols[:, head_width : 2 * head_width]
     value_rows = joined_cols[:, 2 * head_width :]
+
+    def head_sums(one, two, number):
+        part = jnp.concatenate([one, two]).reshape(8, 128)
+        total = call(
+            sums_kernel, "sums", number, struct((8, 128), F32), [part], [VMEM], VMEM,
+            [pltpu.VMEM((7, 8, 128), F32), DMA((7,)), DMA((7,))],
+        ).reshape(2, seq_len)
+        return total[0], total[1]
+
     query_sq, key_sq = head_sums(
-        (jnp.sum(queries * queries, axis=1), jnp.sum(key_rows * key_rows, axis=1))
+        jnp.sum(queries * queries, axis=1), jnp.sum(key_rows * key_rows, axis=1), 2
     )
     query_rate = lax.rsqrt(query_sq / model_width + EPS)[:, None]
     key_rate = lax.rsqrt(key_sq / model_width + EPS)[:, None]
@@ -220,54 +774,48 @@
     value_low = value_rows.reshape(seq_len, head_count, HD).astype(jnp.bfloat16)
     mixture, log_totals = attend_forward(query_low, key_low, value_low, allowed, live_rows)
     mixture_low = mixture.reshape(seq_len, head_width).astype(jnp.bfloat16)
-    mixture_rows, merged = across_rows(mixture_low, merge_low, False)
-    merged_rate = lax.rsqrt(width_sums(jnp.sum(merged * merged, axis=1)) / model_width + EPS)[
-        :, None
-    ]
-    merged_hat = merged * merged_rate
-    residual = block_input.astype(jnp.float32) + merged_hat * gain_merge
-    residual_rows, gated_cols = across_cols(residual.astype(jnp.bfloat16), expand_low, False)
+    merged_part = product(mixture_low, merge_low, False).astype(BF16)
+
+    input_share = lax.dynamic_slice_in_dim(input_rows, row_at * share, share)
+    merged, residual, residual_rows, expand_low, reduce_low = call(
+        merged_kernel, "merged", 3,
+        [mine_f32, mine_f32, rows_shape, struct((model_width, 2 * unit_width), BF16),
+         struct((unit_width, model_width), BF16)],
+        [merged_part, input_share, gain_merge, expand_weight.astype(BF16), reduce_weight.astype(BF16)],
+        [VMEM, VMEM, VMEM, ANY, ANY], [VMEM, VMEM, ANY, ANY, ANY],
+        row_scratch + gather_sems(2),
+    )
+    gated_cols = product(residual_rows, expand_low, False)
     gate_vals = gated_cols[:, :unit_width]
     up_vals = gated_cols[:, unit_width:]
     activity = (jax.nn.silu(gate_vals) * up_vals).astype(jnp.bfloat16)
-    activity_rows, reduced = across_rows(activity, reduce_low, False)
-    reduced_rate = lax.rsqrt(width_sums(jnp.sum(reduced * reduced, axis=1)) / model_width + EPS)[
-        :, None
-    ]
-    reduced_hat = reduced * reduced_rate
-    block_output = residual + reduced_hat * gain_reduce
-    grad_output = cotangent.astype(jnp.float32)
-    reduce_gain_part = jnp.sum(grad_output * reduced_hat, axis=0)
-    grad_hat = grad_output * gain_reduce
-    grad_reduced = norm_back(
-        grad_hat,
-        reduced_hat,
-        reduced_rate,
-        width_sums(jnp.sum(grad_hat * reduced_hat, axis=1)),
-        model_width,
-    )
-    reduced_grad_rows, grad_activity = across_cols(
-        grad_reduced.astype(jnp.bfloat16), reduce_low, True
-    )
-    reduce_grad = column_total(activity_rows, reduced_grad_rows)
+    reduced_part = product(activity, reduce_low, False).astype(BF16)
+
+    block_output, reduced_grad_rows, reduce_gain_part = call(
+        reduced_kernel, "reduced", 4,
+        [struct(block_input.shape, BF16), rows_shape, line],
+        [reduced_part, residual, cot_share, gain_reduce],
+        [VMEM] * 4, [ANY, ANY, VMEM],
+        row_scratch[:2] + [pltpu.VMEM((share, model_width), BF16)] + row_scratch[2:] + [DMA((8,)), DMA((8,))],
+    )
+    grad_activity = product(reduced_grad_rows, reduce_low, True)
     sigmoid_vals = jax.nn.sigmoid(gate_vals)
     grad_gate = grad_activity * up_vals * sigmoid_vals * (1.0 + gate_vals * (1.0 - sigmoid_vals))
     grad_up = grad_activity * jax.nn.silu(gate_vals)
     gated_grad = jnp.concatenate([grad_gate, grad_up], axis=1).astype(jnp.bfloat16)
-    gated_grad_rows, grad_branch = across_rows(gated_grad, expand_low, True)
-    expand_grad = column_total(residual_rows, gated_grad_rows)
-    grad_resid = grad_output + grad_branch
-    merge_gain_part = jnp.sum(grad_resid * merged_hat, axis=0)
-    merge_hat_grad = grad_resid * gain_merge
-    grad_merged = norm_back(
-        merge_hat_grad,
-        merged_hat,
-        merged_rate,
-        width_sums(jnp.sum(merge_hat_grad * merged_hat, axis=1)),
-        model_width,
-    )
-    merged_grad_rows, grad_mixture = across_cols(grad_merged.astype(jnp.bfloat16), merge_low, True)
-    merge_grad = column_total(mixture_rows, merged_grad_rows)
+    branch_part = product(gated_grad, expand_low, True).astype(BF16)
+    expand_part = column_total(residual_rows, gated_grad).astype(BF16)
+    reduce_part = column_total(activity, reduced_grad_rows).astype(BF16)
+
+    grad_resid, merged_grad_rows, merge_gain_part, expand_grad = call(
+        branch_kernel, "branch", 5,
+        [mine_f32, rows_shape, line, struct(expand_weight.shape, BF16)],
+        [branch_part, cot_share, merged, gain_merge, expand_part],
+        [VMEM] * 4 + [ANY], [VMEM, ANY, VMEM, ANY],
+        row_scratch + grad_scratch(expand_weight.shape[0] // 2, expand_weight.shape[1]),
+    )
+    grad_mixture = product(merged_grad_rows, merge_low, True)
+    merge_part = column_total(mixture_low, merged_grad_rows).astype(BF16)
     grad_mix_low = (
         grad_mixture.astype(jnp.bfloat16).reshape(seq_len, head_count, HD)
         * live_rows.astype(jnp.bfloat16)[:, None, None]
@@ -282,32 +830,39 @@
     query_hat_grad = query_norm_grad * gain_query
     key_hat_grad = key_norm_grad * gain_key
     query_dot, key_dot = head_sums(
-        (jnp.sum(query_hat_grad * query_hat, axis=1), jnp.sum(key_hat_grad * key_hat, axis=1))
+        jnp.sum(query_hat_grad * query_hat, axis=1), jnp.sum(key_hat_grad * key_hat, axis=1), 6
     )
     grad_query_rows = norm_back(query_hat_grad, query_hat, query_rate, query_dot, model_width)
     grad_key_rows = norm_back(key_hat_grad, key_hat, key_rate, key_dot, model_width)
     joined_grad = jnp.concatenate(
         [grad_query_rows, grad_key_rows, grad_values.reshape(seq_len, head_width)], axis=1
     ).astype(jnp.bfloat16)
-    joined_grad_rows, grad_input_branch = across_rows(joined_grad, heads_low, True)
-    heads_grad = column_total(input_rows, joined_grad_rows)
-    input_grad = grad_resid + grad_input_branch
-    heads_grad, merge_grad, expand_grad, reduce_grad = (
-        lax.psum(heads_grad.astype(jnp.bfloat16), "dp").astype(jnp.float32),
-        lax.psum(merge_grad.astype(jnp.bfloat16), "dp").astype(jnp.float32),
-        lax.psum(expand_grad.astype(jnp.bfloat16), "dp").astype(jnp.float32),
-        lax.psum(reduce_grad.astype(jnp.bfloat16), "dp").astype(jnp.float32),
-    )
-    gain_parts = jnp.zeros((4, model_width), jnp.float32)
+    input_part = product(joined_grad, heads_low, True).astype(BF16)
+    heads_part = column_total(input_rows, joined_grad).astype(BF16)
+    gain_parts = jnp.zeros((2, model_width), jnp.float32)
     gain_parts = lax.dynamic_update_slice(
         gain_parts, jnp.stack([query_gain_part, key_gain_part]), (jnp.int32(0), row_at * head_width)
     )
-    gain_parts = lax.dynamic_update_slice(
-        gain_parts,
-        jnp.stack([merge_gain_part, reduce_gain_part]),
-        (jnp.int32(2), col_at * col_width),
-    )
-    gains_grad = lax.psum(gain_parts, ("dp", "row", "col"))
+    gain_parts = jnp.concatenate([gain_parts, merge_gain_part, reduce_gain_part]).reshape(8, model_width // 2)
+    gain_shape = (8, model_width // 2)
+
+    input_grad, gains_grad, heads_grad, merge_grad, reduce_grad = call(
+        last_kernel, "last", 7,
+        [struct(block_input.shape, F32), struct(gain_shape, F32), struct(heads_weight.shape, BF16),
+         struct(merge_weight.shape, BF16), struct(reduce_weight.shape, BF16)],
+        [input_part, grad_resid, gain_parts, heads_part, merge_part, reduce_part],
+        [VMEM] * 3 + [ANY] * 3, [ANY, VMEM] + [ANY] * 3,
+        [row_scratch[0], pltpu.VMEM((share, model_width), F32), pltpu.VMEM((8, *gain_shape), F32),
+         pltpu.VMEM((8, *gain_shape), F32), pltpu.VMEM(gain_shape, F32), pltpu.VMEM((2, *gain_shape), F32),
+         DMA((7,)), DMA((7,)), DMA((8,)), DMA((8,)), DMA((15,)), DMA((15,))]
+        + grad_scratch(reduce_weight.shape[0] // 2, reduce_weight.shape[1])
+        + grad_scratch(heads_weight.shape[0] // 2, heads_weight.shape[1])
+        + grad_scratch(merge_weight.shape[0] // 2, merge_weight.shape[1]),
+    )
+    gains_grad = gains_grad.reshape(4, model_width)
+    heads_grad, merge_grad, expand_grad, reduce_grad = (
+        heads_grad.astype(F32), merge_grad.astype(F32), expand_grad.astype(F32), reduce_grad.astype(F32)
+    )
     heads_mean, heads_square, heads_fresh = adamw(
         heads_weight, heads_grad, heads_first, heads_second, LR, DECAY
     )
@@ -324,7 +879,7 @@
         norm_gains, gains_grad, gains_first, gains_second, LR_GAIN, 0.0
     )
     return (
-        block_output.astype(jnp.bfloat16),
+        block_output,
         input_grad,
         heads_grad,
         heads_mean,

time: 2820 us -> 542 us (0.19)
  waiting for transfers between devices: 2470 us -> 0 us
  Pallas kernels: 0 us -> 423 us
  blocking collectives: 163 us -> 0 us
  matrix products: 102 us -> 64.7 us
    reduce_scatter x8 -> x0, waiting for transfers between devices: 1580 us -> none  [the longest x4 1310 us: across_cols(): lax.psum_scatter(partial_rows(jnp.int32(0), lax.axis_size('col') * (gathe...]
    all_gather x8 -> x0, waiting for transfers between devices: 889 us -> none  [the longest x4 660 us: across_rows(): gathered = lax.all_gather(local_rows, 'col', axis=0, tiled=True)]
    pallas_call x0 -> x7, Pallas kernels: none -> 423 us  [call(): pl.pallas_call(kernel, name=name, out_shape=outs, in_specs=in_specs, out_...]
    psum x7 -> x0, blocking collectives: 163 us -> none  [the longest x1 66.1 us: on_device(): gains_grad = lax.psum(gain_parts, ('dp', 'row', 'col'))]
  transfers between devices with their start and end apart: 17 -> 0, of which waited for: 16 -> 0; matrix products, arithmetic and copies ran while one was open for 2% -> 0% of each run, Pallas kernels for 0% -> 0%
where the time goes in v1:
time: 542 us; the launch traced here: 534 us
  Pallas kernels  423 us (78%)
  matrix products  64.7 us (12%)
  other arithmetic  28.7 us (5%)
  local copies, waits for them, and re-layouts  16.2 us (3%)
    pallas_call x7, Pallas kernels, call(): pl.pallas_call(kernel, name=name, out_shape=outs, in_specs=in_specs, out_...  423 us
    dot_general x4, matrix products, product(): lax.dot_general(left_side, right_side, (((1,), (1,)), ((), ())), preferre...  22.4 us
    dot_general x4, matrix products, column_total(): lax.dot_general(left_side, right_side, (((0,), (0,)), ((), ())), preferre...  18.4 us
    dot_general x4, matrix products, product(): return jnp.dot(left_side, right_side, preferred_element_type=jnp.float32)  17.6 us

profile of v1, /device:TPU:9, one launch (start us, length us, event | category | flops | bytes accessed | tf_op | source)
XLA Modules:
  0.0 534.1 jit_solution(2464406279393958234)
XLA Ops:
  4.2 62.4 %bring.1 = (bf16[512,2048]{1,0:T(8,128)(2,1)}, bf16[64,2048]{1,0:T(8,128)(2,1)}, bf16[2048,768]{1,0:T(8,128)(2,1)}, bf16[256,2048]{1,0:T(8,128)(2,1)}) custom-call(bf16[512,256]{1,0:T(8,128)(2,1)} %x.1, bf16[512,256]{1,0:T(8,128)(2,1)} %g.1, bf16[256,768]{1,0:T(8,128)(2,1)} %convert_element_type.122.heads, bf16[256,256]{1,0:T(8,128)(2,1)} %convert_element_type.123.merge), custom_call_target="tpu_custom_call" | custom-call | tf_op jit(solution)/shard_map/bring/pallas_call | solution.py:485
  66.7 4.3 fusion.52
  72.5 15.4 %sums.2 = f32[8,128]{1,0:T(8,128)} custom-call(f32[8,128]{1,0:T(8,128)} %pad_maximum_fusion.13.part), custom_call_target="tpu_custom_call" | custom-call | tf_op jit(solution)/shard_map/sums/pallas_call | solution.py:485
  91.0 2.3 broadcast_multiply_fusion
  98.6 2.1 convolution_convert_fusion.4.part
  102.4 2.7 convert_element_type.133.expand
  106.0 81.9 %merged.1 = (f32[64,2048]{1,0:T(8,128)}, f32[64,2048]{1,0:T(8,128)}, bf16[512,2048]{1,0:T(8,128)(2,1)}, bf16[2048,2048]{1,0:T(8,128)(2,1)}, bf16[1024,2048]{1,0:T(8,128)(2,1)}) custom-call(bf16[512,2048]{1,0:T(8,128)(2,1)} %convolution_convert_fusion.4.part, bf16[64,2048]{1,0:T(8,128)(2,1)} %constant_dynamic-slice_fusion.x, ...), custom_call_target="tpu_custom_call" | custom-call | tf_op jit(solution)/shard_map/merged/pallas_call | solution.py:485
  187.9 7.6 %fusion.53 = f32[512,2048]{1,0:T(8,128)S(1)} fusion(bf16[512,2048]{1,0:T(8,128)(2,1)} %get-tuple-element.50, bf16[2048,2048]{1,0:T(8,128)(2,1)} %get-tuple-element.51), kind=kOutput, calls=%fused_computation.134 | convolution fusion | flops 4294967296 | bytes 14680064 | tf_op jit(solution)/shard_map/dot_general | solution.py:70
  196.1 1.9 copy-done.48
  198.0 3.7 convolution_convert_fusion.3.part
  201.7 72.0 %reduced.1 = (bf16[512,256]{1,0:T(8,128)(2,1)}, bf16[512,2048]{1,0:T(8,128)(2,1)}, f32[1,2048]{1,0:T(1,128)}) custom-call(bf16[512,2048]{1,0:T(8,128)(2,1)} %convolution_convert_fusion.3.part, f32[64,2048]{1,0:T(8,128)} %get-tuple-element.53.residual, bf16[64,2048]{1,0:T(8,128)(2,1)} %get-tuple-element.54.g, f32[1,2048]{1,0:T(1,128)} %get-tuple-element.123.gain), custom_call_target="tpu_custom_call" | custom-call | tf_op jit(solution)/shard_map/reduced/pallas_call | solution.py:485
  273.8 5.7 %multiply_convert_fusion.2 = (bf16[512,1024]{1,0:T(8,128)(2,1)S(1)}, bf16[512,1024]{1,0:T(8,128)(2,1)S(1)}) fusion(f32[512,2048]{1,0:T(8,128)S(1)} %fusion.53, bf16[512,2048]{1,0:T(8,128)(2,1)} %get-tuple-element.56, bf16[1024,2048]{1,0:T(8,128)(2,1)} %get-tuple-element.52), kind=kOutput, calls=%fused_computation.16 | convolution fusion | flops 2154299392 | bytes 12582912 | tf_op jit(solution)/shard_map/dot_general | solution.py:67
  279.5 9.3 %convolution_convert_fusion.6.part = bf16[512,2048]{1,0:T(8,128)(2,1)} fusion(bf16[2048,2048]{1,0:T(8,128)(2,1)} %get-tuple-element.51, bf16[512,1024]{1,0:T(8,128)(2,1)S(1)} %get-tuple-element.102, bf16[512,1024]{1,0:T(8,128)(2,1)S(1)} %get-tuple-element.101), kind=kOutput, calls=%fused_computation.8 | convolution fusion | flops 4300210176 | bytes 12582912 | tf_op jit(solution)/shard_map/dot_general | solution.py:67
  288.8 7.1 %convolution_convert_fusion.expand_part = bf16[2048,2048]{1,0:T(8,128)(2,1)} fusion(bf16[512,2048]{1,0:T(8,128)(2,1)S(1)} %copy-done.50, bf16[512,1024]{1,0:T(8,128)(2,1)S(1)} %get-tuple-element.102, bf16[512,1024]{1,0:T(8,128)(2,1)S(1)} %get-tuple-element.101), kind=kOutput, calls=%fused_computation | convolution fusion | flops 4303355904 | bytes 12582912 | tf_op jit(solution)/shard_map/dot_general | solution.py:74
  295.8 82.8 %branch.1 = (f32[64,2048]{1,0:T(8,128)}, bf16[512,2048]{1,0:T(8,128)(2,1)}, f32[1,2048]{1,0:T(1,128)}, bf16[256,2048]{1,0:T(8,128)(2,1)}) custom-call(bf16[512,2048]{1,0:T(8,128)(2,1)} %convolution_convert_fusion.6.part, bf16[64,2048]{1,0:T(8,128)(2,1)} %get-tuple-element.54.g, f32[64,2048]{1,0:T(8,128)} %get-tuple-element.57.merged, ...), custom_call_target="tpu_custom_call" | custom-call | tf_op jit(solution)/shard_map/branch/pallas_call | solution.py:485
  378.7 2.3 convolution_convert_fusion.9
  391.6 8.7 %sums.3 = f32[8,128]{1,0:T(8,128)} custom-call(f32[8,128]{1,0:T(8,128)} %pad_maximum_fusion.14.part), custom_call_target="tpu_custom_call" | custom-call | tf_op jit(solution)/shard_map/sums/pallas_call | solution.py:485
  401.6 5.0 convolution_convert_fusion.5.part
  407.4 5.2 convolution_convert_fusion.2.heads_part
  414.9 4.4 convolution_convert_fusion.1.reduce_part
  419.3 99.7 %last.1 = (f32[512,256]{1,0:T(8,128)}, f32[8,1024]{1,0:T(8,128)}, bf16[256,768]{1,0:T(8,128)(2,1)}, bf16[256,256]{1,0:T(8,128)(2,1)}, bf16[1024,256]{1,0:T(8,128)(2,1)}) custom-call(bf16[512,2048]{1,0:T(8,128)(2,1)} %convolution_convert_fusion.5.part, f32[64,2048]{1,0:T(8,128)} %get-tuple-element.59.grad_resid, f32[8,1024]{1,0:T(8,128)} %reshape.315.gains, ...), custom_call_target="tpu_custom_call" | custom-call | tf_op jit(solution)/shard_map/last/pallas_call | solution.py:485
  519.1 3.1 fusion.46
  524.4 4.6 fusion.42
  529.1 2.5 fusion.40
  (148 shorter events, 35.6 us)
Async XLA Ops:
  66.6 4.3 copy-start.40
  71.0 18.2 %copy-start = (f32[512,768]{1,0:T(8,128)}, f32[512,768]{1,0:T(8,128)S(1)}, u32[]{:S(2)}) copy-start(f32[512,768]{1,0:T(8,128)S(1)} %fusion.52) | copy-start | bytes 4718596
  90.7 3.5 copy-start.13
  90.7 3.6 copy-start.14
  100.7 4.5 copy-start.3
  196.1 5.6 %copy-start.22 = (bf16[512,1024]{1,0:T(8,128)(2,1)}, bf16[512,1024]{1,0:T(8,128)(2,1)S(1)}, u32[]{:S(2)}) copy-start(bf16[512,1024]{1,0:T(8,128)(2,1)S(1)} %multiply_convert_fusion.3) | copy-start | bytes 3145732
  279.5 9.3 %copy-start.50 = (bf16[512,2048]{1,0:T(8,128)(2,1)S(1)}, bf16[512,2048]{1,0:T(8,128)(2,1)}, u32[]{:S(2)}) copy-start(bf16[512,2048]{1,0:T(8,128)(2,1)} %get-tuple-element.50) | copy-start | bytes 6291460
  295.8 82.8 %copy-start.27 = (bf16[256,2048]{1,0:T(8,128)(2,1)S(1)}, bf16[256,2048]{1,0:T(8,128)(2,1)}, u32[]{:S(2)}) copy-start(bf16[256,2048]{1,0:T(8,128)(2,1)} %get-tuple-element.49) | copy-start | bytes 3145732
  391.0 10.7 %copy-start.36 = (bf16[512,256]{1,0:T(8,128)(2,1)S(1)}, bf16[512,256]{1,0:T(8,128)(2,1)}, u32[]{:S(2)}) copy-start(bf16[512,256]{1,0:T(8,128)(2,1)} %copy.89) | copy-start | bytes 786436
  401.6 5.1 copy-start.45
  401.6 5.1 copy-start.46
  407.4 5.2 copy-start.15
  407.4 5.2 copy-start.19
  419.3 99.7 %copy-start.4 = (f32[256,768]{1,0:T(8,128)S(1)}, f32[256,768]{1,0:T(8,128)}, u32[]{:S(2)}) copy-start(f32[256,768]{1,0:T(8,128)} %param.21) | copy-start | bytes 2359300
  419.3 99.7 %copy-start.31 = (f32[256,768]{1,0:T(8,128)S(1)}, f32[256,768]{1,0:T(8,128)}, u32[]{:S(2)}) copy-start(f32[256,768]{1,0:T(8,128)} %param.23) | copy-start | bytes 2359300
  419.3 99.8 %copy-start.32 = (f32[256,768]{1,0:T(8,128)S(1)}, f32[256,768]{1,0:T(8,128)}, u32[]{:S(2)}) copy-start(f32[256,768]{1,0:T(8,128)} %param.22) | copy-start | bytes 2359300
  519.1 4.3 copy-start.16
  519.1 4.3 copy-start.17
  519.1 4.3 copy-start.21
  524.4 4.6 copy-start.29
  524.4 4.6 copy-start.30
  524.4 4.6 copy-start.33
  529.1 3.3 copy-start.35
  529.1 3.9 copy-start.34
  (27 other events, 50.1 us)

commit v2 on v1

--- a/solution.py
+++ b/solution.py
@@ -585,55 +585,498 @@
     return hat, rate * (grad_hat - hat * dots)
 
 
-def reduced_kernel(
-    part, residual, g, gain, out, rows_all, gain_part,
-    came, mine, done, ssent, scame, gsent, gcame, osent, ocame,
+def dot(left, right):
+    return jnp.dot(left, right, preferred_element_type=F32)
+
+
+def dot_flipped(left, right):
+    return lax.dot_general(left, right, (((1,), (1,)), ((), ())), preferred_element_type=F32)
+
+
+def span(k, count):
+    return pl.ds(pl.multiple_of(k * count, count), count)
+
+
+def near_row(row, dx, dy):
+    return (row // 4 + dy) % 2 * 4 + (row % 4 + dx) % 4
+
+
+def meet_near(weights=False, spread_in=False, spread_out=False, cols=False):
+    dp, row, col = here()
+    barrier = pltpu.get_barrier_semaphore()
+    count = 4
+
+    def greet(**where):
+        pl.semaphore_signal(barrier, inc=1, device_id=where, device_id_type=MESH)
+
+    for dx, dy in ((1, 0), (2, 0), (3, 0), (0, 1)):
+        greet(row=near_row(row, dx, dy))
+    if weights:
+        greet(col=y_peer(col))
+        for d in range(1, 4):
+            greet(col=z_peer(col, d))
+        greet(dp=1 - dp)
+        count = count + 5
+    if cols:
+        for d in range(1, 8):
+            greet(col=(col + d) % 8)
+        count = count + 7
+    for wanted, inward in ((spread_in, True), (spread_out, False)):
+        if wanted:
+            for k in range(8):
+                at_row, at_col = (col, k) if inward else (k, row)
+
+                @pl.when(jnp.logical_not((at_row == row) & (at_col == col)))
+                def _():
+                    greet(row=at_row, col=at_col)
+
+            count = count + 8 - (row == col).astype(jnp.int32)
+    pl.semaphore_wait(barrier, count)
+
+
+class Scatter:
+    def __init__(self, part, total, from_y, from_x, last_y, last_x, stage, sent, arrived):
+        dp, row, col = here()
+        self.row, self.part, self.total = row, part, total
+        self.from_y, self.from_x, self.last_y, self.last_x, self.stage = from_y, from_x, last_y, last_x, stage
+        self.count, self.half = total.shape[0], total.shape[1] // 2
+        number = iter(range(14))
+
+        def copy(source, target, dx, dy):
+            i = next(number)
+            return remote(source, target, sent.at[i], arrived.at[i], row=near_row(row, dx, dy))
+
+        self.y_first = {dx: copy(self.block(dx, 1, 1), from_y.at[dx], 0, 1) for dx in (1, 3, 2, 0)}
+        self.x_first = {
+            (dx, dy): copy(self.block(dx, dy, 0), from_x.at[dy, dx - 1], dx, 0)
+            for dy in (1, 0)
+            for dx in (1, 3, 2)
+        }
+        self.x_last = {dx: copy(stage.at[dx], last_x.at[dx - 1], dx, 0) for dx in (1, 3, 2)}
+        self.y_last = copy(stage.at[0], last_y, 0, 1)
+
+    def block(self, dx, dy, side):
+        return self.part.at[
+            span(near_row(self.row, dx, dy), self.count), pl.ds(side * self.half, self.half)
+        ]
+
+    def start_right(self):
+        for copy in self.y_first.values():
+            copy.start()
+
+    def start_left(self):
+        for copy in self.x_first.values():
+            copy.start()
+
+    def chunks(self, body):
+        @pl.loop(0, self.count // 16)
+        def _(i):
+            body(span(i, 16))
+
+    def middle(self):
+        for dx in (1, 3, 2):
+            self.y_first[dx].wait_recv()
+            own = self.block(dx, 0, 1)
+
+            def add(at):
+                self.stage[dx, at] = (own[at].astype(F32) + self.from_y[dx, at].astype(F32)).astype(BF16)
+
+            self.chunks(add)
+            self.x_last[dx].start()
+        for dx in (1, 3, 2):
+            self.x_first[dx, 1].wait_recv()
+        other = self.block(0, 1, 0)
+
+        def add(at):
+            total = other[at].astype(F32)
+            for k in range(3):
+                total = total + self.from_x[1, k, at].astype(F32)
+            self.stage[0, at] = total.astype(BF16)
+
+        self.chunks(add)
+        self.y_last.start()
+
+    def end(self):
+        self.y_first[0].wait_recv()
+        for dx in (1, 3, 2):
+            self.x_first[dx, 0].wait_recv()
+            self.x_last[dx].wait_recv()
+        self.y_last.wait_recv()
+        left, right = self.block(0, 0, 0), self.block(0, 0, 1)
+
+        def add(at):
+            total = left[at].astype(F32) + self.last_y[at].astype(F32)
+            for k in range(3):
+                total = total + self.from_x[0, k, at].astype(F32)
+            self.total[at, : self.half] = total
+            total = right[at].astype(F32) + self.from_y[0, at].astype(F32)
+            for k in range(3):
+                total = total + self.last_x[k, at].astype(F32)
+            self.total[at, self.half :] = total
+
+        self.chunks(add)
+
+    def finish(self):
+        for copies in (self.y_first, self.x_first, self.x_last):
+            for copy in copies.values():
+                copy.wait_send()
+        self.y_last.wait_send()
+
+
+def scatter_scratch(share, width):
+    half = width // 2
+    return [
+        pltpu.VMEM((share, width), F32),
+        pltpu.VMEM((4, share, half), BF16),
+        pltpu.VMEM((2, 3, share, half), BF16),
+        pltpu.VMEM((share, half), BF16),
+        pltpu.VMEM((3, share, half), BF16),
+        pltpu.VMEM((4, share, half), BF16),
+        DMA((14,)),
+        DMA((14,)),
+    ]
+
+
+class Gather:
+    def __init__(self, whole, share, sent, arrived):
+        dp, row, col = here()
+        self.row = row
+        half = whole.shape[1] // 2
+        number = iter(range(19))
+
+        def copy(fx, fy, side, dx, dy, start=0, count=share):
+            i = next(number)
+            k = near_row(row, fx, fy)
+            ref = whole.at[
+                pl.ds(pl.multiple_of(k * share + start, count), count), pl.ds(side * half, half)
+            ]
+            return remote(ref, ref, sent.at[i], arrived.at[i], row=near_row(row, dx, dy))
+
+        part = share // 2
+        self.y_own = [copy(0, 0, 0, 0, 1), copy(0, 0, 1, 0, 1)]
+        self.x_own = [[copy(0, 0, side, dx, 0) for dx in (1, 3)] for side in range(2)]
+        self.x_other = [copy(0, 1, 0, dx, 0) for dx in (1, 3)]
+        self.on = [
+            [copy(4 - dx, 0, side, dx, 0, i * part, part) for i, dx in enumerate((1, 3))]
+            for side in range(2)
+        ]
+        self.on_other = [copy(4 - dx, 1, 0, dx, 0, i * part, part) for i, dx in enumerate((1, 3))]
+        self.y_near = [copy(4 - dx, 0, 1, 0, 1) for dx in (1, 3)]
+        self.y_far = [copy(2, 0, 1, 0, 1, i * part, part) for i in range(2)]
+
+    def start(self):
+        for copy in (self.y_own[0], *self.x_own[1], self.y_own[1], *self.x_own[0]):
+            copy.start()
+
+    def relay(self):
+        self.y_own[0].wait_recv()
+        for copy in self.x_other:
+            copy.start()
+        for i in range(2):
+            self.x_own[1][i].wait_recv()
+            self.on[1][i].start()
+            self.y_near[i].start()
+
+    def relay_again(self):
+        for i in range(2):
+            self.x_own[0][i].wait_recv()
+            self.on[0][i].start()
+        for i in range(2):
+            self.on[1][i].wait_recv()
+            self.y_far[i].start()
+        for i in range(2):
+            self.x_other[i].wait_recv()
+            self.on_other[i].start()
+
+    def wait(self):
+        self.y_own[1].wait_recv()
+        for copy in (*self.on[0], *self.on_other, *self.y_near, *self.y_far):
+            copy.wait_recv()
+        for copy in (*self.y_own, *self.x_own[0], *self.x_own[1], *self.x_other, *self.on[0], *self.on[1],
+                     *self.on_other, *self.y_near, *self.y_far):
+            copy.wait_send()
+
+
+def gather_scratch():
+    return [DMA((19,)), DMA((19,))]
+
+
+class GradSum:
+    def __init__(self, kind, part, out, other, far, near, sent, arrived):
+        dp, _, col = here()
+        self.kind, self.part, self.dp, self.col = kind, part, dp, col
+        self.other, self.far, self.near = other, far, near
+        self.rows = near.shape[1]
+        self.core = [
+            remote(self.half(c, 1 - dp), other.at[c], sent.at[c], arrived.at[c], dp=1 - dp)
+            for c in range(8)
+        ]
+        self.zs = [
+            [
+                remote(
+                    self.half(z_peer(col, d) // 2 * 2 + k, dp), far.at[d - 1, k], sent.at[6 + 2 * d + k],
+                    arrived.at[6 + 2 * d + k], col=z_peer(col, d),
+                )
+                for k in range(2)
+            ]
+            for d in (1, 3, 2)
+        ]
+        self.ys = remote(near.at[0], near.at[1], sent.at[14], arrived.at[14], col=y_peer(col))
+        self.last = remote(near.at[0], half_shard(out, dp), sent.at[15], arrived.at[15], dp=1 - dp)
+        self.keep = pltpu.make_async_copy(near.at[0], half_shard(out, dp), sent.at[16])
+
+    def half(self, c, h):
+        return half_of(self.kind, self.part, c, h)
+
+    def start(self):
+        for copy in self.core:
+            copy.start()
+
+    def each(self, body):
+        @pl.loop(0, self.rows // 16)
+        def _(i):
+            body(span(i, 16))
+
+    def over_z(self):
+        for copy in self.core:
+            copy.wait()
+
+        @pl.loop(0, 8)
+        def _(c):
+            own = self.half(c, self.dp)
+
+            def add(at):
+                own[at] = (own[at].astype(F32) + self.other[c, at].astype(F32)).astype(BF16)
+
+            self.each(add)
+
+        for pair in self.zs:
+            for copy in pair:
+                copy.start()
+
+    def over_y(self):
+        for pair in self.zs:
+            for copy in pair:
+                copy.wait_recv()
+        yl = self.col % 2
+        keep, give = self.half(self.col, self.dp), self.half(y_peer(self.col), self.dp)
+
+        def add(at):
+            total = give[at].astype(F32)
+            for d in range(3):
+                total = total + self.far[d, 1 - yl, at].astype(F32)
+            self.near[0, at] = total.astype(BF16)
+
+        self.each(add)
+        self.ys.start()
+
+        def add(at):
+            total = keep[at].astype(F32)
+            for d in range(3):
+                total = total + self.far[d, yl, at].astype(F32)
+            keep[at] = total.astype(BF16)
+
+        self.each(add)
+        for pair in self.zs:
+            for copy in pair:
+                copy.wait_send()
+
+    def over_core(self):
+        self.ys.wait()
+        keep = self.half(self.col, self.dp)
+
+        def add(at):
+            self.near[0, at] = (keep[at].astype(F32) + self.near[1, at].astype(F32)).astype(BF16)
+
+        self.each(add)
+        self.last.start()
+        self.keep.start()
+
+    def wait(self):
+        self.last.wait()
+        self.keep.wait()
+
+
+def grad_sum_scratch(rows, width):
+    return [
+        pltpu.VMEM((8, rows, width), BF16),
+        pltpu.VMEM((3, 2, rows, width), BF16),
+        pltpu.VMEM((2, rows, width), BF16),
+        DMA((17,)),
+        DMA((16,)),
+    ]
+
+
+def feed_kernel(
+    rows_in, expand_in, reduce_in, residual, g, merged, gain_merge, gain_reduce,
+    out, grad_resid, rows_out, merge_gain, reduce_gain, expand_grad, reduce_grad,
+    rows, turned, expand, reduce, gate, up, act, act_turned, part, back, hidden, new_rows, done, sums, grad_gate,
+    load, osent, ocame, g1sent, g1came, g2sent, g2came, *refs,
 ):
-    meet(rows=True, spread_out=True)
-    scatter = RowScatter(part, came, ssent, scame)
-    gather = RowGather(mine, rows_all, gsent, gcame)
+    dp, row, col = here()
+    share, width = residual.shape
+    units = act.shape[1]
+    tiles = units // 256
+    own = span(row, share)
+    first = Scatter(part, *refs[:8])
+    second = Scatter(part, *refs[8:16])
+    reduce_sum = GradSum("wide", reduce, reduce_grad, *refs[16:21])
+    expand_sum = GradSum("tall", expand, expand_grad, *refs[21:26])
+    gather = Gather(back, share, g1sent, g1came)
+    last_gather = Gather(new_rows, share, g2sent, g2came)
     spread = Spread(False, lambda k: cols(done, k, 256), lambda k: rows_of(out, k, 64), osent, ocame)
-    scatter.start()
-    total = scatter.total()
-    grad = g[...].astype(F32)
-    hat, back = back_of(grad, total, gain[...])
-    mine[...] = back.astype(BF16)
+
+    get_rows = pltpu.make_async_copy(rows_in, rows, load.at[0])
+    get_reduce = pltpu.make_async_copy(reduce_in, reduce, load.at[1])
+
+    def get_expand(j):
+        at = span(j, 256)
+        return pltpu.make_async_copy(expand_in.at[:, at], expand.at[:, at], load.at[2 + j])
+
+    get_rows.start()
+    for j in range(tiles):
+        get_expand(j).start()
+        get_expand(tiles + j).start()
+    get_reduce.start()
+    meet_near(weights=True, spread_out=True)
+    get_rows.wait()
+
+    @pl.loop(0, tiles)
+    def _(j):
+        get_expand(j).wait()
+        get_expand(tiles + j).wait()
+        at = span(j, 256)
+        gate[:, at] = dot(rows[...], expand[:, at])
+        up[:, at] = dot(rows[...], expand[:, span(tiles + j, 256)])
+
+        @pl.loop(0, rows.shape[0] // 64)
+        def _(i):
+            some = span(i, 64)
+            x = gate[some, at]
+            act[some, at] = (x * jax.nn.sigmoid(x) * up[some, at]).astype(BF16)
+
+    get_reduce.wait()
+
+    def reduced(j):
+        at = span(j, 256)
+        part[:, at] = dot(act[...], reduce[:, at]).astype(BF16)
+
+    n = width // 512
+    pl.loop(n, 2 * n)(reduced)
+    first.start_right()
+    pl.loop(0, n)(reduced)
+    first.start_left()
+
+    @pl.loop(0, tiles)
+    def _(j):
+        at = span(j, 256)
+        act_turned[at, :] = act[:, at].T
+
+    first.middle()
+    first.end()
+    sums[...] = jnp.zeros_like(sums)
+
+    @pl.loop(0, share // 16)
+    def _(i):
+        at = span(i, 16)
+        grad = g[at].astype(F32)
+        hat, change = back_of(grad, first.total[at], gain_reduce[...])
+        back[pl.ds(pl.multiple_of(row * share + i * 16, 16), 16), :] = change.astype(BF16)
+        done[at] = (residual[at] + hat * gain_reduce[...]).astype(BF16)
+        product = grad * hat
+        sums[...] += product[:8] + product[8:]
+
     gather.start()
-    done[...] = (residual[...] + hat * gain[...]).astype(BF16)
     spread.start()
-    gain_part[...] = jnp.sum(grad * hat, axis=0, keepdims=True)
-    scatter.finish()
+    reduce_gain[...] = jnp.sum(sums[...], axis=0, keepdims=True)
+    first.finish()
+    gather.relay()
+
+    @pl.loop(0, 2 * tiles)
+    def _(j):
+        at = span(j, 256)
+        turned[at, :] = rows[:, at].T
+
+    gather.relay_again()
     gather.wait()
+
+    @pl.loop(0, tiles)
+    def _(j):
+        at, up_at = span(j, 256), span(tiles + j, 256)
+        grad_gate[...] = dot_flipped(back[...], reduce[at, :])
+
+        @pl.loop(0, rows.shape[0] // 64)
+        def _(i):
+            some = span(i, 64)
+            x, change = gate[some, at], grad_gate[some]
+            s = jax.nn.sigmoid(x)
+            hidden[some, at] = (change * up[some, at] * s * (1.0 + x * (1.0 - s))).astype(BF16)
+            hidden[some, up_at] = (change * (x * s)).astype(BF16)
+
+    def branch(j):
+        at = span(j, 256)
+        part[:, at] = dot_flipped(hidden[...], expand[at, :]).astype(BF16)
+
+    pl.loop(n, 2 * n)(branch)
+    second.start_right()
+    pl.loop(0, n)(branch)
+    second.start_left()
+
+    @pl.loop(0, tiles)
+    def _(j):
+        at = span(j, 256)
+        for side in range(2):
+            wide = pl.ds(side * (width // 2), width // 2)
+            reduce[at, wide] = dot(act_turned[at, :], back[:, wide]).astype(BF16)
+
+    reduce_sum.start()
+    second.middle()
+
+    def expand_part(j):
+        at = span(j, 256)
+        for side in range(2):
+            wide = pl.ds(side * (width // 2), width // 2)
+            expand[at, wide] = dot(turned[at, :], hidden[:, wide]).astype(BF16)
+
+    pl.loop(0, tiles)(expand_part)
+    second.end()
+    sums[...] = jnp.zeros_like(sums)
+
+    @pl.loop(0, share // 16)
+    def _(i):
+        at = span(i, 16)
+        grad = g[at].astype(F32) + second.total[at]
+        grad_resid[at] = grad
+        hat, change = back_of(grad, merged[at], gain_merge[...])
+        new_rows[pl.ds(pl.multiple_of(row * share + i * 16, 16), 16), :] = change.astype(BF16)
+        product = grad * hat
+        sums[...] += product[:8] + product[8:]
+
+    last_gather.start()
+    merge_gain[...] = jnp.sum(sums[...], axis=0, keepdims=True)
+    pl.loop(tiles, 2 * tiles)(expand_part)
+    expand_sum.start()
+    last_gather.relay()
+    reduce_sum.over_z()
+    last_gather.relay_again()
+    expand_sum.over_z()
+    second.finish()
+    last_gather.wait()
+    put_rows = pltpu.make_async_copy(new_rows, rows_out, load.at[0])
+    put_rows.start()
+    reduce_sum.over_y()
+    expand_sum.over_y()
+    reduce_sum.over_core()
+    expand_sum.over_core()
     spread.wait()
-
-
-def branch_kernel(
-    part, g, merged, gain, expand_part, grad_resid, rows_all, gain_part, expand_grad,
-    came, mine, ssent, scame, gsent, gcame, *grad_refs,
-):
-    meet(rows=True, weights=True)
-    scatter = RowScatter(part, came, ssent, scame)
-    gather = RowGather(mine, rows_all, gsent, gcame)
-    expand = GradScatter("tall", expand_part, expand_grad, *grad_refs)
-    scatter.start()
-    expand.start()
-    expand.over_z()
-    grad = g[...].astype(F32) + scatter.total()
-    grad_resid[...] = grad
-    hat, back = back_of(grad, merged[...], gain[...])
-    mine[...] = back.astype(BF16)
-    gather.start()
-    gain_part[...] = jnp.sum(grad * hat, axis=0, keepdims=True)
-    scatter.finish()
-    expand.over_y()
-    expand.over_core()
-    gather.wait()
-    expand.wait()
+    put_rows.wait()
+    reduce_sum.wait()
+    expand_sum.wait()
 
 
 def last_kernel(
-    part, grad_resid, gains, heads_part, merge_part, reduce_part,
-    input_grad, gains_grad, heads_grad, merge_grad, reduce_grad,
+    part, grad_resid, gains, heads_part, merge_part,
+    input_grad, gains_grad, heads_grad, merge_grad,
     came, done, grow, gcol, gcore, gsum, ssent, scame, osent, ocame, gsent, gcame, *grad_refs,
 ):
     dp, row, col = here()
@@ -641,9 +1084,8 @@
     scatter = RowScatter(part, came, ssent, scame)
     spread = Spread(False, lambda k: cols(done, k, 256), lambda k: rows_of(input_grad, k, 64), osent, ocame)
     grads = [
-        GradScatter("wide", reduce_part, reduce_grad, *grad_refs[:6]),
-        GradScatter("tall", heads_part, heads_grad, *grad_refs[6:12]),
-        GradScatter("wide", merge_part, merge_grad, *grad_refs[12:]),
+        GradScatter("tall", heads_part, heads_grad, *grad_refs[:6]),
+        GradScatter("wide", merge_part, merge_grad, *grad_refs[6:]),
     ]
     row_sums = [
         remote(gains, grow.at[row], gsent.at[d - 1], gcame.at[d - 1], row=row_peer(row, d))
@@ -785,34 +1227,34 @@
         [VMEM, VMEM, VMEM, ANY, ANY], [VMEM, VMEM, ANY, ANY, ANY],
         row_scratch + gather_sems(2),
     )
-    gated_cols = product(residual_rows, expand_low, False)
-    gate_vals = gated_cols[:, :unit_width]
-    up_vals = gated_cols[:, unit_width:]
-    activity = (jax.nn.silu(gate_vals) * up_vals).astype(jnp.bfloat16)
-    reduced_part = product(activity, reduce_low, False).astype(BF16)
-
-    block_output, reduced_grad_rows, reduce_gain_part = call(
-        reduced_kernel, "reduced", 4,
-        [struct(block_input.shape, BF16), rows_shape, line],
-        [reduced_part, residual, cot_share, gain_reduce],
-        [VMEM] * 4, [ANY, ANY, VMEM],
-        row_scratch[:2] + [pltpu.VMEM((share, model_width), BF16)] + row_scratch[2:] + [DMA((8,)), DMA((8,))],
-    )
-    grad_activity = product(reduced_grad_rows, reduce_low, True)
-    sigmoid_vals = jax.nn.sigmoid(gate_vals)
-    grad_gate = grad_activity * up_vals * sigmoid_vals * (1.0 + gate_vals * (1.0 - sigmoid_vals))
-    grad_up = grad_activity * jax.nn.silu(gate_vals)
-    gated_grad = jnp.concatenate([grad_gate, grad_up], axis=1).astype(jnp.bfloat16)
-    branch_part = product(gated_grad, expand_low, True).astype(BF16)
-    expand_part = column_total(residual_rows, gated_grad).astype(BF16)
-    reduce_part = column_total(activity, reduced_grad_rows).astype(BF16)
-
-    grad_resid, merged_grad_rows, merge_gain_part, expand_grad = call(
-        branch_kernel, "branch", 5,
-        [mine_f32, rows_shape, line, struct(expand_weight.shape, BF16)],
-        [branch_part, cot_share, merged, gain_merge, expand_part],
-        [VMEM] * 4 + [ANY], [VMEM, ANY, VMEM, ANY],
-        row_scratch + grad_scratch(expand_weight.shape[0] // 2, expand_weight.shape[1]),
+    block_output, grad_resid, merged_grad_rows, merge_gain_part, reduce_gain_part, expand_grad, reduce_grad = call(
+        feed_kernel, "feed", 4,
+        [struct(block_input.shape, BF16), mine_f32, rows_shape, line, line, struct(expand_weight.shape, BF16),
+         struct(reduce_weight.shape, BF16)],
+        [residual_rows, expand_low, reduce_low, residual, cot_share, merged, gain_merge, gain_reduce],
+        [ANY] * 3 + [VMEM] * 5, [ANY, VMEM, ANY, VMEM, VMEM, ANY, ANY],
+        [
+            pltpu.VMEM((seq_len, model_width), BF16),
+            pltpu.VMEM((model_width, seq_len), BF16),
+            pltpu.VMEM((model_width, 2 * unit_width), BF16),
+            pltpu.VMEM((unit_width, model_width), BF16),
+            pltpu.VMEM((seq_len, unit_width), F32),
+            pltpu.VMEM((seq_len, unit_width), F32),
+            pltpu.VMEM((seq_len, unit_width), BF16),
+            pltpu.VMEM((unit_width, seq_len), BF16),
+            pltpu.VMEM((seq_len, model_width), BF16),
+            pltpu.VMEM((seq_len, model_width), BF16),
+            pltpu.VMEM((seq_len, 2 * unit_width), BF16),
+            pltpu.VMEM((seq_len, model_width), BF16),
+            pltpu.VMEM((share, model_width), BF16),
+            pltpu.VMEM((8, model_width), F32),
+            pltpu.VMEM((seq_len, 256), F32),
+            DMA((10,)), DMA((8,)), DMA((8,)),
+        ]
+        + gather_scratch() + gather_scratch()
+        + scatter_scratch(share, model_width) + scatter_scratch(share, model_width)
+        + grad_sum_scratch(reduce_weight.shape[0] // 2, reduce_weight.shape[1])
+        + grad_sum_scratch(expand_weight.shape[0] // 2, expand_weight.shape[1]),
     )
     grad_mixture = product(merged_grad_rows, merge_low, True)
     merge_part = column_total(mixture_low, merged_grad_rows).astype(BF16)
@@ -846,16 +1288,15 @@
     gain_parts = jnp.concatenate([gain_parts, merge_gain_part, reduce_gain_part]).reshape(8, model_width // 2)
     gain_shape = (8, model_width // 2)
 
-    input_grad, gains_grad, heads_grad, merge_grad, reduce_grad = call(
+    input_grad, gains_grad, heads_grad, merge_grad = call(
         last_kernel, "last", 7,
         [struct(block_input.shape, F32), struct(gain_shape, F32), struct(heads_weight.shape, BF16),
-         struct(merge_weight.shape, BF16), struct(reduce_weight.shape, BF16)],
-        [input_part, grad_resid, gain_parts, heads_part, merge_part, reduce_part],
-        [VMEM] * 3 + [ANY] * 3, [ANY, VMEM] + [ANY] * 3,
+         struct(merge_weight.shape, BF16)],
+        [input_part, grad_resid, gain_parts, heads_part, merge_part],
+        [VMEM] * 3 + [ANY] * 2, [ANY, VMEM] + [ANY] * 2,
         [row_scratch[0], pltpu.VMEM((share, model_width), F32), pltpu.VMEM((8, *gain_shape), F32),
          pltpu.VMEM((8, *gain_shape), F32), pltpu.VMEM(gain_shape, F32), pltpu.VMEM((2, *gain_shape), F32),
          DMA((7,)), DMA((7,)), DMA((8,)), DMA((8,)), DMA((15,)), DMA((15,))]
-        + grad_scratch(reduce_weight.shape[0] // 2, reduce_weight.shape[1])
         + grad_scratch(heads_weight.shape[0] // 2, heads_weight.shape[1])
         + grad_scratch(merge_weight.shape[0] // 2, merge_weight.shape[1]),
     )

time: 542 us -> 491 us (0.906); the launches traced: 534 us -> 490 us
  matrix products: 64.7 us -> 25.3 us
  local copies, waits for them, and re-layouts: 16.2 us -> 10 us
    dot_general x4 -> x2, matrix products: 22.4 us -> 5.78 us  [product(): lax.dot_general(left_side, right_side, (((1,), (1,)), ((), ())), preferre...]
    dot_general x4 -> x2, matrix products: 17.6 us -> 6.36 us  [product(): return jnp.dot(left_side, right_side, preferred_element_type=jnp.float32)]
    dot_general x4 -> x2, matrix products: 18.4 us -> 8.61 us  [column_total(): lax.dot_general(left_side, right_side, (((0,), (0,)), ((), ())), preferre...]
    pallas_call x7 -> x6, Pallas kernels: 423 us -> 422 us  [call(): pl.pallas_call(kernel, name=name, out_shape=outs, in_specs=in_specs, out_...]
where the time goes in v2:
time: 491 us; the launch traced here: 490 us
  Pallas kernels  422 us (86%)
  other arithmetic  31 us (6%)
  matrix products  25.3 us (5%)
  local copies, waits for them, and re-layouts  10 us (2%)
    pallas_call x6, Pallas kernels, call(): pl.pallas_call(kernel, name=name, out_shape=outs, in_specs=in_specs, out_...  422 us

profile of v2, /device:TPU:9, one launch (start us, length us, event | category | flops | bytes accessed | tf_op | source)
XLA Modules:
  0.0 489.9 jit_solution(620408272552846810)
XLA Ops:
  0.7 1.9 convert_element_type.106.heads
  2.6 1.6 convert_element_type.107.merge
  4.2 62.4 %bring.1 = (bf16[512,2048]{1,0:T(8,128)(2,1)}, bf16[64,2048]{1,0:T(8,128)(2,1)}, bf16[2048,768]{1,0:T(8,128)(2,1)}, bf16[256,2048]{1,0:T(8,128)(2,1)}) custom-call(bf16[512,256]{1,0:T(8,128)(2,1)} %x.1, bf16[512,256]{1,0:T(8,128)(2,1)} %g.1, bf16[256,768]{1,0:T(8,128)(2,1)} %convert_element_type.106.heads, bf16[256,256]{1,0:T(8,128)(2,1)} %convert_element_type.107.merge), custom_call_target="tpu_custom_call" | custom-call | tf_op jit(solution)/shard_map/bring/pallas_call | solution.py:485
  66.7 4.3 fusion.49
  72.0 15.4 %sums.2 = f32[8,128]{1,0:T(8,128)} custom-call(f32[8,128]{1,0:T(8,128)} %pad_maximum_fusion.10.part), custom_call_target="tpu_custom_call" | custom-call | tf_op jit(solution)/shard_map/sums/pallas_call | solution.py:485
  89.3 1.5 fusion.45
  92.0 1.8 broadcast_multiply_fusion
  95.5 1.6 fusion.5
  97.8 2.1 convolution_convert_fusion.1.part
  99.9 1.8 constant_dynamic-slice_fusion.x
  101.6 2.7 convert_element_type.117.expand
  104.3 0.8 convert_element_type.118.reduce
  105.2 81.9 %merged.1 = (f32[64,2048]{1,0:T(8,128)}, f32[64,2048]{1,0:T(8,128)}, bf16[512,2048]{1,0:T(8,128)(2,1)}, bf16[2048,2048]{1,0:T(8,128)(2,1)}, bf16[1024,2048]{1,0:T(8,128)(2,1)}) custom-call(bf16[512,2048]{1,0:T(8,128)(2,1)} %convolution_convert_fusion.1.part, bf16[64,2048]{1,0:T(8,128)(2,1)} %constant_dynamic-slice_fusion.x, ...), custom_call_target="tpu_custom_call" | custom-call | tf_op jit(solution)/shard_map/merged/pallas_call | solution.py:485
  187.1 179.2 %feed.1 = (bf16[512,256]{1,0:T(8,128)(2,1)}, f32[64,2048]{1,0:T(8,128)}, bf16[512,2048]{1,0:T(8,128)(2,1)}, f32[1,2048]{1,0:T(1,128)}, f32[1,2048]{1,0:T(1,128)}...) custom-call(bf16[512,2048]{1,0:T(8,128)(2,1)} %get-tuple-element.49.rows_in, ...), custom_call_target="tpu_custom_call" | custom-call | tf_op jit(solution)/shard_map/feed/pallas_call | solution.py:485
  366.4 3.4 convolution_convert_fusion.3.merge_part
  376.2 7.9 %sums.3 = f32[8,128]{1,0:T(8,128)} custom-call(f32[8,128]{1,0:T(8,128)} %pad_maximum_fusion.11.part), custom_call_target="tpu_custom_call" | custom-call | tf_op jit(solution)/shard_map/sums/pallas_call | solution.py:485
  384.9 1.4 multiply_convert_fusion.2
  387.0 5.2 %convolution_convert_fusion.heads_part = bf16[2048,768]{1,0:T(8,128)(2,1)} fusion(bf16[512,2048]{1,0:T(8,128)(2,1)} %get-tuple-element.46, bf16[512,256]{1,0:T(8,128)(2,1)S(1)} %copy.89, bf16[512,256]{1,0:T(8,128)(2,1)} %get-tuple-element.100, bf16[512,256]{1,0:T(8,128)(2,1)} %get-tuple-element.99), kind=kOutput, calls=%fused_computation | convolution fusion | flops 1614544896 | bytes 6029312 | tf_op jit(solution)/shard_map/dot_general | solution.py:74
  392.9 5.0 %convolution_convert_fusion.2.part = bf16[512,2048]{1,0:T(8,128)(2,1)} fusion(bf16[2048,768]{1,0:T(8,128)(2,1)} %get-tuple-element.47, bf16[512,256]{1,0:T(8,128)(2,1)S(1)} %copy.89, bf16[512,256]{1,0:T(8,128)(2,1)S(1)} %copy-done.31, bf16[512,256]{1,0:T(8,128)(2,1)S(1)} %copy-done.30), kind=kOutput, calls=%fused_computation.4 | convolution fusion | flops 1614020608 | bytes 6029312 | tf_op jit(solution)/shard_map/dot_general | solution.py:67
  397.9 75.4 %last.1 = (f32[512,256]{1,0:T(8,128)}, f32[8,1024]{1,0:T(8,128)}, bf16[256,768]{1,0:T(8,128)(2,1)}, bf16[256,256]{1,0:T(8,128)(2,1)}) custom-call(bf16[512,2048]{1,0:T(8,128)(2,1)} %convolution_convert_fusion.2.part, f32[64,2048]{1,0:T(8,128)} %get-tuple-element.57.grad_resid, f32[8,1024]{1,0:T(8,128)} %reshape.315.gains, ...), custom_call_target="tpu_custom_call" | custom-call | tf_op jit(solution)/shard_map/last/pallas_call | solution.py:485
  473.4 3.0 fusion.43
  476.5 1.1 fusion.41
  478.5 7.3 %fusion.39 = (bf16[256,2048]{1,0:T(8,128)(2,1)}, f32[256,2048]{1,0:T(8,128)}, f32[256,2048]{1,0:T(8,128)}, f32[256,2048]{1,0:T(8,128)}, f32[256,2048]{1,0:T(8,128)}) fusion(f32[256,2048]{1,0:T(8,128)S(1)} %copy-done.2, f32[256,2048]{1,0:T(8,128)} %param.29, f32[256,2048]{1,0:T(8,128)} %param.28, bf16[256,2048]{1,0:T(8,128)(2,1)} %get-tuple-element.63), kind=kLoop, calls=%fused_computation.114 | loop fusion | flops 8388608 | bytes 16777216 | tf_op jit(solution)/shard_map/convert_element_type | solution.py:1339
  485.9 2.5 fusion.37
  (126 shorter events, 17.2 us)
Async XLA Ops:
  66.6 21.5 %copy-start.36 = (f32[4,2048]{1,0:T(4,128)S(1)}, f32[4,2048]{1,0:T(4,128)}, u32[]{:S(2)}) copy-start(f32[4,2048]{1,0:T(4,128)} %param.33) | copy-start | bytes 98308
  71.0 18.3 %copy-start = (f32[512,768]{1,0:T(8,128)}, f32[512,768]{1,0:T(8,128)S(1)}, u32[]{:S(2)}) copy-start(f32[512,768]{1,0:T(8,128)S(1)} %fusion.49) | copy-start | bytes 4718596
  99.9 4.5 copy-start.3
  187.1 179.3 %copy-start.17 = (bf16[2,128,512]{2,1,0:T(8,128)(2,1)S(1)}, bf16[2,128,512]{2,1,0:T(8,128)(2,1)}, u32[]{:S(2)}) copy-start(bf16[2,128,512]{2,1,0:T(8,128)(2,1)} %copy-done.16) | copy-start | bytes 786436
  366.3 3.5 copy-start.15
  366.4 3.5 copy-start.22
  375.6 10.7 %copy-start.19 = (bf16[512,256]{0,1:T(8,128)(2,1)S(1)}, bf16[512,256]{0,1:T(8,128)(2,1)}, u32[]{:S(2)}) copy-start(bf16[512,256]{0,1:T(8,128)(2,1)} %copy-done.18) | copy-start | bytes 786436
  386.9 5.3 %copy-start.41 = (f32[1,2048]{1,0:T(1,128)S(1)}, f32[1,2048]{1,0:T(1,128)}, u32[]{:S(2)}) copy-start(f32[1,2048]{1,0:T(1,128)} %get-tuple-element.58) | copy-start | bytes 24580
  386.9 5.3 %copy-start.42 = (f32[1,2048]{1,0:T(1,128)S(1)}, f32[1,2048]{1,0:T(1,128)}, u32[]{:S(2)}) copy-start(f32[1,2048]{1,0:T(1,128)} %get-tuple-element.59) | copy-start | bytes 24580
  387.0 5.9 %copy-start.30 = (bf16[512,256]{1,0:T(8,128)(2,1)S(1)}, bf16[512,256]{1,0:T(8,128)(2,1)}, u32[]{:S(2)}) copy-start(bf16[512,256]{1,0:T(8,128)(2,1)} %get-tuple-element.99) | copy-start | bytes 786436
  387.0 5.9 %copy-start.31 = (bf16[512,256]{1,0:T(8,128)(2,1)S(1)}, bf16[512,256]{1,0:T(8,128)(2,1)}, u32[]{:S(2)}) copy-start(bf16[512,256]{1,0:T(8,128)(2,1)} %get-tuple-element.100) | copy-start | bytes 786436
  397.9 75.4 %copy-start.4 = (f32[256,768]{1,0:T(8,128)S(1)}, f32[256,768]{1,0:T(8,128)}, u32[]{:S(2)}) copy-start(f32[256,768]{1,0:T(8,128)} %param.21) | copy-start | bytes 2359300
  397.9 75.4 %copy-start.26 = (f32[256,768]{1,0:T(8,128)S(1)}, f32[256,768]{1,0:T(8,128)}, u32[]{:S(2)}) copy-start(f32[256,768]{1,0:T(8,128)} %param.23) | copy-start | bytes 2359300
  397.9 75.4 %copy-start.27 = (f32[256,768]{1,0:T(8,128)S(1)}, f32[256,768]{1,0:T(8,128)}, u32[]{:S(2)}) copy-start(f32[256,768]{1,0:T(8,128)} %param.22) | copy-start | bytes 2359300
  473.4 3.1 copy-start.23
  473.4 3.1 copy-start.33
  473.4 3.1 copy-start.34
  473.4 3.1 copy-start.35
  473.4 4.2 copy-start.40
  477.6 8.2 %copy-start.37 = (f32[4,2048]{1,0:T(4,128)}, f32[4,2048]{1,0:T(4,128)S(1)}, u32[]{:S(2)}) copy-start(f32[4,2048]{1,0:T(4,128)S(1)} %reshape.316) | copy-start | bytes 98308
  478.5 7.3 %copy-start.24 = (f32[1024,256]{1,0:T(8,128)S(1)}, f32[1024,256]{1,0:T(8,128)}, u32[]{:S(2)}) copy-start(f32[1024,256]{1,0:T(8,128)} %param.32) | copy-start | bytes 3145732
  478.5 7.3 %copy-start.25 = (f32[1024,256]{1,0:T(8,128)S(1)}, f32[1024,256]{1,0:T(8,128)}, u32[]{:S(2)}) copy-start(f32[1024,256]{1,0:T(8,128)} %param.31) | copy-start | bytes 3145732
  478.5 7.3 %copy-start.28 = (bf16[1024,256]{1,0:T(8,128)(2,1)S(1)}, bf16[1024,256]{1,0:T(8,128)(2,1)}, u32[]{:S(2)}) copy-start(bf16[1024,256]{1,0:T(8,128)(2,1)} %get-tuple-element.64) | copy-start | bytes 1572868
  485.9 3.2 copy-start.29
  (20 other events, 30.1 us)

commit v3 on v2

--- a/solution.py
+++ b/solution.py
@@ -56,12 +56,6 @@
     )
 
 
-def allowed_mask(doc_ids, row_count):
-    index_ids = jnp.arange(row_count, dtype=jnp.int32)
-    distance = index_ids[:, None] - index_ids[None, :]
-    return (doc_ids[:, None] == doc_ids[None, :]) & (distance >= 0) & (distance < WINDOW)
-
-
 def product(left_side, right_side, flipped):
     if flipped:
         return lax.dot_general(
@@ -80,35 +74,13 @@
     return rates * (grad_hat - hat_vals * (dots / model_width)[:, None])
 
 
-def attend_forward(queries, key_rows, value_rows, allowed, live_rows):
+def attend_backward(queries, key_rows, value_rows, shares, grad_mix):
     score_scale = queries.shape[-1] ** (-0.5)
-    scores = (
-        jnp.einsum("qhd,khd->hqk", queries, key_rows, preferred_element_type=jnp.float32)
-        * score_scale
-    )
-    scores = jnp.where(allowed[None], scores, -1e30)
-    highest = jnp.max(scores, axis=-1, keepdims=True)
-    weights = jnp.exp(scores - highest)
-    totals = jnp.sum(weights, axis=-1, keepdims=True)
-    shares = (weights / totals).astype(jnp.bfloat16)
-    mixture = jnp.einsum("hqk,khd->qhd", shares, value_rows, preferred_element_type=jnp.float32)
-    return (mixture * live_rows[:, None, None], highest + jnp.log(totals))
-
-
-def attend_backward(queries, key_rows, value_rows, allowed, log_totals, grad_mix):
-    score_scale = queries.shape[-1] ** (-0.5)
-    scores = (
-        jnp.einsum("qhd,khd->hqk", queries, key_rows, preferred_element_type=jnp.float32)
-        * score_scale
-    )
-    scores = jnp.where(allowed[None], scores, -1e30)
-    shares = jnp.exp(scores - log_totals)
     grad_shares = jnp.einsum(
         "qhd,khd->hqk", grad_mix, value_rows, preferred_element_type=jnp.float32
     )
-    grad_values = jnp.einsum(
-        "hqk,qhd->khd", shares.astype(jnp.bfloat16), grad_mix, preferred_element_type=jnp.float32
-    )
+    grad_values = jnp.einsum("hqk,qhd->khd", shares, grad_mix, preferred_element_type=jnp.float32)
+    shares = shares.astype(F32)
     center = jnp.sum(shares * grad_shares, axis=-1, keepdims=True)
     grad_scores = (shares * (grad_shares - center)).astype(jnp.bfloat16)
     grad_queries = (
@@ -507,28 +479,6 @@
     return ref.at[pl.ds(pl.multiple_of(k * count, count), count)]
 
 
-def bring_kernel(x, g, heads, merge, xs, gs, heads_all, merge_all, xsent, xcame, gsent, gcame, wsent, wcame):
-    meet(weights=True, spread_in=True)
-    spread_x = Spread(True, lambda k: x, lambda k: cols(xs, k, 256), xsent, xcame)
-    spread_g = Spread(True, lambda k: rows_of(g, k, 64), lambda k: cols(gs, k, 256), gsent, gcame)
-    gathers = [
-        WeightGather("tall", heads, heads_all, wsent.at[0], wcame.at[0]),
-        WeightGather("wide", merge, merge_all, wsent.at[1], wcame.at[1]),
-    ]
-    spread_x.start()
-    for gather in gathers:
-        gather.start()
-    spread_g.start()
-    for gather in gathers:
-        gather.relay()
-    for gather in gathers:
-        gather.share()
-    spread_x.wait()
-    spread_g.wait()
-    for gather in gathers:
-        gather.wait()
-
-
 def sums_kernel(part, out, came, sent, arrived):
     dp, row, col = here()
     meet(rows=True)
@@ -545,36 +495,6 @@
     out[...] = total
     for copy in copies:
         copy.wait_send()
-
-
-def merged_kernel(
-    part, x, gain, expand, reduce, merged, residual, rows_all, expand_all, reduce_all,
-    came, mine, ssent, scame, gsent, gcame, wsent, wcame,
-):
-    meet(rows=True, weights=True)
-    scatter = RowScatter(part, came, ssent, scame)
-    gather = RowGather(mine, rows_all, gsent, gcame)
-    weights = [
-        WeightGather("tall", expand, expand_all, wsent.at[0], wcame.at[0]),
-        WeightGather("wide", reduce, reduce_all, wsent.at[1], wcame.at[1]),
-    ]
-    scatter.start()
-    for weight in weights:
-        weight.start()
-    for weight in weights:
-        weight.relay()
-    total = scatter.total()
-    merged[...] = total
-    result = x[...].astype(F32) + total * mean_rate(total) * gain[...]
-    residual[...] = result
-    mine[...] = result.astype(BF16)
-    gather.start()
-    for weight in weights:
-        weight.share()
-    scatter.finish()
-    gather.wait()
-    for weight in weights:
-        weight.wait()
 
 
 def back_of(grad, values, gain):
@@ -1072,6 +992,327 @@
     put_rows.wait()
     reduce_sum.wait()
     expand_sum.wait()
+
+
+class Bring:
+    def __init__(self, kind, shard, whole, sent, arrived):
+        dp, _, col = here()
+        rows, width = shard.shape
+        count = rows // 4
+        near = y_peer(col)
+        number = iter(range(28))
+
+        def block(c, s):
+            if kind == "tall":
+                return whole.at[span(4 * c + 2 * dp + s, count)]
+            return whole.at[span(2 * dp + s, count), span(c, width)]
+
+        def copy(source, target, **where):
+            i = next(number)
+            return remote(source, target, sent.at[i], arrived.at[i], **where)
+
+        mine = [shard.at[span(2 * dp + s, count)] for s in range(2)]
+        place = whole.at[span(col, rows)] if kind == "tall" else whole.at[:, span(col, width)]
+        self.local = pltpu.make_async_copy(shard, place, sent.at[28])
+        steps = (1, 3, 2)
+        self.y_own = [copy(mine[s], block(col, s), col=near) for s in range(2)]
+        self.z_own = [[copy(mine[s], block(col, s), col=z_peer(col, d)) for d in steps] for s in range(2)]
+        self.z_near = [copy(block(near, 0), block(near, 0), col=z_peer(col, d)) for d in steps]
+        far = [z_source(col, d) for d in steps]
+        self.y_far = [copy(block(c, 1), block(c, 1), col=near) for c in far]
+
+        def across(c, s):
+            return copy(block(c, s), block(c, s), dp=1 - dp)
+
+        self.a_near = [across(near, s) for s in range(2)]
+        self.a_far = [[across(c, s) for c in far] for s in range(2)]
+        self.a_last = [[across(y_peer(c), s) for c in far] for s in range(2)]
+
+    def start(self):
+        for copy in (self.y_own[0], *self.z_own[1], *self.z_own[0], self.y_own[1], self.local):
+            copy.start()
+
+    def relay(self):
+        self.y_own[0].wait_recv()
+        for copy in (*self.z_near, self.a_near[0]):
+            copy.start()
+
+    def relay_again(self):
+        for i in range(3):
+            self.z_own[1][i].wait_recv()
+            self.y_far[i].start()
+            self.a_far[1][i].start()
+        self.y_own[1].wait_recv()
+        self.a_near[1].start()
+        for i in range(3):
+            self.z_own[0][i].wait_recv()
+            self.a_far[0][i].start()
+
+    def hand_over(self):
+        for i in range(3):
+            self.z_near[i].wait_recv()
+            self.a_last[0][i].start()
+            self.y_far[i].wait_recv()
+            self.a_last[1][i].start()
+
+    def wait(self):
+        for copy in (*self.a_near, *self.a_far[0], *self.a_far[1], *self.a_last[0], *self.a_last[1]):
+            copy.wait()
+        for copy in (*self.y_own, *self.z_own[0], *self.z_own[1], *self.z_near, *self.y_far):
+            copy.wait_send()
+        self.local.wait()
+
+
+def bring_scratch():
+    return [DMA((29,)), DMA((28,))]
+
+
+class SpreadIn:
+    def __init__(self, source, target, sent, arrived):
+        dp, row, col = here()
+        self.row, self.col = row, col
+        self.copies, self.waits = [], []
+        for k in range(8):
+            out = remote(source(k), target(k, col), sent.at[k], arrived.at[col], row=k, col=row)
+            came = remote(source(k), target(row, k), sent.at[k], arrived.at[k], row=k, col=row)
+            local = pltpu.make_async_copy(source(k), target(k, col), sent.at[k])
+            self.copies.append(((row == k) & (row == col), out, local))
+            self.waits.append(((row == col) & (col == k), came))
+
+    def start(self):
+        for mine, out, local in self.copies:
+            pl.when(jnp.logical_not(mine))(out.start)
+            pl.when(mine)(local.start)
+
+    def wait(self):
+        for mine, came in self.waits:
+            pl.when(jnp.logical_not(mine))(came.wait_recv)
+        for mine, out, local in self.copies:
+            pl.when(jnp.logical_not(mine))(out.wait_send)
+            pl.when(mine)(local.wait)
+
+
+class TokenSums:
+    def __init__(self, stats, mine, came, sent, arrived):
+        dp, row, col = here()
+        self.stats, self.mine, self.came = stats, mine, came
+        self.copies = [
+            remote(mine, came.at[d - 1], sent.at[d - 1], arrived.at[d - 1], row=row_peer(row, d))
+            for d in range(1, 8)
+        ]
+
+    def put(self, at, one, two):
+        lane = lax.broadcasted_iota(jnp.int32, (one.shape[0], 128), 1)
+        self.stats[at] = jnp.where(lane == 0, one, jnp.where(lane == 1, two, 0.0))
+
+    def start(self):
+        self.mine[...] = self.stats[...].T[:8]
+        for copy in self.copies:
+            copy.start()
+
+    def end(self):
+        total = self.mine[...]
+        for d, copy in enumerate(self.copies):
+            copy.wait_recv()
+            total = total + self.came[d]
+        self.stats[...] = jnp.concatenate([total] * 16, axis=0).T
+        for copy in self.copies:
+            copy.wait_send()
+
+
+def sums_scratch(tokens):
+    return [pltpu.VMEM((8, tokens), F32), pltpu.VMEM((7, 8, tokens), F32), DMA((7,)), DMA((7,))]
+
+
+def turn(values, cosine, sine):
+    heads = [values[:, i : i + HD] for i in range(0, values.shape[1], HD)]
+    return jnp.concatenate([h * cosine + pltpu.roll(h, HD // 2, 1) * sine for h in heads], axis=1)
+
+
+QUERY_BLOCK = 128
+
+
+def key_span(b):
+    start = max(0, b * QUERY_BLOCK - WINDOW)
+    return start, (b + 1) * QUERY_BLOCK - start
+
+
+def attend_kernel(
+    x, g, heads_in, merge_in, expand_in, reduce_in, cosine, sine, docs, doc_row, gain_query, gain_key, gain_merge,
+    xs_out, share_out, heads_out, merge_out, expand_out, reduce_out, raw_out, qkv_out, probs_out, mix_out, rates_out,
+    merged, residual, rows_out,
+    xs, heads32, merge32, expand32, reduce32, heads16, merge16, expand16, reduce16, heads, merge, raw, qkv, probs, mix,
+    rates, part, rows, load, put, xsent, xcame, gsent, gcame, asent, acame, bsent, bcame, *refs,
+):
+    dp, row, col = here()
+    share, width = merged.shape
+    tokens = xs.shape[0]
+    head_width = mix.shape[1]
+    own = span(row, share)
+    loads = [
+        pltpu.make_async_copy(source, target, load.at[i])
+        for i, (source, target) in enumerate(
+            ((heads_in, heads32), (merge_in, merge32), (reduce_in, reduce32), (expand_in, expand32))
+        )
+    ]
+    for copy in loads:
+        copy.start()
+    spread_x = SpreadIn(
+        lambda k: rows_of(x, k, share), lambda k, c: xs.at[span(k, share), span(c, 256)], xsent, xcame
+    )
+    spread_g = SpreadIn(
+        lambda k: rows_of(g, k, share), lambda k, c: share_out.at[:, span(c, 256)], gsent, gcame
+    )
+    gather_x = Gather(xs, share, asent, acame)
+    gather = Gather(rows, share, bsent, bcame)
+    scatter = Scatter(part, *refs[:8])
+    sums = TokenSums(rates, *refs[8:12])
+    bring_heads = Bring("tall", heads16, heads, *refs[12:14])
+    bring_merge = Bring("wide", merge16, merge, *refs[14:16])
+    bring_reduce = Bring("wide", reduce16, reduce_out, *refs[16:18])
+    bring_expand = Bring("tall", expand16, expand_out, *refs[18:20])
+    puts = [
+        pltpu.make_async_copy(source, target, put.at[i])
+        for i, (source, target) in enumerate(
+            ((xs, xs_out), (heads, heads_out), (merge, merge_out), (raw, raw_out), (qkv, qkv_out),
+             (probs, probs_out), (mix, mix_out), (rates, rates_out), (rows, rows_out))
+        )
+    ]
+
+    def narrow(source, target):
+        @pl.loop(0, source.shape[0] // 16)
+        def _(i):
+            at = span(i, 16)
+            target[at] = source[at].astype(BF16)
+
+    meet(rows=True, weights=True, spread_in=True)
+    spread_x.start()
+    loads[0].wait()
+    narrow(heads32, heads16)
+    bring_heads.start()
+    loads[1].wait()
+    narrow(merge32, merge16)
+    bring_merge.start()
+    loads[2].wait()
+    narrow(reduce32, reduce16)
+    loads[3].wait()
+    narrow(expand32, expand16)
+    spread_x.wait()
+    gather_x.start()
+    bring_heads.relay()
+    gather_x.relay()
+    bring_merge.relay()
+    bring_heads.relay_again()
+    gather_x.relay_again()
+    bring_heads.hand_over()
+    bring_reduce.start()
+    bring_expand.start()
+    spread_g.start()
+    gather_x.wait()
+    bring_heads.wait()
+    puts[0].start()
+    puts[1].start()
+
+    for i in range(2):
+        raw[:, i * head_width : (i + 1) * head_width] = dot(
+            xs[...], heads[:, i * head_width : (i + 1) * head_width]
+        )
+
+    @pl.loop(0, tokens // 64)
+    def _(i):
+        at = span(i, 64)
+        squares = raw[at] * raw[at]
+        sums.put(
+            at,
+            jnp.sum(squares[:, :head_width], axis=1, keepdims=True),
+            jnp.sum(squares[:, head_width:], axis=1, keepdims=True),
+        )
+
+    sums.start()
+    qkv[:, 2 * head_width :] = dot(xs[...], heads[:, 2 * head_width :]).astype(BF16)
+    bring_merge.relay_again()
+    bring_expand.relay()
+    bring_reduce.relay()
+    bring_merge.hand_over()
+    sums.end()
+
+    @pl.loop(0, tokens // 64)
+    def _(i):
+        at = span(i, 64)
+        rate = lax.rsqrt(rates[at] * (1.0 / width) + EPS)
+        rates[at] = rate
+        for j, gain in enumerate((gain_query, gain_key)):
+            some = slice(j * head_width, (j + 1) * head_width)
+            hat = raw[at, some] * rate[:, j : j + 1]
+            qkv[at, some] = turn(hat * gain[...], cosine[at], sine[at]).astype(BF16)
+
+    puts[3].start()
+    puts[4].start()
+    puts[7].start()
+    for b in range(tokens // QUERY_BLOCK):
+        start, count = key_span(b)
+        query_at = pl.ds(b * QUERY_BLOCK, QUERY_BLOCK)
+        key_at = pl.ds(start, count)
+        there = lax.broadcasted_iota(jnp.int32, (QUERY_BLOCK, count), 0) + (b * QUERY_BLOCK - start)
+        distance = there - lax.broadcasted_iota(jnp.int32, (QUERY_BLOCK, count), 1)
+        doc = docs[query_at, 0:1]
+        allowed = (doc == doc_row[0:1, start : start + count]) & (distance >= 0) & (distance < WINDOW)
+        live = (doc < 5.0).astype(F32)
+        for h in range(head_width // HD):
+            query, key, value = (
+                slice(i * head_width + h * HD, i * head_width + (h + 1) * HD) for i in range(3)
+            )
+            scores = dot_flipped(qkv[query_at, query], qkv[key_at, key]) * HD**-0.5
+            scores = jnp.where(allowed, scores, -1e30)
+            weights = jnp.exp(scores - jnp.max(scores, axis=1, keepdims=True))
+            shares = (weights / jnp.sum(weights, axis=1, keepdims=True)).astype(BF16)
+            probs[h, b, :, :count] = shares
+            if count < probs.shape[3]:
+                probs[h, b, :, count:] = jnp.zeros((QUERY_BLOCK, probs.shape[3] - count), BF16)
+            mix[query_at, h * HD : (h + 1) * HD] = (dot(shares, qkv[key_at, value]) * live).astype(BF16)
+
+    puts[5].start()
+    puts[6].start()
+    bring_merge.wait()
+    puts[2].start()
+
+    def merge_part(j):
+        at = span(j, 256)
+        part[:, at] = dot(mix[...], merge[:, at]).astype(BF16)
+
+    n = width // 512
+    pl.loop(n, 2 * n)(merge_part)
+    scatter.start_right()
+    pl.loop(0, n)(merge_part)
+    scatter.start_left()
+    bring_expand.relay_again()
+    scatter.middle()
+    bring_reduce.relay_again()
+    scatter.end()
+
+    @pl.loop(0, share // 16)
+    def _(i):
+        at = span(i, 16)
+        total = scatter.total[at]
+        merged[at] = total
+        mine = pl.ds(pl.multiple_of(row * share + i * 16, 16), 16)
+        result = xs[mine, :].astype(F32) + total * mean_rate(total) * gain_merge[...]
+        residual[at] = result
+        rows[mine, :] = result.astype(BF16)
+
+    gather.start()
+    gather.relay()
+    bring_expand.hand_over()
+    gather.relay_again()
+    bring_reduce.hand_over()
+    gather.wait()
+    puts[8].start()
+    scatter.finish()
+    spread_g.wait()
+    bring_expand.wait()
+    bring_reduce.wait()
+    for copy in puts:
+        copy.wait()
 
 
 def last_kernel(
@@ -1163,7 +1404,6 @@
     share = seq_len // lax.axis_size("row")
     head_count = head_width // HD
     doc_ids, places, live_rows = positions(doc_lengths[0], seq_len)
-    allowed = allowed_mask(doc_ids, seq_len)
     gain_query = lax.dynamic_slice_in_dim(norm_gains[0], row_at * head_width, head_width)
     gain_key = lax.dynamic_slice_in_dim(norm_gains[1], row_at * head_width, head_width)
     gain_merge, gain_reduce = norm_gains[2:3], norm_gains[3:4]
@@ -1179,18 +1419,74 @@
         DMA((7,)),
     ]
 
-    input_rows, cot_share, heads_low, merge_low = call(
-        bring_kernel, "bring", 1,
-        [rows_shape, struct((share, model_width), BF16), struct((model_width, 3 * head_width), BF16),
-         struct((head_width, model_width), BF16)],
-        [block_input, cotangent, heads_weight.astype(BF16), merge_weight.astype(BF16)],
-        [ANY] * 4, [ANY] * 4,
-        [DMA((8,)), DMA((8,)), DMA((8,)), DMA((8,))] + gather_sems(2),
-    )
-    joined_cols = product(input_rows, heads_low, False)
-    queries = joined_cols[:, :head_width]
-    key_rows = joined_cols[:, head_width : 2 * head_width]
-    value_rows = joined_cols[:, 2 * head_width :]
+    half_dim = HD // 2
+    frequency = THETA ** (-2.0 * jnp.arange(half_dim, dtype=F32) / HD)
+    angles = places.astype(F32)[:, None] * frequency[None, :]
+    cosine, sine = jnp.cos(angles), jnp.sin(angles)
+    cosine = jnp.concatenate([cosine, cosine], axis=1)
+    sine = jnp.concatenate([-sine, sine], axis=1)
+    docs = jnp.broadcast_to(doc_ids.astype(F32)[:, None], (seq_len, 128))
+    doc_row = jnp.broadcast_to(doc_ids.astype(F32)[None, :], (8, seq_len))
+    blocks = seq_len // QUERY_BLOCK
+
+    (
+        input_rows, cot_share, heads_low, merge_low, expand_low, reduce_low, raw, qkv, probs, mixture_low, rates,
+        merged, residual, residual_rows,
+    ) = call(
+        attend_kernel, "attend", 1,
+        [
+            rows_shape,
+            struct((share, model_width), BF16),
+            struct((model_width, 3 * head_width), BF16),
+            struct((head_width, model_width), BF16),
+            struct((model_width, 2 * unit_width), BF16),
+            struct((unit_width, model_width), BF16),
+            struct((seq_len, 2 * head_width), F32),
+            struct((seq_len, 3 * head_width), BF16),
+            struct((head_count, blocks, QUERY_BLOCK, WINDOW + QUERY_BLOCK), BF16),
+            struct((seq_len, head_width), BF16),
+            struct((seq_len, 128), F32),
+            mine_f32,
+            mine_f32,
+            rows_shape,
+        ],
+        [
+            block_input, cotangent, heads_weight, merge_weight, expand_weight, reduce_weight, cosine, sine, docs,
+            doc_row, gain_query[None], gain_key[None], gain_merge,
+        ],
+        [ANY] * 6 + [VMEM] * 7,
+        [ANY] * 11 + [VMEM] * 2 + [ANY],
+        [
+            pltpu.VMEM((seq_len, model_width), BF16),
+            pltpu.VMEM(heads_weight.shape, F32),
+            pltpu.VMEM(merge_weight.shape, F32),
+            pltpu.VMEM(expand_weight.shape, F32),
+            pltpu.VMEM(reduce_weight.shape, F32),
+            pltpu.VMEM(heads_weight.shape, BF16),
+            pltpu.VMEM(merge_weight.shape, BF16),
+            pltpu.VMEM(expand_weight.shape, BF16),
+            pltpu.VMEM(reduce_weight.shape, BF16),
+            pltpu.VMEM((model_width, 3 * head_width), BF16),
+            pltpu.VMEM((head_width, model_width), BF16),
+            pltpu.VMEM((seq_len, 2 * head_width), F32),
+            pltpu.VMEM((seq_len, 3 * head_width), BF16),
+            pltpu.VMEM((head_count, blocks, QUERY_BLOCK, WINDOW + QUERY_BLOCK), BF16),
+            pltpu.VMEM((seq_len, head_width), BF16),
+            pltpu.VMEM((seq_len, 128), F32),
+            pltpu.VMEM((seq_len, model_width), BF16),
+            pltpu.VMEM((seq_len, model_width), BF16),
+            DMA((4,)), DMA((9,)), DMA((8,)), DMA((8,)), DMA((8,)), DMA((8,)),
+        ]
+        + gather_scratch() + gather_scratch()
+        + scatter_scratch(share, model_width) + sums_scratch(seq_len)
+        + bring_scratch() + bring_scratch() + bring_scratch() + bring_scratch(),
+    )
+    query_rate, key_rate = rates[:, 0:1], rates[:, 1:2]
+    query_hat = raw[:, :head_width] * query_rate
+    key_hat = raw[:, head_width:] * key_rate
+    query_low, key_low, value_low = (
+        qkv[:, i * head_width : (i + 1) * head_width].reshape(seq_len, head_count, HD) for i in range(3)
+    )
 
     def head_sums(one, two, number):
         part = jnp.concatenate([one, two]).reshape(8, 128)
@@ -1200,33 +1496,6 @@
         ).reshape(2, seq_len)
         return total[0], total[1]
 
-    query_sq, key_sq = head_sums(
-        jnp.sum(queries * queries, axis=1), jnp.sum(key_rows * key_rows, axis=1), 2
-    )
-    query_rate = lax.rsqrt(query_sq / model_width + EPS)[:, None]
-    key_rate = lax.rsqrt(key_sq / model_width + EPS)[:, None]
-    query_hat = queries * query_rate
-    key_hat = key_rows * key_rate
-    query_low = rotate(
-        (query_hat * gain_query).reshape(seq_len, head_count, HD), places, 1.0
-    ).astype(jnp.bfloat16)
-    key_low = rotate((key_hat * gain_key).reshape(seq_len, head_count, HD), places, 1.0).astype(
-        jnp.bfloat16
-    )
-    value_low = value_rows.reshape(seq_len, head_count, HD).astype(jnp.bfloat16)
-    mixture, log_totals = attend_forward(query_low, key_low, value_low, allowed, live_rows)
-    mixture_low = mixture.reshape(seq_len, head_width).astype(jnp.bfloat16)
-    merged_part = product(mixture_low, merge_low, False).astype(BF16)
-
-    input_share = lax.dynamic_slice_in_dim(input_rows, row_at * share, share)
-    merged, residual, residual_rows, expand_low, reduce_low = call(
-        merged_kernel, "merged", 3,
-        [mine_f32, mine_f32, rows_shape, struct((model_width, 2 * unit_width), BF16),
-         struct((unit_width, model_width), BF16)],
-        [merged_part, input_share, gain_merge, expand_weight.astype(BF16), reduce_weight.astype(BF16)],
-        [VMEM, VMEM, VMEM, ANY, ANY], [VMEM, VMEM, ANY, ANY, ANY],
-        row_scratch + gather_sems(2),
-    )
     block_output, grad_resid, merged_grad_rows, merge_gain_part, reduce_gain_part, expand_grad, reduce_grad = call(
         feed_kernel, "feed", 4,
         [struct(block_input.shape, BF16), mine_f32, rows_shape, line, line, struct(expand_weight.shape, BF16),
@@ -1262,9 +1531,11 @@
         grad_mixture.astype(jnp.bfloat16).reshape(seq_len, head_count, HD)
         * live_rows.astype(jnp.bfloat16)[:, None, None]
     )
-    grad_queries, grad_keys, grad_values = attend_backward(
-        query_low, key_low, value_low, allowed, log_totals, grad_mix_low
-    )
+    shares = jnp.zeros((head_count, seq_len, seq_len), BF16)
+    for b in range(blocks):
+        start, count = key_span(b)
+        shares = lax.dynamic_update_slice(shares, probs[:, b, :, :count], (0, b * QUERY_BLOCK, start))
+    grad_queries, grad_keys, grad_values = attend_backward(query_low, key_low, value_low, shares, grad_mix_low)
     query_norm_grad = rotate(grad_queries, places, -1.0).reshape(seq_len, head_width)
     key_norm_grad = rotate(grad_keys, places, -1.0).reshape(seq_len, head_width)
     query_gain_part = jnp.sum(query_norm_grad * query_hat, axis=0)

time: 491 us -> 434 us (0.88)
  Pallas kernels: 422 us -> 386 us
  other arithmetic: 31 us -> 19.4 us
  matrix products: 25.3 us -> 14.5 us
    pallas_call x6 -> x4, Pallas kernels: 422 us -> 386 us  [call(): pl.pallas_call(kernel, name=name, out_shape=outs, in_specs=in_specs, out_...]
    dot_general x5 -> x1, matrix products: 9.21 us -> 0.31 us  [attend_backward(): jnp.einsum('hqk,qhd->khd', shares, grad_mix, preferred_element_type=jnp.f...]
    convert_element_type x5 -> x2, other arithmetic: 7.1 us -> 0.01 us  [the longest x1 0.01 us: on_device(): angles = places.astype(F32)[:, None] * frequency[None, :]]
where the time goes in v3:
time: 434 us; the launch traced here: 433 us
  Pallas kernels  386 us (89%)
  other arithmetic  19.4 us (4%)
  matrix products  14.5 us (3%)
  local copies, waits for them, and re-layouts  11.8 us (3%)
    pallas_call x4, Pallas kernels, call(): pl.pallas_call(kernel, name=name, out_shape=outs, in_specs=in_specs, out_...  386 us

profile of v3, /device:TPU:9, one launch (start us, length us, event | category | flops | bytes accessed | tf_op | source)
XLA Modules:
  0.0 433.4 jit_solution(9143921932940934096)
XLA Ops:
  0.7 0.8 reduce-window.8
  1.5 0.7 convert_reduce_fusion
  2.9 1.5 fusion.30
  5.0 0.8 broadcast_in_dim.23.docs
  5.8 1.0 fusion.13
  7.1 1.0 pad_maximum_fusion.5
  8.1 127.2 %attend.1 = (bf16[512,2048]{1,0:T(8,128)(2,1)}, bf16[64,2048]{1,0:T(8,128)(2,1)}, bf16[2048,768]{1,0:T(8,128)(2,1)}, bf16[256,2048]{1,0:T(8,128)(2,1)}, bf16[204...) custom-call(bf16[512,256]{1,0:T(8,128)(2,1)} %x.3, ...), custom_call_target="tpu_custom_call" | custom-call | tf_op jit(solution)/shard_map/attend/pallas_call | solution.py:457
  135.3 176.6 %feed.1 = (bf16[512,256]{1,0:T(8,128)(2,1)}, f32[64,2048]{1,0:T(8,128)}, bf16[512,2048]{1,0:T(8,128)(2,1)}, f32[1,2048]{1,0:T(1,128)}, f32[1,2048]{1,0:T(1,128)}...) custom-call(bf16[512,2048]{1,0:T(8,128)(2,1)} %get-tuple-element.51.rows_in, ...), custom_call_target="tpu_custom_call" | custom-call | tf_op jit(solution)/shard_map/feed/pallas_call | solution.py:457
  311.9 2.5 convolution_convert_fusion.4
  314.8 1.7 convolution_convert_fusion.2.merge_part
  317.3 0.8 copy.95
  323.1 8.8 %sums.1 = f32[8,128]{1,0:T(8,128)} custom-call(f32[8,128]{1,0:T(8,128)} %pad_maximum_fusion.8.part), custom_call_target="tpu_custom_call" | custom-call | tf_op jit(solution)/shard_map/sums/pallas_call | solution.py:457
  331.9 0.8 multiply_bitcast_fusion.1
  333.0 5.2 %convolution_convert_fusion.1.part = bf16[512,2048]{1,0:T(8,128)(2,1)} fusion(bf16[2048,768]{1,0:T(8,128)(2,1)} %get-tuple-element.64, bf16[512,256]{1,0:T(8,128)(2,1)S(1)} %copy-done.19, bf16[512,256]{1,0:T(8,128)(2,1)S(1)} %get-tuple-element.110, bf16[512,256]{1,0:T(8,128)(2,1)S(1)} %get-tuple-element.109), kind=kOutput, calls=%fused_computation.3 | convolution fusion | flops 1614020608 | bytes 6029312 | tf_op jit(solution)/shard_map/dot_general | solution.py:61
  338.2 3.5 convolution_convert_fusion.heads_part
  341.7 73.9 %last.1 = (f32[512,256]{1,0:T(8,128)}, f32[8,1024]{1,0:T(8,128)}, bf16[256,768]{1,0:T(8,128)(2,1)}, bf16[256,256]{1,0:T(8,128)(2,1)}) custom-call(bf16[512,2048]{1,0:T(8,128)(2,1)} %convolution_convert_fusion.1.part, f32[64,2048]{1,0:T(8,128)} %get-tuple-element.65.grad_resid, f32[8,1024]{1,0:T(8,128)} %reshape.212.gains, ...), custom_call_target="tpu_custom_call" | custom-call | tf_op jit(solution)/shard_map/last/pallas_call | solution.py:457
  415.7 0.9 reshape.213
  417.4 2.0 fusion.25
  419.4 3.1 fusion.27
  422.6 2.7 fusion.21
  425.2 1.2 copy-done.5
  427.3 4.6 %fusion.23 = (bf16[256,2048]{1,0:T(8,128)(2,1)}, f32[256,2048]{1,0:T(8,128)}, f32[256,2048]{1,0:T(8,128)}, f32[256,2048]{1,0:T(8,128)}, f32[256,2048]{1,0:T(8,128)}) fusion(f32[256,2048]{1,0:T(8,128)S(1)} %copy-done, f32[256,2048]{1,0:T(8,128)S(1)} %copy-done.5, f32[256,2048]{1,0:T(8,128)S(1)} %copy-done.6, bf16[256,2048]{1,0:T(8,128)(2,1)S(1)} %copy-done.7), kind=kLoop, calls=%fused_computation.84 | loop fusion | flops 8388608 | bytes 16777216 | tf_op jit(solution)/shard_map/convert_element_type | solution.py:1610
  431.9 0.7 copy.109
  432.6 0.8 copy.110
  (100 shorter events, 9.3 us)
Async XLA Ops:
  135.3 176.6 %copy-start.32 = (bf16[256,2048]{1,0:T(8,128)(2,1)S(1)}, bf16[256,2048]{1,0:T(8,128)(2,1)}, u32[]{:S(2)}) copy-start(bf16[256,2048]{1,0:T(8,128)(2,1)} %get-tuple-element.62) | copy-start | bytes 3145732
  311.9 2.9 copy-start.4
  311.9 2.9 copy-start.22
  321.3 11.7 %copy-start.19 = (bf16[512,256]{1,0:T(8,128)(2,1)S(1)}, bf16[512,256]{1,0:T(8,128)(2,1)}, u32[]{:S(2)}) copy-start(bf16[512,256]{1,0:T(8,128)(2,1)} %copy.95) | copy-start | bytes 786436
  333.0 5.2 %copy-start.31 = (bf16[512,2048]{1,0:T(8,128)(2,1)S(1)}, bf16[512,2048]{1,0:T(8,128)(2,1)}, u32[]{:S(2)}) copy-start(bf16[512,2048]{1,0:T(8,128)(2,1)} %get-tuple-element.68) | copy-start | bytes 6291460
  341.7 74.9 %copy-start.23 = (f32[4,2048]{1,0:T(4,128)S(1)}, f32[4,2048]{1,0:T(4,128)}, u32[]{:S(2)}) copy-start(f32[4,2048]{1,0:T(4,128)} %param.33) | copy-start | bytes 98308
  341.7 74.9 %copy-start.25 = (f32[4,2048]{1,0:T(4,128)S(1)}, f32[4,2048]{1,0:T(4,128)}, u32[]{:S(2)}) copy-start(f32[4,2048]{1,0:T(4,128)} %param.35) | copy-start | bytes 98308
  341.7 75.0 %copy-start.26 = (f32[4,2048]{1,0:T(4,128)S(1)}, f32[4,2048]{1,0:T(4,128)}, u32[]{:S(2)}) copy-start(f32[4,2048]{1,0:T(4,128)} %param.34) | copy-start | bytes 98308
  341.7 75.7 %copy-start.9 = (f32[256,256]{1,0:T(8,128)S(1)}, f32[256,256]{1,0:T(8,128)}, u32[]{:S(2)}) copy-start(f32[256,256]{1,0:T(8,128)} %merge_in.1) | copy-start | bytes 786436
  341.7 75.7 %copy-start.20 = (f32[256,256]{1,0:T(8,128)S(1)}, f32[256,256]{1,0:T(8,128)}, u32[]{:S(2)}) copy-start(f32[256,256]{1,0:T(8,128)} %param.26) | copy-start | bytes 786436
  341.7 75.6 %copy-start.21 = (f32[256,256]{1,0:T(8,128)S(1)}, f32[256,256]{1,0:T(8,128)}, u32[]{:S(2)}) copy-start(f32[256,256]{1,0:T(8,128)} %param.25) | copy-start | bytes 786436
  415.7 3.7 copy-start.3
  415.7 3.7 copy-start.12
  415.7 3.6 copy-start.13
  416.6 5.9 %copy-start.24 = (f32[4,2048]{1,0:T(4,128)}, f32[4,2048]{1,0:T(4,128)S(1)}, u32[]{:S(2)}) copy-start(f32[4,2048]{1,0:T(4,128)S(1)} %reshape.213) | copy-start | bytes 98308
  419.3 3.2 copy-start.2
  419.3 3.2 copy-start.10
  419.4 3.2 copy-start.11
  419.4 3.2 copy-start.15
  422.5 3.9 copy-start.5
  422.6 4.5 %copy-start.6 = (f32[256,2048]{1,0:T(8,128)S(1)}, f32[256,2048]{1,0:T(8,128)}, u32[]{:S(2)}) copy-start(f32[256,2048]{1,0:T(8,128)} %param.28) | copy-start | bytes 6291460
  422.6 4.7 %copy-start.7 = (bf16[256,2048]{1,0:T(8,128)(2,1)S(1)}, bf16[256,2048]{1,0:T(8,128)(2,1)}, u32[]{:S(2)}) copy-start(bf16[256,2048]{1,0:T(8,128)(2,1)} %get-tuple-element.73) | copy-start | bytes 3145732
  427.3 4.6 %copy-start.18 = (bf16[512,256]{1,0:T(8,128)(2,1)S(1)}, bf16[512,256]{1,0:T(8,128)(2,1)}, u32[]{:S(2)}) copy-start(bf16[512,256]{1,0:T(8,128)(2,1)} %get-tuple-element.162) | copy-start | bytes 786436
  427.3 5.3 %copy-start.16 = (f32[512,256]{1,0:T(8,128)S(1)}, f32[512,256]{1,0:T(8,128)}, u32[]{:S(2)}) copy-start(f32[512,256]{1,0:T(8,128)} %get-tuple-element.163) | copy-start | bytes 1572868
  (9 other events, 16.8 us)

commit v4 on v3

v4 whole, which is shorter than its diff:
```python
import functools

import jax
import jax.numpy as jnp
from jax import lax
from jax.experimental import pallas as pl
from jax.experimental.pallas import tpu as pltpu
from jax.sharding import PartitionSpec as P

HD = 128
WINDOW = 256
STEP = 5


EPS = 1e-06
THETA = 500000.0
LR = 0.02
LR_GAIN = 0.2
BETA_ONE = 0.5
BETA_TWO = 0.5
DECAY = 0.1
ADAM_EPS = 1e-08

BF16 = jnp.bfloat16
F32 = jnp.float32
MESH = pl.DeviceIdType.MESH
ANY = pl.BlockSpec(memory_space=pl.ANY)
VMEM = pl.BlockSpec(memory_space=pltpu.VMEM)
DMA = pltpu.SemaphoreType.DMA


def positions(lengths, row_count):
    doc_ends = jnp.cumsum(lengths)
    index_ids = jnp.arange(row_count, dtype=jnp.int32)
    passed = doc_ends[None, :] <= index_ids[:, None]
    doc_ids = jnp.sum(passed.astype(jnp.int32), axis=1)
    starts = jnp.sum(jnp.where(passed, lengths[None, :], 0), axis=1)
    live_rows = (doc_ids < lengths.shape[0] - 1).astype(jnp.float32)
    return (doc_ids, index_ids - starts, live_rows)


def adamw(weight, gradient, first_mom, second_mom, step_rate, decay_rate):
    mean_new = BETA_ONE * first_mom + (1.0 - BETA_ONE) * gradient
    square_new = BETA_TWO * second_mom + (1.0 - BETA_TWO) * gradient * gradient
    fix_one = 1.0 - BETA_ONE**STEP
    fix_two = 1.0 - BETA_TWO**STEP
    update = mean_new / fix_one / (jnp.sqrt(square_new / fix_two) + ADAM_EPS) + decay_rate * weight
    return (mean_new, square_new, weight - step_rate * update)


def here():
    return lax.axis_index("dp"), lax.axis_index("row"), lax.axis_index("col")


def row_peer(row, d):
    return (row // 4 + d // 4) % 2 * 4 + (row % 4 + d % 4) % 4


def z_peer(col, d):
    return (col // 2 + d) % 4 * 2 + col % 2


def z_source(col, d):
    return (col // 2 + 4 - d) % 4 * 2 + col % 2


def y_peer(col):
    return col // 2 * 2 + 1 - col % 2


def remote(source, target, sent, arrived, **where):
    return pltpu.make_async_remote_copy(
        src_ref=source,
        dst_ref=target,
        send_sem=sent,
        recv_sem=arrived,
        device_id=where,
        device_id_type=MESH,
    )


def meet(rows=False, cols=False, weights=False, core=False, spread_in=False, spread_out=False):
    dp, row, col = here()
    barrier = pltpu.get_barrier_semaphore()
    count = 0

    def greet(**where):
        pl.semaphore_signal(barrier, inc=1, device_id=where, device_id_type=MESH)

    if rows:
        for d in range(1, 8):
            greet(row=row_peer(row, d))
        count = count + 7
    if cols:
        for d in range(1, 8):
            greet(col=(col + d) % 8)
        count = count + 7
    if weights:
        greet(col=y_peer(col))
        for d in (1, 3):
            greet(col=z_peer(col, d))
        count = count + 3
    if core:
        greet(dp=1 - dp)
        count = count + 1
    for wanted, inward in ((spread_in, True), (spread_out, False)):
        if wanted:
            for k in range(8):
                at_row, at_col = (col, k) if inward else (k, row)

                @pl.when(jnp.logical_not((at_row == row) & (at_col == col)))
                def _():
                    greet(row=at_row, col=at_col)

            count = count + 8 - (row == col).astype(jnp.int32)
    pl.semaphore_wait(barrier, count)


class Spread:
    def __init__(self, inward, source, target, sent, arrived):
        dp, row, col = here()
        self.row, self.col, self.inward = row, col, inward
        self.copies = []
        for k in range(8):
            to_row, to_col = (k, row) if inward else (col, k)
            mine = (row == to_row) & (col == to_col)
            copy = remote(
                source(k),
                target(col if inward else row),
                sent.at[k],
                arrived.at[col if inward else row],
                row=to_row,
                col=to_col,
            )
            waiter = remote(source(k), target(k), sent.at[k], arrived.at[k], row=to_row, col=to_col)
            local = pltpu.make_async_copy(
                source(k), target(col if inward else row), sent.at[k]
            )
            self.copies.append((mine, copy, waiter, local))

    def start(self):
        for mine, copy, _, local in self.copies:
            pl.when(jnp.logical_not(mine))(copy.start)
            pl.when(mine)(local.start)

    def wait(self):
        for k, (mine, copy, waiter, local) in enumerate(self.copies):
            from_row, from_col = (self.col, k) if self.inward else (k, self.row)
            me = (from_row == self.row) & (from_col == self.col)
            pl.when(jnp.logical_not(me))(waiter.wait_recv)
            pl.when(jnp.logical_not(mine))(copy.wait_send)
            pl.when(mine)(local.wait)


def half_of(kind, ref, c, h):
    if kind == "tall":
        count = ref.shape[0] // 16
        return ref.at[pl.ds(pl.multiple_of((2 * c + h) * count, count), count)]
    count, width = ref.shape[0] // 2, ref.shape[1] // 8
    return ref.at[
        pl.ds(pl.multiple_of(h * count, count), count), pl.ds(pl.multiple_of(c * width, width), width)
    ]


def half_shard(ref, h):
    count = ref.shape[0] // 2
    return ref.at[pl.ds(pl.multiple_of(h * count, count), count)]


def mean_rate(values):
    return lax.rsqrt(jnp.mean(values * values, axis=-1, keepdims=True) + EPS)


def call(kernel, name, number, outs, ins, in_specs, out_specs, scratch):
    return pl.pallas_call(
        kernel,
        name=name,
        out_shape=outs,
        in_specs=in_specs,
        out_specs=out_specs,
        scratch_shapes=scratch,
        compiler_params=pltpu.CompilerParams(
            collective_id=number, has_side_effects=True, vmem_limit_bytes=62 * 2**20
        ),
    )(*ins)


def struct(shape, kind):
    return jax.ShapeDtypeStruct(shape, kind)


def dot(left, right):
    return jnp.dot(left, right, preferred_element_type=F32)


def dot_flipped(left, right):
    return lax.dot_general(left, right, (((1,), (1,)), ((), ())), preferred_element_type=F32)


def span(k, count):
    return pl.ds(pl.multiple_of(k * count, count), count)


def near_row(row, dx, dy):
    return (row // 4 + dy) % 2 * 4 + (row % 4 + dx) % 4


class Scatter:
    def __init__(self, part, total, from_y, from_x, last_y, last_x, stage, sent, arrived):
        dp, row, col = here()
        self.row, self.part, self.total = row, part, total
        self.from_y, self.from_x, self.last_y, self.last_x, self.stage = from_y, from_x, last_y, last_x, stage
        self.count, self.half = total.shape[0], total.shape[1] // 2
        number = iter(range(14))

        def copy(source, target, dx, dy):
            i = next(number)
            return remote(source, target, sent.at[i], arrived.at[i], row=near_row(row, dx, dy))

        self.y_first = {dx: copy(self.block(dx, 1, 1), from_y.at[dx], 0, 1) for dx in (1, 3, 2, 0)}
        self.x_first = {
            (dx, dy): copy(self.block(dx, dy, 0), from_x.at[dy, dx - 1], dx, 0)
            for dy in (1, 0)
            for dx in (1, 3, 2)
        }
        self.x_last = {dx: copy(stage.at[dx], last_x.at[dx - 1], dx, 0) for dx in (1, 3, 2)}
        self.y_last = copy(stage.at[0], last_y, 0, 1)

    def block(self, dx, dy, side):
        return self.part.at[
            span(near_row(self.row, dx, dy), self.count), pl.ds(side * self.half, self.half)
        ]

    def start_right(self):
        for copy in self.y_first.values():
            copy.start()

    def start_left(self):
        for copy in self.x_first.values():
            copy.start()

    def chunks(self, body):
        @pl.loop(0, self.count // 16)
        def _(i):
            body(span(i, 16))

    def middle(self):
        for dx in (1, 3, 2):
            self.y_first[dx].wait_recv()
            own = self.block(dx, 0, 1)

            def add(at):
                self.stage[dx, at] = (own[at].astype(F32) + self.from_y[dx, at].astype(F32)).astype(BF16)

            self.chunks(add)
            self.x_last[dx].start()
        for dx in (1, 3, 2):
            self.x_first[dx, 1].wait_recv()
        other = self.block(0, 1, 0)

        def add(at):
            total = other[at].astype(F32)
            for k in range(3):
                total = total + self.from_x[1, k, at].astype(F32)
            self.stage[0, at] = total.astype(BF16)

        self.chunks(add)
        self.y_last.start()

    def end(self):
        self.y_first[0].wait_recv()
        for dx in (1, 3, 2):
            self.x_first[dx, 0].wait_recv()
            self.x_last[dx].wait_recv()
        self.y_last.wait_recv()
        left, right = self.block(0, 0, 0), self.block(0, 0, 1)

        def add(at):
            total = left[at].astype(F32) + self.last_y[at].astype(F32)
            for k in range(3):
                total = total + self.from_x[0, k, at].astype(F32)
            self.total[at, : self.half] = total
            total = right[at].astype(F32) + self.from_y[0, at].astype(F32)
            for k in range(3):
                total = total + self.last_x[k, at].astype(F32)
            self.total[at, self.half :] = total

        self.chunks(add)

    def finish(self):
        for copies in (self.y_first, self.x_first, self.x_last):
            for copy in copies.values():
                copy.wait_send()
        self.y_last.wait_send()


def scatter_scratch(share, width):
    half = width // 2
    return [
        pltpu.VMEM((share, width), F32),
        pltpu.VMEM((4, share, half), BF16),
        pltpu.VMEM((2, 3, share, half), BF16),
        pltpu.VMEM((share, half), BF16),
        pltpu.VMEM((3, share, half), BF16),
        pltpu.VMEM((4, share, half), BF16),
        DMA((14,)),
        DMA((14,)),
    ]


class Gather:
    def __init__(self, whole, share, sent, arrived):
        dp, row, col = here()
        self.row = row
        half = whole.shape[1] // 2
        number = iter(range(19))

        def copy(fx, fy, side, dx, dy, start=0, count=share):
            i = next(number)
            k = near_row(row, fx, fy)
            ref = whole.at[
                pl.ds(pl.multiple_of(k * share + start, count), count), pl.ds(side * half, half)
            ]
            return remote(ref, ref, sent.at[i], arrived.at[i], row=near_row(row, dx, dy))

        part = share // 2
        self.y_own = [copy(0, 0, 0, 0, 1), copy(0, 0, 1, 0, 1)]
        self.x_own = [[copy(0, 0, side, dx, 0) for dx in (1, 3)] for side in range(2)]
        self.x_other = [copy(0, 1, 0, dx, 0) for dx in (1, 3)]
        self.on = [
            [copy(4 - dx, 0, side, dx, 0, i * part, part) for i, dx in enumerate((1, 3))]
            for side in range(2)
        ]
        self.on_other = [copy(4 - dx, 1, 0, dx, 0, i * part, part) for i, dx in enumerate((1, 3))]
        self.y_near = [copy(4 - dx, 0, 1, 0, 1) for dx in (1, 3)]
        self.y_far = [copy(2, 0, 1, 0, 1, i * part, part) for i in range(2)]

    def start(self):
        for copy in (self.y_own[0], *self.x_own[1], self.y_own[1], *self.x_own[0]):
            copy.start()

    def relay(self):
        self.y_own[0].wait_recv()
        for copy in self.x_other:
            copy.start()
        for i in range(2):
            self.x_own[1][i].wait_recv()
            self.on[1][i].start()
            self.y_near[i].start()

    def relay_again(self):
        for i in range(2):
            self.x_own[0][i].wait_recv()
            self.on[0][i].start()
        for i in range(2):
            self.on[1][i].wait_recv()
            self.y_far[i].start()
        for i in range(2):
            self.x_other[i].wait_recv()
            self.on_other[i].start()

    def wait(self):
        self.y_own[1].wait_recv()
        for copy in (*self.on[0], *self.on_other, *self.y_near, *self.y_far):
            copy.wait_recv()
        for copy in (*self.y_own, *self.x_own[0], *self.x_own[1], *self.x_other, *self.on[0], *self.on[1],
                     *self.on_other, *self.y_near, *self.y_far):
            copy.wait_send()


def gather_scratch():
    return [DMA((19,)), DMA((19,))]


def cols(ref, k, width):
    return ref.at[:, pl.ds(pl.multiple_of(k * width, width), width)]


def rows_of(ref, k, count):
    return ref.at[pl.ds(pl.multiple_of(k * count, count), count)]


def back_of(grad, values, gain):
    rate = mean_rate(values)
    hat = values * rate
    grad_hat = grad * gain
    dots = jnp.mean(grad_hat * hat, axis=-1, keepdims=True)
    return hat, rate * (grad_hat - hat * dots)


class GradSum:
    def __init__(self, kind, part, out, other, between, far, near, sent, arrived):
        dp, _, col = here()
        self.kind, self.part, self.dp, self.col = kind, part, dp, col
        self.other, self.between, self.far, self.near = other, between, far, near
        self.rows = near.shape[1]
        number = iter(range(18))

        def copy(source, target, **where):
            i = next(number)
            return remote(source, target, sent.at[i], arrived.at[i], **where)

        self.core = [copy(self.half(c, 1 - dp), other.at[c], dp=1 - dp) for c in range(8)]
        self.steps = (1, 3)
        self.on = [
            [
                copy(self.piece(self.z_block(2, k), i), between.at[i, k], col=z_peer(col, d))
                for k in range(2)
            ]
            for i, d in enumerate(self.steps)
        ]
        self.zs = [
            [copy(self.half(self.z_block(d, k), dp), far.at[i, k], col=z_peer(col, d)) for k in range(2)]
            for i, d in enumerate(self.steps)
        ]
        self.ys = copy(near.at[0], near.at[1], col=y_peer(col))
        self.last = copy(near.at[0], half_shard(out, dp), dp=1 - dp)
        self.keep = pltpu.make_async_copy(near.at[0], half_shard(out, dp), sent.at[18])

    def z_block(self, d, k):
        return z_peer(self.col, d) // 2 * 2 + k

    def half(self, c, h):
        return half_of(self.kind, self.part, c, h)

    def piece(self, c, i):
        return self.half(c, self.dp).at[pl.ds(i * (self.rows // 2), self.rows // 2)]

    def start(self):
        for copy in self.core:
            copy.start()

    def each(self, rows, body):
        @pl.loop(0, rows // 16)
        def _(i):
            body(span(i, 16))

    def over_core(self):
        for copy in self.core:
            copy.wait()

        @pl.loop(0, 8)
        def _(c):
            own = self.half(c, self.dp)

            def add(at):
                own[at] = (own[at].astype(F32) + self.other[c, at].astype(F32)).astype(BF16)

            self.each(self.rows, add)

        for pair in self.on:
            for copy in pair:
                copy.start()

    def over_z(self):
        for i, d in enumerate(self.steps):
            for k in range(2):
                self.on[i][k].wait_recv()
                own = self.piece(self.z_block(d, k), i)

                def add(at):
                    own[at] = (own[at].astype(F32) + self.between[i, k, at].astype(F32)).astype(BF16)

                self.each(self.rows // 2, add)
            for k in range(2):
                self.zs[i][k].start()

    def over_y(self):
        for pair in self.zs:
            for copy in pair:
                copy.wait_recv()
        yl = self.col % 2
        keep, give = self.half(self.col, self.dp), self.half(y_peer(self.col), self.dp)

        def total(at, ref, k):
            return (
                ref[at].astype(F32) + self.far[0, k, at].astype(F32) + self.far[1, k, at].astype(F32)
            ).astype(BF16)

        def add(at):
            self.near[0, at] = total(at, give, 1 - yl)

        self.each(self.rows, add)
        self.ys.start()

        def add(at):
            keep[at] = total(at, keep, yl)

        self.each(self.rows, add)
        for pair in (*self.zs, *self.on):
            for copy in pair:
                copy.wait_send()

    def end(self):
        self.ys.wait()
        keep = self.half(self.col, self.dp)

        def add(at):
            self.near[0, at] = (keep[at].astype(F32) + self.near[1, at].astype(F32)).astype(BF16)

        self.each(self.rows, add)
        self.last.start()
        self.keep.start()

    def wait(self):
        self.last.wait()
        self.keep.wait()


def grad_sum_scratch(shape):
    rows, width = shape[0] // 2, shape[1]
    return [
        pltpu.VMEM((8, rows, width), BF16),
        pltpu.VMEM((2, 2, rows // 2, width), BF16),
        pltpu.VMEM((2, 2, rows, width), BF16),
        pltpu.VMEM((2, rows, width), BF16),
        DMA((19,)),
        DMA((18,)),
    ]


class Bring:
    def __init__(self, kind, shard, whole, sent, arrived):
        dp, _, col = here()
        rows, width = shard.shape
        near = y_peer(col)
        number = iter(range(20))

        def block(c, s=None):
            count, at = (rows // 2, dp) if s is None else (rows // 4, 2 * dp + s)
            if kind == "tall":
                return whole.at[span((2 if s is None else 4) * c + at, count)]
            return whole.at[span(at, count), span(c, width)]

        def copy(source, target, **where):
            i = next(number)
            return remote(source, target, sent.at[i], arrived.at[i], **where)

        mine = half_shard(shard, dp)
        place = whole.at[span(col, rows)] if kind == "tall" else whole.at[:, span(col, width)]
        self.local = pltpu.make_async_copy(shard, place, sent.at[20])
        self.y_own = copy(mine, block(col), col=near)
        self.z_own = [copy(mine, block(col), col=z_peer(col, d)) for d in (1, 3)]
        self.z_near = [copy(block(near), block(near), col=z_peer(col, d)) for d in (1, 3)]
        self.on, self.on_near, self.a_own, self.a_near = [], [], [], []
        self.a_far, self.a_far_near = [], []
        for i, d in enumerate((1, 3)):
            came, two = z_source(col, d), z_peer(col, 2)
            self.on.append(copy(block(came, i), block(came, i), col=z_peer(col, d)))
            self.on_near.append(copy(block(y_peer(came), i), block(y_peer(came), i), col=z_peer(col, d)))
            self.a_own.append(copy(block(came), block(came), dp=1 - dp))
            self.a_near.append(copy(block(y_peer(came)), block(y_peer(came)), dp=1 - dp))
            self.a_far.append(copy(block(two, i), block(two, i), dp=1 - dp))
            self.a_far_near.append(copy(block(y_peer(two), i), block(y_peer(two), i), dp=1 - dp))
        self.a_y = copy(block(near), block(near), dp=1 - dp)

    def start(self):
        for copy in (self.y_own, *self.z_own, self.local):
            copy.start()

    def relay(self):
        self.y_own.wait_recv()
        for copy in (*self.z_near, self.a_y):
            copy.start()

    def relay_own(self):
        for i in range(2):
            self.z_own[i].wait_recv()
            self.on[i].start()
            self.a_own[i].start()

    def relay_near(self):
        for i in range(2):
            self.z_near[i].wait_recv()
            self.on_near[i].start()
            self.a_near[i].start()

    def hand_over(self):
        for i in range(2):
            self.on[i].wait_recv()
            self.a_far[i].start()
        for i in range(2):
            self.on_near[i].wait_recv()
            self.a_far_near[i].start()

    def wait(self):
        for copy in (self.a_y, *self.a_own, *self.a_near, *self.a_far, *self.a_far_near):
            copy.wait()
        for copy in (self.y_own, *self.z_own, *self.z_near, *self.on, *self.on_near):
            copy.wait_send()
        self.local.wait()


def bring_scratch():
    return [DMA((21,)), DMA((20,))]


class SpreadIn:
    def __init__(self, source, target, sent, arrived):
        dp, row, col = here()
        self.row, self.col = row, col
        self.copies, self.waits = [], []
        for k in range(8):
            out = remote(source(k), target(k, col), sent.at[k], arrived.at[col], row=k, col=row)
            came = remote(source(k), target(row, k), sent.at[k], arrived.at[k], row=k, col=row)
            local = pltpu.make_async_copy(source(k), target(k, col), sent.at[k])
            self.copies.append(((row == k) & (row == col), out, local))
            self.waits.append(((row == col) & (col == k), came))

    def start(self):
        for mine, out, local in self.copies:
            pl.when(jnp.logical_not(mine))(out.start)
            pl.when(mine)(local.start)

    def wait(self):
        for mine, came in self.waits:
            pl.when(jnp.logical_not(mine))(came.wait_recv)
        for mine, out, local in self.copies:
            pl.when(jnp.logical_not(mine))(out.wait_send)
            pl.when(mine)(local.wait)


class TokenSums:
    def __init__(self, stats, mine, came, sent, arrived):
        dp, row, col = here()
        self.stats, self.mine, self.came = stats, mine, came
        self.copies = [
            remote(mine, came.at[d - 1], sent.at[d - 1], arrived.at[d - 1], row=row_peer(row, d))
            for d in range(1, 8)
        ]

    def put(self, at, one, two):
        lane = lax.broadcasted_iota(jnp.int32, (one.shape[0], 128), 1)
        self.stats[at] = jnp.where(lane == 0, one, jnp.where(lane == 1, two, 0.0))

    def start(self):
        self.mine[...] = self.stats[...].T[:8]
        for copy in self.copies:
            copy.start()

    def end(self):
        total = self.mine[...]
        for d, copy in enumerate(self.copies):
            copy.wait_recv()
            total = total + self.came[d]
        self.stats[...] = jnp.concatenate([total] * 16, axis=0).T
        for copy in self.copies:
            copy.wait_send()


def sums_scratch(tokens):
    return [pltpu.VMEM((8, tokens), F32), pltpu.VMEM((7, 8, tokens), F32), DMA((7,)), DMA((7,))]


def turn(values, cosine, sine):
    heads = [values[:, i : i + HD] for i in range(0, values.shape[1], HD)]
    return jnp.concatenate([h * cosine + pltpu.roll(h, HD // 2, 1) * sine for h in heads], axis=1)


QUERY_BLOCK = 128


def key_span(b):
    start = max(0, b * QUERY_BLOCK - WINDOW)
    return start, (b + 1) * QUERY_BLOCK - start


def attend_kernel(
    x, g, heads_in, merge_in, expand_in, reduce_in, cosine, sine, docs, doc_row, gain_query, gain_key, gain_merge,
    xs_out, share_out, heads_out, merge_out, expand_out, reduce_out, raw_out, qkv_out, probs_out, mix_out, rates_out,
    merged, residual, rows_out,
    xs, heads32, merge32, expand32, reduce32, heads16, merge16, expand16, reduce16, heads, merge, raw, qkv, probs, mix,
    rates, part, rows, load, put, xsent, xcame, gsent, gcame, asent, acame, bsent, bcame, *refs,
):
    dp, row, col = here()
    share, width = merged.shape
    tokens = xs.shape[0]
    head_width = mix.shape[1]
    own = span(row, share)
    loads = [
        pltpu.make_async_copy(source, target, load.at[i])
        for i, (source, target) in enumerate(
            ((heads_in, heads32), (merge_in, merge32), (reduce_in, reduce32), (expand_in, expand32))
        )
    ]
    for copy in loads:
        copy.start()
    spread_x = SpreadIn(
        lambda k: rows_of(x, k, share), lambda k, c: xs.at[span(k, share), span(c, 256)], xsent, xcame
    )
    spread_g = SpreadIn(
        lambda k: rows_of(g, k, share), lambda k, c: share_out.at[:, span(c, 256)], gsent, gcame
    )
    gather_x = Gather(xs, share, asent, acame)
    gather = Gather(rows, share, bsent, bcame)
    scatter = Scatter(part, *refs[:8])
    sums = TokenSums(rates, *refs[8:12])
    bring_heads = Bring("tall", heads16, heads, *refs[12:14])
    bring_merge = Bring("wide", merge16, merge, *refs[14:16])
    bring_reduce = Bring("wide", reduce16, reduce_out, *refs[16:18])
    bring_expand = Bring("tall", expand16, expand_out, *refs[18:20])
    puts = [
        pltpu.make_async_copy(source, target, put.at[i])
        for i, (source, target) in enumerate(
            ((xs, xs_out), (heads, heads_out), (merge, merge_out), (raw, raw_out), (qkv, qkv_out),
             (probs, probs_out), (mix, mix_out), (rates, rates_out), (rows, rows_out))
        )
    ]

    def narrow(source, target):
        @pl.loop(0, source.shape[0] // 16)
        def _(i):
            at = span(i, 16)
            target[at] = source[at].astype(BF16)

    meet(rows=True, weights=True, core=True, spread_in=True)
    spread_x.start()
    loads[0].wait()
    narrow(heads32, heads16)
    bring_heads.start()
    loads[1].wait()
    narrow(merge32, merge16)
    bring_merge.start()
    loads[2].wait()
    narrow(reduce32, reduce16)
    loads[3].wait()
    narrow(expand32, expand16)
    spread_x.wait()
    gather_x.start()
    bring_heads.relay()
    bring_heads.relay_own()
    gather_x.relay()
    bring_heads.relay_near()
    bring_merge.relay()
    gather_x.relay_again()
    bring_heads.hand_over()
    bring_expand.start()
    bring_reduce.start()
    gather_x.wait()
    bring_heads.wait()
    puts[0].start()
    puts[1].start()

    for i in range(2):
        raw[:, i * head_width : (i + 1) * head_width] = dot(
            xs[...], heads[:, i * head_width : (i + 1) * head_width]
        )

    @pl.loop(0, tokens // 64)
    def _(i):
        at = span(i, 64)
        squares = raw[at] * raw[at]
        sums.put(
            at,
            jnp.sum(squares[:, :head_width], axis=1, keepdims=True),
            jnp.sum(squares[:, head_width:], axis=1, keepdims=True),
        )

    sums.start()
    qkv[:, 2 * head_width :] = dot(xs[...], heads[:, 2 * head_width :]).astype(BF16)
    bring_merge.relay_own()
    bring_merge.relay_near()
    sums.end()
    spread_g.start()

    @pl.loop(0, tokens // 64)
    def _(i):
        at = span(i, 64)
        rate = lax.rsqrt(rates[at] * (1.0 / width) + EPS)
        rates[at] = rate
        for j, gain in enumerate((gain_query, gain_key)):
            some = slice(j * head_width, (j + 1) * head_width)
            hat = raw[at, some] * rate[:, j : j + 1]
            qkv[at, some] = turn(hat * gain[...], cosine[at], sine[at]).astype(BF16)

    puts[3].start()
    puts[4].start()
    puts[7].start()
    for b in range(tokens // QUERY_BLOCK):
        start, count = key_span(b)
        query_at = pl.ds(b * QUERY_BLOCK, QUERY_BLOCK)
        key_at = pl.ds(start, count)
        there = lax.broadcasted_iota(jnp.int32, (QUERY_BLOCK, count), 0) + (b * QUERY_BLOCK - start)
        distance = there - lax.broadcasted_iota(jnp.int32, (QUERY_BLOCK, count), 1)
        doc = docs[query_at, 0:1]
        allowed = (doc == doc_row[0:1, start : start + count]) & (distance >= 0) & (distance < WINDOW)
        live = (doc < 5.0).astype(F32)
        for h in range(head_width // HD):
            query, key, value = (
                slice(i * head_width + h * HD, i * head_width + (h + 1) * HD) for i in range(3)
            )
            scores = dot_flipped(qkv[query_at, query], qkv[key_at, key]) * HD**-0.5
            scores = jnp.where(allowed, scores, -1e30)
            weights = jnp.exp(scores - jnp.max(scores, axis=1, keepdims=True))
            shares = (weights / jnp.sum(weights, axis=1, keepdims=True)).astype(BF16)
            probs[h, b, :, :count] = shares
            if count < probs.shape[3]:
                probs[h, b, :, count:] = jnp.zeros((QUERY_BLOCK, probs.shape[3] - count), BF16)
            mix[query_at, h * HD : (h + 1) * HD] = (dot(shares, qkv[key_at, value]) * live).astype(BF16)

    puts[5].start()
    puts[6].start()
    bring_expand.relay()
    bring_reduce.relay()
    bring_merge.hand_over()
    bring_merge.wait()
    puts[2].start()

    def merge_part(j):
        at = span(j, 256)
        part[:, at] = dot(mix[...], merge[:, at]).astype(BF16)

    n = width // 512
    pl.loop(n, 2 * n)(merge_part)
    scatter.start_right()
    pl.loop(0, n)(merge_part)
    scatter.start_left()
    bring_expand.relay_own()
    bring_reduce.relay_own()
    scatter.middle()
    bring_expand.relay_near()
    bring_reduce.relay_near()
    scatter.end()

    @pl.loop(0, share // 16)
    def _(i):
        at = span(i, 16)
        total = scatter.total[at]
        merged[at] = total
        mine = pl.ds(pl.multiple_of(row * share + i * 16, 16), 16)
        result = xs[mine, :].astype(F32) + total * mean_rate(total) * gain_merge[...]
        residual[at] = result
        rows[mine, :] = result.astype(BF16)

    gather.start()
    gather.relay()
    bring_expand.hand_over()
    gather.relay_again()
    bring_reduce.hand_over()
    gather.wait()
    puts[8].start()
    scatter.finish()
    spread_g.wait()
    bring_expand.wait()
    bring_reduce.wait()
    for copy in puts:
        copy.wait()


def rest_kernel(
    rows_in, expand_in, reduce_in, heads_in, merge_in, xs_in, raw_in, qkv_in, probs_in, mix_in, rates_in,
    residual, g, merged, cosine, sine, docs, gain_query, gain_key, gain_merge, gain_reduce,
    out, input_grad, gains_grad, heads_grad, merge_grad, expand_grad, reduce_grad,
    rows, turned, expand, reduce, heads, merge, gate, up, act, act_turned, part, back, hidden, probs, mix, mix_turned,
    rates, stats, grad_mix, done, final, grad_resid, sums, grad_gate,
    gains, gain_row, gain_col, gain_core, gain_sum, load, late, osent, ocame, isent, icame, nsent, ncame,
    g1sent, g1came, g2sent, g2came, *refs,
):
    dp, row, col = here()
    share, width = residual.shape
    tokens, units = act.shape
    head_width = mix.shape[1]
    tiles = units // 256
    n = width // 512
    scatter = [Scatter(part, *refs[:6], *refs[6 + 2 * i : 8 + 2 * i]) for i in range(3)]
    token_sums = TokenSums(stats, *refs[12:16])
    reduce_sum = GradSum("wide", reduce, reduce_grad, *refs[16:22])
    expand_sum = GradSum("tall", expand, expand_grad, *refs[22:28])
    merge_sum = GradSum("wide", merge, merge_grad, *refs[28:34])
    heads_sum = GradSum("tall", heads, heads_grad, *refs[34:40])
    gather = Gather(back, share, g1sent, g1came)
    last_gather = Gather(back, share, g2sent, g2came)
    spread = Spread(False, lambda k: cols(done, k, 256), lambda k: rows_of(out, k, 64), osent, ocame)
    spread_grad = Spread(False, lambda k: cols(final, k, 256), lambda k: rows_of(input_grad, k, 64), isent, icame)
    row_gains = [
        remote(gains, gain_row.at[row], nsent.at[d - 1], ncame.at[d - 1], row=row_peer(row, d))
        for d in range(1, 8)
    ]
    col_gains = [
        remote(gain_sum.at[0], gain_col.at[col], nsent.at[6 + d], ncame.at[6 + d], col=(col + d) % 8)
        for d in range(1, 8)
    ]
    core_gains = remote(gain_sum.at[1], gain_core, nsent.at[14], ncame.at[14], dp=1 - dp)

    raw, qkv, new_rows = up.at[:, : 2 * head_width], act.at[:, : 3 * head_width], back
    heads_change = gate.at[:, : 3 * head_width]
    joined = hidden.at[:, : 3 * head_width]
    get_rows = pltpu.make_async_copy(rows_in, rows, load.at[0])
    get_reduce = pltpu.make_async_copy(reduce_in, reduce, load.at[1])

    def get_expand(j):
        at = span(j, 256)
        return pltpu.make_async_copy(expand_in.at[:, at], expand.at[:, at], load.at[2 + j])

    early = [
        pltpu.make_async_copy(source, target, late.at[i])
        for i, (source, target) in enumerate(
            ((heads_in, heads), (merge_in, merge), (probs_in, probs), (mix_in, mix), (rates_in, rates))
        )
    ]
    get_raw = pltpu.make_async_copy(raw_in, raw, late.at[5])
    get_qkv = pltpu.make_async_copy(qkv_in, qkv, late.at[6])
    get_xs = pltpu.make_async_copy(xs_in, rows, late.at[7])

    get_rows.start()
    for j in range(tiles):
        get_expand(j).start()
        get_expand(tiles + j).start()
    get_reduce.start()
    meet(rows=True, cols=True, core=True, spread_out=True)
    get_rows.wait()

    @pl.loop(0, tiles)
    def _(j):
        get_expand(j).wait()
        get_expand(tiles + j).wait()
        at = span(j, 256)
        gate[:, at] = dot(rows[...], expand[:, at])
        up[:, at] = dot(rows[...], expand[:, span(tiles + j, 256)])

        @pl.loop(0, tokens // 64)
        def _(i):
            some = span(i, 64)
            x = gate[some, at]
            act[some, at] = (x * jax.nn.sigmoid(x) * up[some, at]).astype(BF16)

    get_reduce.wait()

    def reduced(j):
        at = span(j, 256)
        part[:, at] = dot(act[...], reduce[:, at]).astype(BF16)

    pl.loop(n, 2 * n)(reduced)
    scatter[0].start_right()
    pl.loop(0, n)(reduced)
    scatter[0].start_left()

    @pl.loop(0, tiles)
    def _(j):
        at = span(j, 256)
        act_turned[at, :] = act[:, at].T

    for copy in early:
        copy.start()
    get_qkv.start()

    scatter[0].middle()
    scatter[0].end()
    sums[...] = jnp.zeros_like(sums)

    @pl.loop(0, share // 16)
    def _(i):
        at = span(i, 16)
        grad = g[at].astype(F32)
        hat, change = back_of(grad, scatter[0].total[at], gain_reduce[...])
        back[pl.ds(pl.multiple_of(row * share + i * 16, 16), 16), :] = change.astype(BF16)
        done[at] = (residual[at] + hat * gain_reduce[...]).astype(BF16)
        product = grad * hat
        sums[...] += product[:8] + product[8:]

    gather.start()
    gains[...] = jnp.zeros_like(gains)
    gains[3:4] = jnp.sum(sums[...], axis=0, keepdims=True)
    scatter[0].finish()
    gather.relay()

    @pl.loop(0, 2 * tiles)
    def _(j):
        at = span(j, 256)
        turned[at, :] = rows[:, at].T

    get_xs.start()
    gather.relay_again()
    gather.wait()
    spread.start()

    @pl.loop(0, tiles)
    def _(j):
        at, up_at = span(j, 256), span(tiles + j, 256)
        grad_gate[...] = dot_flipped(back[...], reduce[at, :])

        @pl.loop(0, tokens // 64)
        def _(i):
            some = span(i, 64)
            x, change = gate[some, at], grad_gate[some]
            s = jax.nn.sigmoid(x)
            hidden[some, at] = (change * up[some, at] * s * (1.0 + x * (1.0 - s))).astype(BF16)
            hidden[some, up_at] = (change * (x * s)).astype(BF16)

    get_raw.start()

    def branch(j):
        at = span(j, 256)
        part[:, at] = dot_flipped(hidden[...], expand[at, :]).astype(BF16)

    pl.loop(n, 2 * n)(branch)
    scatter[1].start_right()
    pl.loop(0, n)(branch)
    scatter[1].start_left()

    @pl.loop(0, tiles)
    def _(j):
        at = span(j, 256)
        for side in range(2):
            wide = pl.ds(side * (width // 2), width // 2)
            reduce[at, wide] = dot(act_turned[at, :], back[:, wide]).astype(BF16)

    reduce_sum.start()
    scatter[1].middle()

    def expand_part(j):
        at = span(j, 256)
        for side in range(2):
            wide = pl.ds(side * (width // 2), width // 2)
            expand[at, wide] = dot(turned[at, :], hidden[:, wide]).astype(BF16)

    pl.loop(0, tiles)(expand_part)
    scatter[1].end()
    sums[...] = jnp.zeros_like(sums)

    @pl.loop(0, share // 16)
    def _(i):
        at = span(i, 16)
        grad = g[at].astype(F32) + scatter[1].total[at]
        grad_resid[at] = grad
        hat, change = back_of(grad, merged[at], gain_merge[...])
        new_rows[pl.ds(pl.multiple_of(row * share + i * 16, 16), 16), :] = change.astype(BF16)
        product = grad * hat
        sums[...] += product[:8] + product[8:]

    last_gather.start()
    gains[2:3] = jnp.sum(sums[...], axis=0, keepdims=True)
    pl.loop(tiles, 2 * tiles)(expand_part)
    expand_sum.start()
    last_gather.relay()
    reduce_sum.over_core()
    last_gather.relay_again()
    get_xs.wait()

    @pl.loop(0, 2 * tiles)
    def _(j):
        at = span(j, 256)
        turned[at, :] = rows[:, at].T

    for copy in early:
        copy.wait()
    get_raw.wait()
    get_qkv.wait()
    mix_turned[...] = mix[...].T
    expand_sum.over_core()
    reduce_sum.over_z()
    scatter[1].finish()
    last_gather.wait()

    live = (docs[:, 0:1] < 5.0).astype(F32)
    grad_mix[...] = (dot_flipped(new_rows[...], merge[...]) * live).astype(BF16)
    heads_change[:, head_width:] = jnp.zeros((tokens, 2 * head_width), F32)
    for b in range(tokens // QUERY_BLOCK):
        start, count = key_span(b)
        query_at = pl.ds(b * QUERY_BLOCK, QUERY_BLOCK)
        key_at = pl.ds(start, count)
        for h in range(head_width // HD):
            query, key, value = (
                slice(i * head_width + h * HD, i * head_width + (h + 1) * HD) for i in range(3)
            )
            shares = probs[h, b, :, :count]
            change = grad_mix[query_at, h * HD : (h + 1) * HD]
            grad_shares = dot_flipped(change, qkv[key_at, value])
            weighted = shares.astype(F32) * grad_shares
            center = jnp.sum(weighted, axis=1, keepdims=True)
            grad_scores = (weighted - shares.astype(F32) * center).astype(BF16)
            heads_change[query_at, query] = dot(grad_scores, qkv[key_at, key]) * HD**-0.5
            heads_change[key_at, key] += dot(grad_scores.T, qkv[query_at, query]) * HD**-0.5
            heads_change[key_at, value] += dot(shares.T, change)

    sums[...] = jnp.zeros_like(sums)

    @pl.loop(0, tokens // 64)
    def _(i):
        at = span(i, 64)
        dots = []
        for j, gain in enumerate((gain_query, gain_key)):
            some = slice(j * head_width, (j + 1) * head_width)
            change = turn(heads_change[at, some], cosine[at], -sine[at])
            hat = raw[at, some] * rates[at, j : j + 1]
            product = change * hat
            sums[:, some] += jnp.sum(product.reshape(8, 8, head_width), axis=0)
            heads_change[at, some] = change * gain[...]
            dots.append(jnp.sum(product * gain[...], axis=1, keepdims=True))
        token_sums.put(at, *dots)

    token_sums.start()
    gains[0:1, span(row, head_width)] = jnp.sum(sums[:, :head_width], axis=0, keepdims=True)
    gains[1:2, span(row, head_width)] = jnp.sum(sums[:, head_width : 2 * head_width], axis=0, keepdims=True)
    for copy in row_gains:
        copy.start()
    for side in range(4):
        wide = pl.ds(side * (width // 4), width // 4)
        merge[:, wide] = dot(mix_turned[...], new_rows[:, wide]).astype(BF16)
    merge_sum.start()
    joined[:, 2 * head_width :] = heads_change[:, 2 * head_width :].astype(BF16)
    token_sums.end()

    @pl.loop(0, tokens // 64)
    def _(i):
        at = span(i, 64)
        dots = stats[at] * (1.0 / width)
        for j in range(2):
            some = slice(j * head_width, (j + 1) * head_width)
            rate = rates[at, j : j + 1]
            hat = raw[at, some] * rate
            joined[at, some] = (rate * (heads_change[at, some] - hat * dots[:, j : j + 1])).astype(BF16)

    def input_part(j):
        at = span(j, 256)
        part[:, at] = dot_flipped(joined[...], heads[at, :]).astype(BF16)

    pl.loop(n, 2 * n)(input_part)
    scatter[2].start_right()
    pl.loop(0, n)(input_part)
    scatter[2].start_left()

    @pl.loop(0, 2 * tiles)
    def _(j):
        at = span(j, 256)
        heads[at, :] = dot(turned[at, :], joined[...]).astype(BF16)

    heads_sum.start()
    merge_sum.over_core()
    scatter[2].middle()
    expand_sum.over_z()
    heads_sum.over_core()
    scatter[2].end()
    final[...] = grad_resid[...] + scatter[2].total[...]
    spread_grad.start()
    for copy in row_gains:
        copy.wait()
    gain_row[row] = gains[...]
    total = gain_row[0]
    for k in range(1, 8):
        total = total + gain_row[k]
    gain_sum[0] = total
    gain_col[col] = total
    for copy in col_gains:
        copy.start()
    merge_sum.over_z()
    heads_sum.over_z()
    for copy in col_gains:
        copy.wait()
    total = gain_col[0]
    for k in range(1, 8):
        total = total + gain_col[k]
    gain_sum[1] = total
    core_gains.start()
    reduce_sum.over_y()
    expand_sum.over_y()
    reduce_sum.end()
    merge_sum.over_y()
    heads_sum.over_y()
    expand_sum.end()
    merge_sum.end()
    heads_sum.end()
    core_gains.wait()
    gains_grad[...] = gain_sum[1] + gain_core[...]
    scatter[2].finish()
    spread.wait()
    spread_grad.wait()
    for grad in (reduce_sum, expand_sum, merge_sum, heads_sum):
        grad.wait()


def on_device(
    block_input,
    cotangent,
    doc_lengths,
    heads_weight,
    heads_first,
    heads_second,
    merge_weight,
    merge_first,
    merge_second,
    expand_weight,
    expand_first,
    expand_second,
    reduce_weight,
    reduce_first,
    reduce_second,
    norm_gains,
    gains_first,
    gains_second,
):
    row_at = lax.axis_index("row")
    col_width = block_input.shape[1]
    model_width = col_width * lax.axis_size("col")
    head_width = merge_weight.shape[0]
    unit_width = reduce_weight.shape[0]
    seq_len = block_input.shape[0] * lax.axis_size("row") // lax.axis_size("col")
    share = seq_len // lax.axis_size("row")
    head_count = head_width // HD
    doc_ids, places, live_rows = positions(doc_lengths[0], seq_len)
    gain_query = lax.dynamic_slice_in_dim(norm_gains[0], row_at * head_width, head_width)
    gain_key = lax.dynamic_slice_in_dim(norm_gains[1], row_at * head_width, head_width)
    gain_merge, gain_reduce = norm_gains[2:3], norm_gains[3:4]
    rows_shape = struct((seq_len, model_width), BF16)
    mine_f32 = struct((share, model_width), F32)
    half_dim = HD // 2
    frequency = THETA ** (-2.0 * jnp.arange(half_dim, dtype=F32) / HD)
    angles = places.astype(F32)[:, None] * frequency[None, :]
    cosine, sine = jnp.cos(angles), jnp.sin(angles)
    cosine = jnp.concatenate([cosine, cosine], axis=1)
    sine = jnp.concatenate([-sine, sine], axis=1)
    docs = jnp.broadcast_to(doc_ids.astype(F32)[:, None], (seq_len, 128))
    doc_row = jnp.broadcast_to(doc_ids.astype(F32)[None, :], (8, seq_len))
    blocks = seq_len // QUERY_BLOCK

    (
        input_rows, cot_share, heads_low, merge_low, expand_low, reduce_low, raw, qkv, probs, mixture_low, rates,
        merged, residual, residual_rows,
    ) = call(
        attend_kernel, "attend", 1,
        [
            rows_shape,
            struct((share, model_width), BF16),
            struct((model_width, 3 * head_width), BF16),
            struct((head_width, model_width), BF16),
            struct((model_width, 2 * unit_width), BF16),
            struct((unit_width, model_width), BF16),
            struct((seq_len, 2 * head_width), F32),
            struct((seq_len, 3 * head_width), BF16),
            struct((head_count, blocks, QUERY_BLOCK, WINDOW + QUERY_BLOCK), BF16),
            struct((seq_len, head_width), BF16),
            struct((seq_len, 128), F32),
            mine_f32,
            mine_f32,
            rows_shape,
        ],
        [
            block_input, cotangent, heads_weight, merge_weight, expand_weight, reduce_weight, cosine, sine, docs,
            doc_row, gain_query[None], gain_key[None], gain_merge,
        ],
        [ANY] * 6 + [VMEM] * 7,
        [ANY] * 11 + [VMEM] * 2 + [ANY],
        [
            pltpu.VMEM((seq_len, model_width), BF16),
            pltpu.VMEM(heads_weight.shape, F32),
            pltpu.VMEM(merge_weight.shape, F32),
            pltpu.VMEM(expand_weight.shape, F32),
            pltpu.VMEM(reduce_weight.shape, F32),
            pltpu.VMEM(heads_weight.shape, BF16),
            pltpu.VMEM(merge_weight.shape, BF16),
            pltpu.VMEM(expand_weight.shape, BF16),
            pltpu.VMEM(reduce_weight.shape, BF16),
            pltpu.VMEM((model_width, 3 * head_width), BF16),
            pltpu.VMEM((head_width, model_width), BF16),
            pltpu.VMEM((seq_len, 2 * head_width), F32),
            pltpu.VMEM((seq_len, 3 * head_width), BF16),
            pltpu.VMEM((head_count, blocks, QUERY_BLOCK, WINDOW + QUERY_BLOCK), BF16),
            pltpu.VMEM((seq_len, head_width), BF16),
            pltpu.VMEM((seq_len, 128), F32),
            pltpu.VMEM((seq_len, model_width), BF16),
            pltpu.VMEM((seq_len, model_width), BF16),
            DMA((4,)), DMA((9,)), DMA((8,)), DMA((8,)), DMA((8,)), DMA((8,)),
        ]
        + gather_scratch() + gather_scratch()
        + scatter_scratch(share, model_width) + sums_scratch(seq_len)
        + bring_scratch() + bring_scratch() + bring_scratch() + bring_scratch(),
    )
    gain_shape = (4, model_width)
    block_output, input_grad, gains_grad, heads_grad, merge_grad, expand_grad, reduce_grad = call(
        rest_kernel, "rest", 2,
        [
            struct(block_input.shape, BF16),
            struct(block_input.shape, F32),
            struct(gain_shape, F32),
            struct(heads_weight.shape, BF16),
            struct(merge_weight.shape, BF16),
            struct(expand_weight.shape, BF16),
            struct(reduce_weight.shape, BF16),
        ],
        [
            residual_rows, expand_low, reduce_low, heads_low, merge_low, input_rows, raw, qkv, probs, mixture_low, rates,
            residual, cot_share, merged, cosine, sine, docs, gain_query[None], gain_key[None], gain_merge, gain_reduce,
        ],
        [ANY] * 11 + [VMEM] * 10,
        [ANY] * 2 + [VMEM] + [ANY] * 4,
        [
            pltpu.VMEM((seq_len, model_width), BF16),
            pltpu.VMEM((model_width, seq_len), BF16),
            pltpu.VMEM((model_width, 2 * unit_width), BF16),
            pltpu.VMEM((unit_width, model_width), BF16),
            pltpu.VMEM((model_width, 3 * head_width), BF16),
            pltpu.VMEM((head_width, model_width), BF16),
            pltpu.VMEM((seq_len, unit_width), F32),
            pltpu.VMEM((seq_len, unit_width), F32),
            pltpu.VMEM((seq_len, unit_width), BF16),
            pltpu.VMEM((unit_width, seq_len), BF16),
            pltpu.VMEM((seq_len, model_width), BF16),
            pltpu.VMEM((seq_len, model_width), BF16),
            pltpu.VMEM((seq_len, 2 * unit_width), BF16),
            pltpu.VMEM((head_count, blocks, QUERY_BLOCK, WINDOW + QUERY_BLOCK), BF16),
            pltpu.VMEM((seq_len, head_width), BF16),
            pltpu.VMEM((head_width, seq_len), BF16),
            pltpu.VMEM((seq_len, 128), F32),
            pltpu.VMEM((seq_len, 128), F32),
            pltpu.VMEM((seq_len, head_width), BF16),
            pltpu.VMEM((share, model_width), BF16),
            pltpu.VMEM((share, model_width), F32),
            pltpu.VMEM((share, model_width), F32),
            pltpu.VMEM((8, model_width), F32),
            pltpu.VMEM((seq_len, 256), F32),
            pltpu.VMEM(gain_shape, F32),
            pltpu.VMEM((8, *gain_shape), F32),
            pltpu.VMEM((8, *gain_shape), F32),
            pltpu.VMEM(gain_shape, F32),
            pltpu.VMEM((2, *gain_shape), F32),
            DMA((10,)), DMA((8,)), DMA((8,)), DMA((8,)), DMA((8,)), DMA((8,)), DMA((15,)), DMA((15,)),
        ]
        + gather_scratch() + gather_scratch()
        + scatter_scratch(share, model_width) + [DMA((14,))] * 4
        + sums_scratch(seq_len)
        + grad_sum_scratch(reduce_weight.shape) + grad_sum_scratch(expand_weight.shape)
        + grad_sum_scratch(merge_weight.shape) + grad_sum_scratch(heads_weight.shape),
    )
    heads_grad, merge_grad, expand_grad, reduce_grad = (
        heads_grad.astype(F32), merge_grad.astype(F32), expand_grad.astype(F32), reduce_grad.astype(F32)
    )
    heads_mean, heads_square, heads_fresh = adamw(
        heads_weight, heads_grad, heads_first, heads_second, LR, DECAY
    )
    merge_mean, merge_square, merge_fresh = adamw(
        merge_weight, merge_grad, merge_first, merge_second, LR, DECAY
    )
    expand_mean, expand_square, expand_fresh = adamw(
        expand_weight, expand_grad, expand_first, expand_second, LR, DECAY
    )
    reduce_mean, reduce_square, reduce_fresh = adamw(
        reduce_weight, reduce_grad, reduce_first, reduce_second, LR, DECAY
    )
    gains_mean, gains_square, gains_fresh = adamw(
        norm_gains, gains_grad, gains_first, gains_second, LR_GAIN, 0.0
    )
    return (
        block_output,
        input_grad,
        heads_grad,
        heads_mean,
        heads_square,
        heads_fresh,
        heads_fresh.astype(jnp.bfloat16),
        merge_grad,
        merge_mean,
        merge_square,
        merge_fresh,
        merge_fresh.astype(jnp.bfloat16),
        expand_grad,
        expand_mean,
        expand_square,
        expand_fresh,
        expand_fresh.astype(jnp.bfloat16),
        reduce_grad,
        reduce_mean,
        reduce_square,
        reduce_fresh,
        reduce_fresh.astype(jnp.bfloat16),
        gains_grad,
        gains_mean,
        gains_square,
        gains_fresh,
    )


def solution(mesh):
    return jax.shard_map(
        on_device,
        mesh=mesh,
        in_specs=(
            P(("dp", "row"), "col"),
            P(("dp", "row"), "col"),
            P(("dp", "col"), None),
            P("col", "row"),
            P("col", "row"),
            P("col", "row"),
            P("row", "col"),
            P("row", "col"),
            P("row", "col"),
            P("col", "row"),
            P("col", "row"),
            P("col", "row"),
            P("row", "col"),
            P("row", "col"),
            P("row", "col"),
            P(),
            P(),
            P(),
        ),
        out_specs=(
            P(("dp", "row"), "col"),
            P(("dp", "row"), "col"),
            P("col", "row"),
            P("col", "row"),
            P("col", "row"),
            P("col", "row"),
            P("col", "row"),
            P("row", "col"),
            P("row", "col"),
            P("row", "col"),
            P("row", "col"),
            P("row", "col"),
            P("col", "row"),
            P("col", "row"),
            P("col", "row"),
            P("col", "row"),
            P("col", "row"),
            P("row", "col"),
            P("row", "col"),
            P("row", "col"),
            P("row", "col"),
            P("row", "col"),
            P(),
            P(),
            P(),
            P(),
        ),
        check_vma=False,
    )
```

time: 434 us -> 333 us (0.77); the launches traced: 433 us -> 327 us
  Pallas kernels: 386 us -> 300 us
  matrix products: 14.5 us -> 0 us
    pallas_call x4 -> x2, Pallas kernels: 386 us -> 300 us  [call(): pl.pallas_call(kernel, name=name, out_shape=outs, in_specs=in_specs, out_...]
    dot_general x8 -> x0, matrix products: 14.5 us -> none  [the longest x2 7.68 us: product(): lax.dot_general(left_side, right_side, (((1,), (1,)), ((), ())), preferre...]
where the time goes in v4:
time: 333 us; the launch traced here: 327 us
  Pallas kernels  300 us (90%)
  other arithmetic  16.4 us (5%)
  local copies, waits for them, and re-layouts  9.05 us (3%)
    pallas_call x2, Pallas kernels, call(): pl.pallas_call(kernel, name=name, out_shape=outs, in_specs=in_specs, out_...  300 us

profile of v4, /device:TPU:9, one launch (start us, length us, event | category | flops | bytes accessed | tf_op | source)
XLA Modules:
  0.0 326.6 jit_solution(9879182448070112356)
XLA Ops:
  0.7 0.8 reduce-window.8
  1.5 0.7 convert_reduce_fusion
  2.3 0.6 broadcast_in_dim.22.doc_row
  2.9 1.5 fusion.15
  4.4 0.6 constant_dynamic-slice_fusion
  5.0 0.8 broadcast_in_dim.21.docs
  5.8 1.0 fusion.4
  6.8 1.0 pad_maximum_fusion
  7.8 101.1 %attend.1 = (bf16[512,2048]{1,0:T(8,128)(2,1)}, bf16[64,2048]{1,0:T(8,128)(2,1)}, bf16[2048,768]{1,0:T(8,128)(2,1)}, bf16[256,2048]{1,0:T(8,128)(2,1)}, bf16[204...) custom-call(bf16[512,256]{1,0:T(8,128)(2,1)} %x.1, ...), custom_call_target="tpu_custom_call" | custom-call | tf_op jit(solution)/shard_map/attend/pallas_call | solution.py:175
  109.0 199.1 %rest.1 = (bf16[512,256]{1,0:T(8,128)(2,1)}, f32[512,256]{1,0:T(8,128)}, f32[4,2048]{1,0:T(4,128)}, bf16[256,768]{1,0:T(8,128)(2,1)}, bf16[256,256]{1,0:T(8,128)...) custom-call(bf16[512,2048]{1,0:T(8,128)(2,1)} %get-tuple-element.47.rows_in, ...), custom_call_target="tpu_custom_call" | custom-call | tf_op jit(solution)/shard_map/rest/pallas_call | solution.py:175
  308.2 1.6 multiply_subtract_fusion.4
  309.8 2.0 fusion.11
  311.8 2.0 fusion.13
  313.9 0.4 copy-done.7
  314.2 0.7 copy-done.8
  314.9 0.1 copy-done.11
  315.1 2.7 fusion.7
  317.7 1.2 copy-done.3
  319.0 0.6 copy-done.4
  319.6 0.2 copy-done.5
  319.8 4.6 %fusion.9 = (bf16[256,2048]{1,0:T(8,128)(2,1)}, f32[256,2048]{1,0:T(8,128)}, f32[256,2048]{1,0:T(8,128)}, f32[256,2048]{1,0:T(8,128)}, f32[256,2048]{1,0:T(8,128)}) fusion(f32[256,2048]{1,0:T(8,128)S(1)} %copy-done, f32[256,2048]{1,0:T(8,128)S(1)} %copy-done.3, f32[256,2048]{1,0:T(8,128)S(1)} %copy-done.4, bf16[256,2048]{1,0:T(8,128)(2,1)S(1)} %copy-done.5), kind=kLoop, calls=%fused_computation.33 | loop fusion | flops 8388608 | bytes 16777216 | tf_op jit(solution)/shard_map/convert_element_type | solution.py:1359
  324.5 0.7 copy.47
  325.2 0.8 copy.48
  326.0 0.6 copy.49
  (39 shorter events, 0.1 us)
Async XLA Ops:
  108.9 199.3 %copy-start.17 = (f32[4,2048]{1,0:T(4,128)S(1)}, f32[4,2048]{1,0:T(4,128)}, u32[]{:S(2)}) copy-start(f32[4,2048]{1,0:T(4,128)} %param.33) | copy-start | bytes 98308
  108.9 199.3 %copy-start.19 = (f32[4,2048]{1,0:T(4,128)S(1)}, f32[4,2048]{1,0:T(4,128)}, u32[]{:S(2)}) copy-start(f32[4,2048]{1,0:T(4,128)} %param.35) | copy-start | bytes 98308
  109.0 199.3 %copy-start.20 = (f32[4,2048]{1,0:T(4,128)S(1)}, f32[4,2048]{1,0:T(4,128)}, u32[]{:S(2)}) copy-start(f32[4,2048]{1,0:T(4,128)} %param.34) | copy-start | bytes 98308
  109.0 200.8 %copy-start.6 = (f32[256,256]{1,0:T(8,128)S(1)}, f32[256,256]{1,0:T(8,128)}, u32[]{:S(2)}) copy-start(f32[256,256]{1,0:T(8,128)} %merge_in.1) | copy-start | bytes 786436
  109.0 200.8 %copy-start.15 = (f32[256,256]{1,0:T(8,128)S(1)}, f32[256,256]{1,0:T(8,128)}, u32[]{:S(2)}) copy-start(f32[256,256]{1,0:T(8,128)} %param.26) | copy-start | bytes 786436
  109.0 200.8 %copy-start.16 = (f32[256,256]{1,0:T(8,128)S(1)}, f32[256,256]{1,0:T(8,128)}, u32[]{:S(2)}) copy-start(f32[256,256]{1,0:T(8,128)} %param.25) | copy-start | bytes 786436
  109.0 202.8 %copy-start.10 = (f32[256,768]{1,0:T(8,128)S(1)}, f32[256,768]{1,0:T(8,128)}, u32[]{:S(2)}) copy-start(f32[256,768]{1,0:T(8,128)} %param.22) | copy-start | bytes 2359300
  308.2 3.6 %copy-start.2 = (f32[256,768]{1,0:T(8,128)S(1)}, f32[256,768]{1,0:T(8,128)}, u32[]{:S(2)}) copy-start(f32[256,768]{1,0:T(8,128)} %heads_in.1) | copy-start | bytes 2359300
  308.2 3.6 %copy-start.9 = (f32[256,768]{1,0:T(8,128)S(1)}, f32[256,768]{1,0:T(8,128)}, u32[]{:S(2)}) copy-start(f32[256,768]{1,0:T(8,128)} %param.23) | copy-start | bytes 2359300
  308.2 3.6 %copy-start.13 = (bf16[256,768]{1,0:T(8,128)(2,1)S(1)}, bf16[256,768]{1,0:T(8,128)(2,1)}, u32[]{:S(2)}) copy-start(bf16[256,768]{1,0:T(8,128)(2,1)} %get-tuple-element.63) | copy-start | bytes 1179652
  311.8 2.1 copy-start.1
  311.8 2.4 copy-start.7
  311.8 3.1 copy-start.8
  311.8 3.2 copy-start.11
  315.1 2.7 copy-start
  315.1 3.9 %copy-start.3 = (f32[256,2048]{1,0:T(8,128)S(1)}, f32[256,2048]{1,0:T(8,128)}, u32[]{:S(2)}) copy-start(f32[256,2048]{1,0:T(8,128)} %param.29) | copy-start | bytes 6291460
  315.1 4.5 %copy-start.4 = (f32[256,2048]{1,0:T(8,128)S(1)}, f32[256,2048]{1,0:T(8,128)}, u32[]{:S(2)}) copy-start(f32[256,2048]{1,0:T(8,128)} %param.28) | copy-start | bytes 6291460
  315.1 4.8 %copy-start.5 = (bf16[256,2048]{1,0:T(8,128)(2,1)S(1)}, bf16[256,2048]{1,0:T(8,128)(2,1)}, u32[]{:S(2)}) copy-start(bf16[256,2048]{1,0:T(8,128)(2,1)} %get-tuple-element.65) | copy-start | bytes 3145732
  319.8 4.6 %copy-start.14 = (bf16[512,256]{1,0:T(8,128)(2,1)S(1)}, bf16[512,256]{1,0:T(8,128)(2,1)}, u32[]{:S(2)}) copy-start(bf16[512,256]{1,0:T(8,128)(2,1)} %get-tuple-element.130) | copy-start | bytes 786436
  319.8 5.3 %copy-start.12 = (f32[512,256]{1,0:T(8,128)S(1)}, f32[512,256]{1,0:T(8,128)}, u32[]{:S(2)}) copy-start(f32[512,256]{1,0:T(8,128)} %get-tuple-element.131) | copy-start | bytes 1572868
  319.8 6.1 %copy-start.18 = (f32[4,2048]{1,0:T(4,128)S(1)}, f32[4,2048]{1,0:T(4,128)}, u32[]{:S(2)}) copy-start(f32[4,2048]{1,0:T(4,128)} %get-tuple-element.152) | copy-start | bytes 98308

commit v5 on v4

--- a/solution.py
+++ b/solution.py
@@ -309,62 +309,63 @@
 
 
 class Gather:
-    def __init__(self, whole, share, sent, arrived):
+    def __init__(self, whole, share, left, sent, arrived):
         dp, row, col = here()
         self.row = row
-        half = whole.shape[1] // 2
         number = iter(range(19))
+        sides = (pl.ds(0, left), pl.ds(left, whole.shape[1] - left))
+        right = left < whole.shape[1]
 
         def copy(fx, fy, side, dx, dy, start=0, count=share):
             i = next(number)
             k = near_row(row, fx, fy)
-            ref = whole.at[
-                pl.ds(pl.multiple_of(k * share + start, count), count), pl.ds(side * half, half)
-            ]
+            ref = whole.at[pl.ds(pl.multiple_of(k * share + start, count), count), sides[side]]
             return remote(ref, ref, sent.at[i], arrived.at[i], row=near_row(row, dx, dy))
 
         part = share // 2
-        self.y_own = [copy(0, 0, 0, 0, 1), copy(0, 0, 1, 0, 1)]
-        self.x_own = [[copy(0, 0, side, dx, 0) for dx in (1, 3)] for side in range(2)]
+        self.y_left = copy(0, 0, 0, 0, 1)
+        self.x_left = [copy(0, 0, 0, dx, 0) for dx in (1, 3)]
         self.x_other = [copy(0, 1, 0, dx, 0) for dx in (1, 3)]
-        self.on = [
-            [copy(4 - dx, 0, side, dx, 0, i * part, part) for i, dx in enumerate((1, 3))]
-            for side in range(2)
-        ]
-        self.on_other = [copy(4 - dx, 1, 0, dx, 0, i * part, part) for i, dx in enumerate((1, 3))]
-        self.y_near = [copy(4 - dx, 0, 1, 0, 1) for dx in (1, 3)]
-        self.y_far = [copy(2, 0, 1, 0, 1, i * part, part) for i in range(2)]
+        steps = list(enumerate((1, 3)))
+        self.on_left = [copy(4 - dx, 0, 0, dx, 0, i * part, part) for i, dx in steps]
+        self.on_other = [copy(4 - dx, 1, 0, dx, 0, i * part, part) for i, dx in steps]
+        self.y_right, self.x_right, self.on_right, self.y_near, self.y_far = [], [], [], [], []
+        if right:
+            self.y_right = [copy(0, 0, 1, 0, 1)]
+            self.x_right = [copy(0, 0, 1, dx, 0) for dx in (1, 3)]
+            self.on_right = [copy(4 - dx, 0, 1, dx, 0, i * part, part) for i, dx in steps]
+            self.y_near = [copy(4 - dx, 0, 1, 0, 1) for dx in (1, 3)]
+            self.y_far = [copy(2, 0, 1, 0, 1, i * part, part) for i in range(2)]
 
     def start(self):
-        for copy in (self.y_own[0], *self.x_own[1], self.y_own[1], *self.x_own[0]):
+        for copy in (self.y_left, *self.x_right, *self.y_right, *self.x_left):
             copy.start()
 
     def relay(self):
-        self.y_own[0].wait_recv()
+        self.y_left.wait_recv()
         for copy in self.x_other:
             copy.start()
-        for i in range(2):
-            self.x_own[1][i].wait_recv()
-            self.on[1][i].start()
+        for i, came in enumerate(self.x_right):
+            came.wait_recv()
+            self.on_right[i].start()
             self.y_near[i].start()
 
     def relay_again(self):
         for i in range(2):
-            self.x_own[0][i].wait_recv()
-            self.on[0][i].start()
-        for i in range(2):
-            self.on[1][i].wait_recv()
+            self.x_left[i].wait_recv()
+            self.on_left[i].start()
+        for i, came in enumerate(self.on_right):
+            came.wait_recv()
             self.y_far[i].start()
         for i in range(2):
             self.x_other[i].wait_recv()
             self.on_other[i].start()
 
     def wait(self):
-        self.y_own[1].wait_recv()
-        for copy in (*self.on[0], *self.on_other, *self.y_near, *self.y_far):
+        for copy in (*self.y_right, *self.on_left, *self.on_other, *self.y_near, *self.y_far):
             copy.wait_recv()
-        for copy in (*self.y_own, *self.x_own[0], *self.x_own[1], *self.x_other, *self.on[0], *self.on[1],
-                     *self.on_other, *self.y_near, *self.y_far):
+        for copy in (self.y_left, *self.x_left, *self.x_other, *self.on_left, *self.on_other, *self.y_right,
+                     *self.x_right, *self.on_right, *self.y_near, *self.y_far):
             copy.wait_send()
 
 
@@ -389,18 +390,17 @@
 
 
 class GradSum:
-    def __init__(self, kind, part, out, other, between, far, near, sent, arrived):
+    def __init__(self, kind, part, out, between, far, near, sent, arrived):
         dp, _, col = here()
-        self.kind, self.part, self.dp, self.col = kind, part, dp, col
-        self.other, self.between, self.far, self.near = other, between, far, near
-        self.rows = near.shape[1]
-        number = iter(range(18))
+        self.kind, self.part, self.col = kind, part, col
+        self.between, self.far, self.near = between, far, near
+        self.rows, self.width = near.shape[1], near.shape[2]
+        number = iter(range(10))
 
         def copy(source, target, **where):
             i = next(number)
             return remote(source, target, sent.at[i], arrived.at[i], **where)
 
-        self.core = [copy(self.half(c, 1 - dp), other.at[c], dp=1 - dp) for c in range(8)]
         self.steps = (1, 3)
         self.on = [
             [
@@ -410,44 +410,32 @@
             for i, d in enumerate(self.steps)
         ]
         self.zs = [
-            [copy(self.half(self.z_block(d, k), dp), far.at[i, k], col=z_peer(col, d)) for k in range(2)]
+            [copy(self.block(self.z_block(d, k)), far.at[i, k], col=z_peer(col, d)) for k in range(2)]
             for i, d in enumerate(self.steps)
         ]
         self.ys = copy(near.at[0], near.at[1], col=y_peer(col))
         self.last = copy(near.at[0], half_shard(out, dp), dp=1 - dp)
-        self.keep = pltpu.make_async_copy(near.at[0], half_shard(out, dp), sent.at[18])
+        self.keep = pltpu.make_async_copy(near.at[0], half_shard(out, dp), sent.at[10])
 
     def z_block(self, d, k):
         return z_peer(self.col, d) // 2 * 2 + k
 
-    def half(self, c, h):
-        return half_of(self.kind, self.part, c, h)
+    def block(self, c):
+        if self.kind == "tall":
+            return self.part.at[span(c, self.rows)]
+        return self.part.at[:, span(c, self.width)]
 
     def piece(self, c, i):
-        return self.half(c, self.dp).at[pl.ds(i * (self.rows // 2), self.rows // 2)]
+        return self.block(c).at[pl.ds(i * (self.rows // 2), self.rows // 2)]
+
+    def each(self, rows, body):
+        count = min(rows, 32768 // self.width // 16 * 16)
+
+        @pl.loop(0, rows // count)
+        def _(i):
+            body(span(i, count))
 
     def start(self):
-        for copy in self.core:
-            copy.start()
-
-    def each(self, rows, body):
-        @pl.loop(0, rows // 16)
-        def _(i):
-            body(span(i, 16))
-
-    def over_core(self):
-        for copy in self.core:
-            copy.wait()
-
-        @pl.loop(0, 8)
-        def _(c):
-            own = self.half(c, self.dp)
-
-            def add(at):
-                own[at] = (own[at].astype(F32) + self.other[c, at].astype(F32)).astype(BF16)
-
-            self.each(self.rows, add)
-
         for pair in self.on:
             for copy in pair:
                 copy.start()
@@ -462,7 +450,6 @@
                     own[at] = (own[at].astype(F32) + self.between[i, k, at].astype(F32)).astype(BF16)
 
                 self.each(self.rows // 2, add)
-            for k in range(2):
                 self.zs[i][k].start()
 
     def over_y(self):
@@ -470,7 +457,7 @@
             for copy in pair:
                 copy.wait_recv()
         yl = self.col % 2
-        keep, give = self.half(self.col, self.dp), self.half(y_peer(self.col), self.dp)
+        keep, give = self.block(self.col), self.block(y_peer(self.col))
 
         def total(at, ref, k):
             return (
@@ -493,7 +480,7 @@
 
     def end(self):
         self.ys.wait()
-        keep = self.half(self.col, self.dp)
+        keep = self.block(self.col)
 
         def add(at):
             self.near[0, at] = (keep[at].astype(F32) + self.near[1, at].astype(F32)).astype(BF16)
@@ -510,12 +497,11 @@
 def grad_sum_scratch(shape):
     rows, width = shape[0] // 2, shape[1]
     return [
-        pltpu.VMEM((8, rows, width), BF16),
         pltpu.VMEM((2, 2, rows // 2, width), BF16),
         pltpu.VMEM((2, 2, rows, width), BF16),
         pltpu.VMEM((2, rows, width), BF16),
-        DMA((19,)),
-        DMA((18,)),
+        DMA((11,)),
+        DMA((10,)),
     ]
 
 
@@ -554,8 +540,11 @@
             self.a_far_near.append(copy(block(y_peer(two), i), block(y_peer(two), i), dp=1 - dp))
         self.a_y = copy(block(near), block(near), dp=1 - dp)
 
-    def start(self):
-        for copy in (self.y_own, *self.z_own, self.local):
+    def start_y(self):
+        self.y_own.start()
+
+    def start_z(self):
+        for copy in (*self.z_own, self.local):
             copy.start()
 
     def relay(self):
@@ -691,8 +680,8 @@
     spread_g = SpreadIn(
         lambda k: rows_of(g, k, share), lambda k, c: share_out.at[:, span(c, 256)], gsent, gcame
     )
-    gather_x = Gather(xs, share, asent, acame)
-    gather = Gather(rows, share, bsent, bcame)
+    gather_x = Gather(xs, share, width, asent, acame)
+    gather = Gather(rows, share, width // 2, bsent, bcame)
     scatter = Scatter(part, *refs[:8])
     sums = TokenSums(rates, *refs[8:12])
     bring_heads = Bring("tall", heads16, heads, *refs[12:14])
@@ -717,10 +706,12 @@
     spread_x.start()
     loads[0].wait()
     narrow(heads32, heads16)
-    bring_heads.start()
+    bring_heads.start_y()
+    bring_heads.start_z()
     loads[1].wait()
     narrow(merge32, merge16)
-    bring_merge.start()
+    bring_merge.start_y()
+    bring_merge.start_z()
     loads[2].wait()
     narrow(reduce32, reduce16)
     loads[3].wait()
@@ -730,12 +721,14 @@
     bring_heads.relay()
     bring_heads.relay_own()
     gather_x.relay()
+    bring_expand.start_y()
+    bring_reduce.start_y()
     bring_heads.relay_near()
     bring_merge.relay()
     gather_x.relay_again()
     bring_heads.hand_over()
-    bring_expand.start()
-    bring_reduce.start()
+    bring_expand.start_z()
+    bring_reduce.start_z()
     gather_x.wait()
     bring_heads.wait()
     puts[0].start()
@@ -853,7 +846,8 @@
     out, input_grad, gains_grad, heads_grad, merge_grad, expand_grad, reduce_grad,
     rows, turned, expand, reduce, heads, merge, gate, up, act, act_turned, part, back, hidden, probs, mix, mix_turned,
     rates, stats, grad_mix, done, final, grad_resid, sums, grad_gate,
-    gains, gain_row, gain_col, gain_core, gain_sum, load, late, osent, ocame, isent, icame, nsent, ncame,
+    gains, gain_row, gain_col, gain_core, gain_sum, act_other, turned_other, hidden_other, back_other, mix_other,
+    joined_other, free, load, late, osent, ocame, isent, icame, nsent, ncame, xsent, xcame,
     g1sent, g1came, g2sent, g2came, *refs,
 ):
     dp, row, col = here()
@@ -864,12 +858,15 @@
     n = width // 512
     scatter = [Scatter(part, *refs[:6], *refs[6 + 2 * i : 8 + 2 * i]) for i in range(3)]
     token_sums = TokenSums(stats, *refs[12:16])
-    reduce_sum = GradSum("wide", reduce, reduce_grad, *refs[16:22])
-    expand_sum = GradSum("tall", expand, expand_grad, *refs[22:28])
-    merge_sum = GradSum("wide", merge, merge_grad, *refs[28:34])
-    heads_sum = GradSum("tall", heads, heads_grad, *refs[34:40])
-    gather = Gather(back, share, g1sent, g1came)
-    last_gather = Gather(back, share, g2sent, g2came)
+    half_units, half_width, half_heads = units // 2, width // 2, head_width // 2
+    reduce_part, merge_part = reduce.at[pl.ds(0, half_units)], merge.at[pl.ds(0, half_heads)]
+    expand_part, heads_part = expand.at[pl.ds(0, half_width)], heads.at[pl.ds(0, half_width)]
+    reduce_sum = GradSum("wide", reduce_part, reduce_grad, *refs[16:21])
+    expand_sum = GradSum("tall", expand_part, expand_grad, *refs[21:26])
+    merge_sum = GradSum("wide", merge_part, merge_grad, *refs[26:31])
+    heads_sum = GradSum("tall", heads_part, heads_grad, *refs[31:36])
+    gather = Gather(back, share, width // 2, g1sent, g1came)
+    last_gather = Gather(back, share, width // 2, g2sent, g2came)
     spread = Spread(False, lambda k: cols(done, k, 256), lambda k: rows_of(out, k, 64), osent, ocame)
     spread_grad = Spread(False, lambda k: cols(final, k, 256), lambda k: rows_of(input_grad, k, 64), isent, icame)
     row_gains = [
@@ -902,6 +899,28 @@
     get_qkv = pltpu.make_async_copy(qkv_in, qkv, late.at[6])
     get_xs = pltpu.make_async_copy(xs_in, rows, late.at[7])
 
+    def hand(i, source, target):
+        return remote(source, target, xsent.at[i], xcame.at[i], dp=1 - dp)
+
+    hand_act = hand(0, act_turned.at[span(1 - dp, half_units)], act_other)
+    hand_rows = hand(1, turned.at[span(1 - dp, half_width)], turned_other)
+    hand_back = hand(2, back, back_other)
+    hand_hidden = hand(3, hidden, hidden_other)
+    hand_mix = hand(4, mix_turned.at[span(1 - dp, half_heads)], mix_other)
+    hand_new = hand(5, back, back_other)
+    hand_xs = hand(6, turned.at[span(1 - dp, half_width)], turned_other)
+    hand_joined = hand(7, joined, joined_other)
+
+    def turn_rows(j):
+        values = rows[:, span(j, 256)].T
+        turned[span(j, 128), :] = values[:128]
+        turned[span(2 * tiles + j, 128), :] = values[128:]
+
+    def two(target, at, wide, own, own_at, right, other, right_other):
+        target[at, wide] = (
+            dot(own[own_at, :], right[:, wide]) + dot(other[at, :], right_other[:, wide])
+        ).astype(BF16)
+
     get_rows.start()
     for j in range(tiles):
         get_expand(j).start()
@@ -940,6 +959,7 @@
         at = span(j, 256)
         act_turned[at, :] = act[:, at].T
 
+    hand_act.start()
     for copy in early:
         copy.start()
     get_qkv.start()
@@ -964,14 +984,12 @@
     scatter[0].finish()
     gather.relay()
 
-    @pl.loop(0, 2 * tiles)
-    def _(j):
-        at = span(j, 256)
-        turned[at, :] = rows[:, at].T
-
+    pl.loop(0, 2 * tiles)(turn_rows)
+    hand_rows.start()
     get_xs.start()
     gather.relay_again()
     gather.wait()
+    hand_back.start()
     spread.start()
 
     @pl.loop(0, tiles)
@@ -987,6 +1005,7 @@
             hidden[some, at] = (change * up[some, at] * s * (1.0 + x * (1.0 - s))).astype(BF16)
             hidden[some, up_at] = (change * (x * s)).astype(BF16)
 
+    hand_hidden.start()
     get_raw.start()
 
     def branch(j):
@@ -998,23 +1017,29 @@
     pl.loop(0, n)(branch)
     scatter[1].start_left()
 
+    hand_act.wait()
+    hand_back.wait()
+    halves = [pl.ds(side * (width // 2), width // 2) for side in range(2)]
+
+    @pl.loop(0, tiles // 2)
+    def _(j):
+        for wide in halves:
+            two(reduce, span(j, 256), wide, act_turned, span(dp * (tiles // 2) + j, 256), back, act_other, back_other)
+
+    pl.semaphore_signal(free.at[0], inc=1, device_id={"dp": 1 - dp}, device_id_type=MESH)
+    reduce_sum.start()
+    scatter[1].middle()
+    hand_rows.wait()
+    hand_hidden.wait()
+
     @pl.loop(0, tiles)
     def _(j):
-        at = span(j, 256)
-        for side in range(2):
-            wide = pl.ds(side * (width // 2), width // 2)
-            reduce[at, wide] = dot(act_turned[at, :], back[:, wide]).astype(BF16)
-
-    reduce_sum.start()
-    scatter[1].middle()
-
-    def expand_part(j):
-        at = span(j, 256)
-        for side in range(2):
-            wide = pl.ds(side * (width // 2), width // 2)
-            expand[at, wide] = dot(turned[at, :], hidden[:, wide]).astype(BF16)
-
-    pl.loop(0, tiles)(expand_part)
+        for wide in halves:
+            two(expand, span(j, 256), wide, turned, span(dp * tiles + j, 256), hidden, turned_other, hidden_other)
+
+    pl.semaphore_signal(free.at[1], inc=1, device_id={"dp": 1 - dp}, device_id_type=MESH)
+    expand_sum.start()
+    reduce_sum.over_z()
     scatter[1].end()
     sums[...] = jnp.zeros_like(sums)
 
@@ -1030,27 +1055,23 @@
 
     last_gather.start()
     gains[2:3] = jnp.sum(sums[...], axis=0, keepdims=True)
-    pl.loop(tiles, 2 * tiles)(expand_part)
-    expand_sum.start()
+    get_xs.wait()
+    pl.loop(0, 2 * tiles)(turn_rows)
+    pl.semaphore_wait(free.at[1], 1)
+    hand_xs.start()
     last_gather.relay()
-    reduce_sum.over_core()
     last_gather.relay_again()
-    get_xs.wait()
-
-    @pl.loop(0, 2 * tiles)
-    def _(j):
-        at = span(j, 256)
-        turned[at, :] = rows[:, at].T
-
     for copy in early:
         copy.wait()
     get_raw.wait()
     get_qkv.wait()
     mix_turned[...] = mix[...].T
-    expand_sum.over_core()
-    reduce_sum.over_z()
+    hand_mix.start()
+    expand_sum.over_z()
     scatter[1].finish()
     last_gather.wait()
+    pl.semaphore_wait(free.at[0], 1)
+    hand_new.start()
 
     live = (docs[:, 0:1] < 5.0).astype(F32)
     grad_mix[...] = (dot_flipped(new_rows[...], merge[...]) * live).astype(BF16)
@@ -1073,6 +1094,7 @@
             heads_change[key_at, key] += dot(grad_scores.T, qkv[query_at, query]) * HD**-0.5
             heads_change[key_at, value] += dot(shares.T, change)
 
+    reduce_sum.over_y()
     sums[...] = jnp.zeros_like(sums)
 
     @pl.loop(0, tokens // 64)
@@ -1094,9 +1116,14 @@
     gains[1:2, span(row, head_width)] = jnp.sum(sums[:, head_width : 2 * head_width], axis=0, keepdims=True)
     for copy in row_gains:
         copy.start()
+    hand_mix.wait()
+    hand_new.wait()
+    mine = span(dp, half_heads)
     for side in range(4):
         wide = pl.ds(side * (width // 4), width // 4)
-        merge[:, wide] = dot(mix_turned[...], new_rows[:, wide]).astype(BF16)
+        merge[:half_heads, wide] = (
+            dot(mix_turned[mine, :], back[:, wide]) + dot(mix_other[...], back_other[:, wide])
+        ).astype(BF16)
     merge_sum.start()
     joined[:, 2 * head_width :] = heads_change[:, 2 * head_width :].astype(BF16)
     token_sums.end()
@@ -1111,28 +1138,7 @@
             hat = raw[at, some] * rate
             joined[at, some] = (rate * (heads_change[at, some] - hat * dots[:, j : j + 1])).astype(BF16)
 
-    def input_part(j):
-        at = span(j, 256)
-        part[:, at] = dot_flipped(joined[...], heads[at, :]).astype(BF16)
-
-    pl.loop(n, 2 * n)(input_part)
-    scatter[2].start_right()
-    pl.loop(0, n)(input_part)
-    scatter[2].start_left()
-
-    @pl.loop(0, 2 * tiles)
-    def _(j):
-        at = span(j, 256)
-        heads[at, :] = dot(turned[at, :], joined[...]).astype(BF16)
-
-    heads_sum.start()
-    merge_sum.over_core()
-    scatter[2].middle()
-    expand_sum.over_z()
-    heads_sum.over_core()
-    scatter[2].end()
-    final[...] = grad_resid[...] + scatter[2].total[...]
-    spread_grad.start()
+    hand_joined.start()
     for copy in row_gains:
         copy.wait()
     gain_row[row] = gains[...]
@@ -1143,8 +1149,33 @@
     gain_col[col] = total
     for copy in col_gains:
         copy.start()
+
+    def input_part(j):
+        at = span(j, 256)
+        part[:, at] = dot_flipped(joined[...], heads[at, :]).astype(BF16)
+
+    pl.loop(n, 2 * n)(input_part)
+    scatter[2].start_right()
+    pl.loop(0, n)(input_part)
+    scatter[2].start_left()
+
+    hand_xs.wait()
+    hand_joined.wait()
+    everything = pl.ds(0, 3 * head_width)
+
+    @pl.loop(0, tiles)
+    def _(j):
+        two(heads, span(j, 256), everything, turned, span(dp * tiles + j, 256), joined, turned_other, joined_other)
+
+    heads_sum.start()
+    expand_sum.over_y()
     merge_sum.over_z()
+    reduce_sum.end()
+    scatter[2].middle()
     heads_sum.over_z()
+    scatter[2].end()
+    final[...] = (grad_resid[...] + scatter[2].total[...]).astype(BF16)
+    spread_grad.start()
     for copy in col_gains:
         copy.wait()
     total = gain_col[0]
@@ -1152,9 +1183,6 @@
         total = total + gain_col[k]
     gain_sum[1] = total
     core_gains.start()
-    reduce_sum.over_y()
-    expand_sum.over_y()
-    reduce_sum.end()
     merge_sum.over_y()
     heads_sum.over_y()
     expand_sum.end()
@@ -1270,7 +1298,7 @@
         rest_kernel, "rest", 2,
         [
             struct(block_input.shape, BF16),
-            struct(block_input.shape, F32),
+            struct(block_input.shape, BF16),
             struct(gain_shape, F32),
             struct(heads_weight.shape, BF16),
             struct(merge_weight.shape, BF16),
@@ -1304,7 +1332,7 @@
             pltpu.VMEM((seq_len, 128), F32),
             pltpu.VMEM((seq_len, head_width), BF16),
             pltpu.VMEM((share, model_width), BF16),
-            pltpu.VMEM((share, model_width), F32),
+            pltpu.VMEM((share, model_width), BF16),
             pltpu.VMEM((share, model_width), F32),
             pltpu.VMEM((8, model_width), F32),
             pltpu.VMEM((seq_len, 256), F32),
@@ -1313,7 +1341,14 @@
             pltpu.VMEM((8, *gain_shape), F32),
             pltpu.VMEM(gain_shape, F32),
             pltpu.VMEM((2, *gain_shape), F32),
-            DMA((10,)), DMA((8,)), DMA((8,)), DMA((8,)), DMA((8,)), DMA((8,)), DMA((15,)), DMA((15,)),
+            pltpu.VMEM((unit_width // 2, seq_len), BF16),
+            pltpu.VMEM((model_width // 2, seq_len), BF16),
+            pltpu.VMEM((seq_len, model_width), BF16),
+            pltpu.VMEM((seq_len, model_width), BF16),
+            pltpu.VMEM((head_width // 2, seq_len), BF16),
+            pltpu.VMEM((seq_len, 3 * head_width), BF16),
+            pltpu.SemaphoreType.REGULAR((2,)),
+            DMA((10,)), DMA((8,)), DMA((8,)), DMA((8,)), DMA((8,)), DMA((8,)), DMA((15,)), DMA((15,)), DMA((8,)), DMA((8,)),
         ]
         + gather_scratch() + gather_scratch()
         + scatter_scratch(share, model_width) + [DMA((14,))] * 4
@@ -1341,7 +1376,7 @@
     )
     return (
         block_output,
-        input_grad,
+        input_grad.astype(F32),
         heads_grad,
         heads_mean,
         heads_square,

time: 333 us -> 296 us (0.89)
  Pallas kernels: 300 us -> 263 us
    pallas_call x2, Pallas kernels: 300 us -> 263 us  [call(): pl.pallas_call(kernel, name=name, out_shape=outs, in_specs=in_specs, out_...]
where the time goes in v5:
time: 296 us; the launch traced here: 291 us
  Pallas kernels  263 us (89%)
  other arithmetic  18.2 us (6%)
  local copies, waits for them, and re-layouts  8.27 us (3%)
    pallas_call x2, Pallas kernels, call(): pl.pallas_call(kernel, name=name, out_shape=outs, in_specs=in_specs, out_...  263 us

profile of v5, /device:TPU:9, one launch (start us, length us, event | category | flops | bytes accessed | tf_op | source)
XLA Modules:
  0.0 290.8 jit_solution(17182246361978834036)
XLA Ops:
  0.7 0.8 reduce-window.8
  1.5 0.7 convert_reduce_fusion
  2.3 0.6 broadcast_in_dim.22.doc_row
  2.9 1.5 fusion.15
  4.4 0.6 constant_dynamic-slice_fusion
  5.0 0.8 broadcast_in_dim.21.docs
  5.8 1.0 fusion.4
  6.8 1.0 pad_maximum_fusion
  7.8 101.0 %attend.1 = (bf16[512,2048]{1,0:T(8,128)(2,1)}, bf16[64,2048]{1,0:T(8,128)(2,1)}, bf16[2048,768]{1,0:T(8,128)(2,1)}, bf16[256,2048]{1,0:T(8,128)(2,1)}, bf16[204...) custom-call(bf16[512,256]{1,0:T(8,128)(2,1)} %x.1, ...), custom_call_target="tpu_custom_call" | custom-call | tf_op jit(solution)/shard_map/attend/pallas_call | solution.py:175
  108.9 162.4 %rest.1 = (bf16[512,256]{1,0:T(8,128)(2,1)}, bf16[512,256]{1,0:T(8,128)(2,1)}, f32[4,2048]{1,0:T(4,128)}, bf16[256,768]{1,0:T(8,128)(2,1)}, bf16[256,256]{1,0:T(...) custom-call(bf16[512,2048]{1,0:T(8,128)(2,1)} %get-tuple-element.47.rows_in, ...), custom_call_target="tpu_custom_call" | custom-call | tf_op jit(solution)/shard_map/rest/pallas_call | solution.py:175
  271.4 1.6 multiply_subtract_fusion.4
  273.0 1.8 convert_element_type.52
  274.8 2.0 fusion.11
  276.8 2.0 fusion.13
  278.8 0.4 copy-done.7
  279.3 0.7 copy-done.8
  279.9 0.1 copy-done.11
  280.1 2.7 fusion.7
  282.7 1.2 copy-done.3
  284.0 0.6 copy-done.4
  284.6 0.2 copy-done.5
  284.8 4.6 %fusion.9 = (bf16[256,2048]{1,0:T(8,128)(2,1)}, f32[256,2048]{1,0:T(8,128)}, f32[256,2048]{1,0:T(8,128)}, f32[256,2048]{1,0:T(8,128)}, f32[256,2048]{1,0:T(8,128)}) fusion(f32[256,2048]{1,0:T(8,128)S(1)} %copy-done, f32[256,2048]{1,0:T(8,128)S(1)} %copy-done.3, f32[256,2048]{1,0:T(8,128)S(1)} %copy-done.4, bf16[256,2048]{1,0:T(8,128)(2,1)S(1)} %copy-done.5), kind=kLoop, calls=%fused_computation.33 | loop fusion | flops 8388608 | bytes 16777216 | tf_op jit(solution)/shard_map/convert_element_type | solution.py:1394
  289.5 0.7 copy.46
  290.2 0.6 copy.47
  (37 shorter events, 0.1 us)
Async XLA Ops:
  108.9 162.5 %copy-start.16 = (f32[4,2048]{1,0:T(4,128)S(1)}, f32[4,2048]{1,0:T(4,128)}, u32[]{:S(2)}) copy-start(f32[4,2048]{1,0:T(4,128)} %param.33) | copy-start | bytes 98308
  108.9 162.5 %copy-start.18 = (f32[4,2048]{1,0:T(4,128)S(1)}, f32[4,2048]{1,0:T(4,128)}, u32[]{:S(2)}) copy-start(f32[4,2048]{1,0:T(4,128)} %param.35) | copy-start | bytes 98308
  108.9 162.5 %copy-start.19 = (f32[4,2048]{1,0:T(4,128)S(1)}, f32[4,2048]{1,0:T(4,128)}, u32[]{:S(2)}) copy-start(f32[4,2048]{1,0:T(4,128)} %param.34) | copy-start | bytes 98308
  108.9 165.9 %copy-start.6 = (f32[256,256]{1,0:T(8,128)S(1)}, f32[256,256]{1,0:T(8,128)}, u32[]{:S(2)}) copy-start(f32[256,256]{1,0:T(8,128)} %merge_in.1) | copy-start | bytes 786436
  108.9 165.9 %copy-start.14 = (f32[256,256]{1,0:T(8,128)S(1)}, f32[256,256]{1,0:T(8,128)}, u32[]{:S(2)}) copy-start(f32[256,256]{1,0:T(8,128)} %param.26) | copy-start | bytes 786436
  108.9 165.9 %copy-start.15 = (f32[256,256]{1,0:T(8,128)S(1)}, f32[256,256]{1,0:T(8,128)}, u32[]{:S(2)}) copy-start(f32[256,256]{1,0:T(8,128)} %param.25) | copy-start | bytes 786436
  271.3 5.4 %copy-start.2 = (f32[256,768]{1,0:T(8,128)S(1)}, f32[256,768]{1,0:T(8,128)}, u32[]{:S(2)}) copy-start(f32[256,768]{1,0:T(8,128)} %heads_in.1) | copy-start | bytes 2359300
  271.4 5.4 %copy-start.9 = (f32[256,768]{1,0:T(8,128)S(1)}, f32[256,768]{1,0:T(8,128)}, u32[]{:S(2)}) copy-start(f32[256,768]{1,0:T(8,128)} %param.23) | copy-start | bytes 2359300
  271.4 5.4 %copy-start.10 = (f32[256,768]{1,0:T(8,128)S(1)}, f32[256,768]{1,0:T(8,128)}, u32[]{:S(2)}) copy-start(f32[256,768]{1,0:T(8,128)} %param.22) | copy-start | bytes 2359300
  271.4 5.4 %copy-start.12 = (bf16[256,768]{1,0:T(8,128)(2,1)S(1)}, bf16[256,768]{1,0:T(8,128)(2,1)}, u32[]{:S(2)}) copy-start(bf16[256,768]{1,0:T(8,128)(2,1)} %get-tuple-element.63) | copy-start | bytes 1179652
  276.8 2.1 copy-start.1
  276.8 2.5 copy-start.7
  276.8 3.1 %copy-start.8 = (f32[1024,256]{1,0:T(8,128)S(1)}, f32[1024,256]{1,0:T(8,128)}, u32[]{:S(2)}) copy-start(f32[1024,256]{1,0:T(8,128)} %param.31) | copy-start | bytes 3145732
  276.8 3.2 %copy-start.11 = (bf16[1024,256]{1,0:T(8,128)(2,1)S(1)}, bf16[1024,256]{1,0:T(8,128)(2,1)}, u32[]{:S(2)}) copy-start(bf16[1024,256]{1,0:T(8,128)(2,1)} %get-tuple-element.66) | copy-start | bytes 1572868
  280.1 2.7 copy-start
  280.1 3.9 %copy-start.3 = (f32[256,2048]{1,0:T(8,128)S(1)}, f32[256,2048]{1,0:T(8,128)}, u32[]{:S(2)}) copy-start(f32[256,2048]{1,0:T(8,128)} %param.29) | copy-start | bytes 6291460
  280.1 4.5 %copy-start.4 = (f32[256,2048]{1,0:T(8,128)S(1)}, f32[256,2048]{1,0:T(8,128)}, u32[]{:S(2)}) copy-start(f32[256,2048]{1,0:T(8,128)} %param.28) | copy-start | bytes 6291460
  280.1 4.8 %copy-start.5 = (bf16[256,2048]{1,0:T(8,128)(2,1)S(1)}, bf16[256,2048]{1,0:T(8,128)(2,1)}, u32[]{:S(2)}) copy-start(bf16[256,2048]{1,0:T(8,128)(2,1)} %get-tuple-element.65) | copy-start | bytes 3145732
  284.8 4.6 %copy-start.13 = (bf16[512,256]{1,0:T(8,128)(2,1)S(1)}, bf16[512,256]{1,0:T(8,128)(2,1)}, u32[]{:S(2)}) copy-start(bf16[512,256]{1,0:T(8,128)(2,1)} %get-tuple-element.130) | copy-start | bytes 786436
  284.8 5.3 %copy-start.17 = (f32[4,2048]{1,0:T(4,128)S(1)}, f32[4,2048]{1,0:T(4,128)}, u32[]{:S(2)}) copy-start(f32[4,2048]{1,0:T(4,128)} %get-tuple-element.152) | copy-start | bytes 98308

commit v6 on v5

--- a/solution.py
+++ b/solution.py
@@ -1,4 +1,4 @@
-import functools
+import math
 
 import jax
 import jax.numpy as jnp
@@ -29,14 +29,15 @@
 DMA = pltpu.SemaphoreType.DMA
 
 
-def positions(lengths, row_count):
-    doc_ends = jnp.cumsum(lengths)
-    index_ids = jnp.arange(row_count, dtype=jnp.int32)
-    passed = doc_ends[None, :] <= index_ids[:, None]
-    doc_ids = jnp.sum(passed.astype(jnp.int32), axis=1)
-    starts = jnp.sum(jnp.where(passed, lengths[None, :], 0), axis=1)
-    live_rows = (doc_ids < lengths.shape[0] - 1).astype(jnp.float32)
-    return (doc_ids, index_ids - starts, live_rows)
+def documents(lengths, shape, axis):
+    tokens = lax.broadcasted_iota(jnp.int32, shape, axis)
+    docs, starts, end = jnp.zeros(shape, F32), jnp.zeros(shape, jnp.int32), jnp.int32(0)
+    for j in range(lengths.shape[1]):
+        end = end + lengths[0, j]
+        passed = tokens >= end
+        docs = docs + passed.astype(F32)
+        starts = starts + jnp.where(passed, lengths[0, j], 0)
+    return docs, starts
 
 
 def adamw(weight, gradient, first_mom, second_mom, step_rate, decay_rate):
@@ -506,9 +507,9 @@
 
 
 class Bring:
-    def __init__(self, kind, shard, whole, sent, arrived):
+    def __init__(self, kind, shape, whole, sent, arrived):
         dp, _, col = here()
-        rows, width = shard.shape
+        rows, width = shape
         near = y_peer(col)
         number = iter(range(20))
 
@@ -522,11 +523,9 @@
             i = next(number)
             return remote(source, target, sent.at[i], arrived.at[i], **where)
 
-        mine = half_shard(shard, dp)
-        place = whole.at[span(col, rows)] if kind == "tall" else whole.at[:, span(col, width)]
-        self.local = pltpu.make_async_copy(shard, place, sent.at[20])
-        self.y_own = copy(mine, block(col), col=near)
-        self.z_own = [copy(mine, block(col), col=z_peer(col, d)) for d in (1, 3)]
+        self.place = whole.at[span(col, rows)] if kind == "tall" else whole.at[:, span(col, width)]
+        self.y_own = copy(block(col), block(col), col=near)
+        self.z_own = [copy(block(col), block(col), col=z_peer(col, d)) for d in (1, 3)]
         self.z_near = [copy(block(near), block(near), col=z_peer(col, d)) for d in (1, 3)]
         self.on, self.on_near, self.a_own, self.a_near = [], [], [], []
         self.a_far, self.a_far_near = [], []
@@ -544,7 +543,7 @@
         self.y_own.start()
 
     def start_z(self):
-        for copy in (*self.z_own, self.local):
+        for copy in self.z_own:
             copy.start()
 
     def relay(self):
@@ -577,11 +576,10 @@
             copy.wait()
         for copy in (self.y_own, *self.z_own, *self.z_near, *self.on, *self.on_near):
             copy.wait_send()
-        self.local.wait()
 
 
 def bring_scratch():
-    return [DMA((21,)), DMA((20,))]
+    return [DMA((20,)), DMA((20,))]
 
 
 class SpreadIn:
@@ -654,68 +652,125 @@
     return start, (b + 1) * QUERY_BLOCK - start
 
 
-def attend_kernel(
-    x, g, heads_in, merge_in, expand_in, reduce_in, cosine, sine, docs, doc_row, gain_query, gain_key, gain_merge,
-    xs_out, share_out, heads_out, merge_out, expand_out, reduce_out, raw_out, qkv_out, probs_out, mix_out, rates_out,
-    merged, residual, rows_out,
-    xs, heads32, merge32, expand32, reduce32, heads16, merge16, expand16, reduce16, heads, merge, raw, qkv, probs, mix,
-    rates, part, rows, load, put, xsent, xcame, gsent, gcame, asent, acame, bsent, bcame, *refs,
+def layer_kernel(
+    x, g_in, heads_in, merge_in, expand_in, reduce_in, lengths, gain_all,
+    out, input_grad, gains_grad, heads_grad, merge_grad, expand_grad, reduce_grad, xs_keep, raw_keep, qkv_keep,
+    rows, turned, expand, reduce, heads, merge, gate, up, act, act_turned, part, back, hidden, probs, mix, mix_turned,
+    rates, stats, grad_mix, done, final, grad_resid, merged, residual, g, sums, grad_gate,
+    gains, gain_row, gain_col, gain_core, gain_sum, act_other, turned_other, hidden_other, back_other, mix_other,
+    joined_other, docs, doc_row, cosine, sine, free, load, keep, late, osent, ocame, isent, icame, nsent, ncame, xsent, xcame,
+    asent, acame, bsent, bcame, g1sent, g1came, g2sent, g2came, g3sent, g3came, g4sent, g4came, *refs,
 ):
     dp, row, col = here()
-    share, width = merged.shape
-    tokens = xs.shape[0]
+    share, width = residual.shape
+    tokens, units = act.shape
     head_width = mix.shape[1]
-    own = span(row, share)
-    loads = [
-        pltpu.make_async_copy(source, target, load.at[i])
-        for i, (source, target) in enumerate(
-            ((heads_in, heads32), (merge_in, merge32), (reduce_in, reduce32), (expand_in, expand32))
-        )
+    tiles = units // 256
+    n = width // 512
+    gain_query, gain_key = (gain_all.at[i : i + 1, span(row, head_width)] for i in range(2))
+    gain_merge, gain_reduce = (gain_all.at[i : i + 1] for i in range(2, 4))
+    scatter = [Scatter(part, *refs[:6], *refs[6 + 2 * i : 8 + 2 * i]) for i in range(4)]
+    first_sums = TokenSums(rates, *refs[14:18])
+    token_sums = TokenSums(stats, *refs[18:22])
+    half_units, half_width, half_heads = units // 2, width // 2, head_width // 2
+    reduce_part, merge_part_ref = reduce.at[pl.ds(0, half_units)], merge.at[pl.ds(0, half_heads)]
+    expand_part, heads_part = expand.at[pl.ds(0, half_width)], heads.at[pl.ds(0, half_width)]
+    reduce_sum = GradSum("wide", reduce_part, reduce_grad, *refs[22:27])
+    expand_sum = GradSum("tall", expand_part, expand_grad, *refs[27:32])
+    merge_sum = GradSum("wide", merge_part_ref, merge_grad, *refs[32:37])
+    heads_sum = GradSum("tall", heads_part, heads_grad, *refs[37:42])
+    bring_heads = Bring("tall", heads_in.shape, heads, *refs[42:44])
+    bring_merge = Bring("wide", merge_in.shape, merge, *refs[44:46])
+    bring_reduce = Bring("wide", reduce_in.shape, reduce, *refs[46:48])
+    bring_expand = Bring("tall", expand_in.shape, expand, *refs[48:50])
+    gather_x = Gather(back, share, width, g1sent, g1came)
+    row_gather = Gather(rows, share, width // 2, g2sent, g2came)
+    gather = Gather(back, share, width // 2, g3sent, g3came)
+    last_gather = Gather(back, share, width // 2, g4sent, g4came)
+    spread_x = SpreadIn(
+        lambda k: rows_of(x, k, share), lambda k, c: back.at[span(k, share), span(c, 256)], asent, acame
+    )
+    spread_g = SpreadIn(lambda k: rows_of(g_in, k, share), lambda k, c: g.at[:, span(c, 256)], bsent, bcame)
+    spread = Spread(False, lambda k: cols(done, k, 256), lambda k: rows_of(out, k, 64), osent, ocame)
+    spread_grad = Spread(False, lambda k: cols(final, k, 256), lambda k: rows_of(input_grad, k, 64), isent, icame)
+    row_gains = [
+        remote(gains, gain_row.at[row], nsent.at[d - 1], ncame.at[d - 1], row=row_peer(row, d))
+        for d in range(1, 8)
     ]
+    col_gains = [
+        remote(gain_sum.at[0], gain_col.at[col], nsent.at[6 + d], ncame.at[6 + d], col=(col + d) % 8)
+        for d in range(1, 8)
+    ]
+    core_gains = remote(gain_sum.at[1], gain_core, nsent.at[14], ncame.at[14], dp=1 - dp)
+
+    raw, qkv, new_rows = up.at[:, : 2 * head_width], act.at[:, : 3 * head_width], back
+    heads_change = gate.at[:, : 3 * head_width]
+    joined = hidden.at[:, : 3 * head_width]
+    puts = [
+        pltpu.make_async_copy(source, target, keep.at[i])
+        for i, (source, target) in enumerate(((back, xs_keep), (raw, raw_keep), (qkv, qkv_keep)))
+    ]
+    get_xs = pltpu.make_async_copy(xs_keep, rows, late.at[0])
+    get_raw = pltpu.make_async_copy(raw_keep, raw, late.at[1])
+    get_qkv = pltpu.make_async_copy(qkv_keep, qkv, late.at[2])
+
+    shard_rows, quarter = heads_in.shape[0], reduce_in.shape[0] // 4
+    heads32 = gate.at[:shard_rows, : heads_in.shape[1]]
+    merge32 = gate.at[:shard_rows, heads_in.shape[1] :]
+    reduce32 = [gate.at[shard_rows:, pl.ds(i * 256, 256)] for i in range(4)]
+    expand32 = [up.at[pl.ds(i * shard_rows, shard_rows)] for i in range(2)]
+    moves = (
+        [(heads_in, heads32), (merge_in, merge32)]
+        + [(reduce_in.at[pl.ds(i * quarter, quarter)], reduce32[i]) for i in range(4)]
+        + [(expand_in.at[:, pl.ds(i * units, units)], expand32[i]) for i in range(2)]
+    )
+    loads = [pltpu.make_async_copy(source, target, load.at[i]) for i, (source, target) in enumerate(moves)]
     for copy in loads:
         copy.start()
-    spread_x = SpreadIn(
-        lambda k: rows_of(x, k, share), lambda k, c: xs.at[span(k, share), span(c, 256)], xsent, xcame
-    )
-    spread_g = SpreadIn(
-        lambda k: rows_of(g, k, share), lambda k, c: share_out.at[:, span(c, 256)], gsent, gcame
-    )
-    gather_x = Gather(xs, share, width, asent, acame)
-    gather = Gather(rows, share, width // 2, bsent, bcame)
-    scatter = Scatter(part, *refs[:8])
-    sums = TokenSums(rates, *refs[8:12])
-    bring_heads = Bring("tall", heads16, heads, *refs[12:14])
-    bring_merge = Bring("wide", merge16, merge, *refs[14:16])
-    bring_reduce = Bring("wide", reduce16, reduce_out, *refs[16:18])
-    bring_expand = Bring("tall", expand16, expand_out, *refs[18:20])
-    puts = [
-        pltpu.make_async_copy(source, target, put.at[i])
-        for i, (source, target) in enumerate(
-            ((xs, xs_out), (heads, heads_out), (merge, merge_out), (raw, raw_out), (qkv, qkv_out),
-             (probs, probs_out), (mix, mix_out), (rates, rates_out), (rows, rows_out))
-        )
-    ]
-
-    def narrow(source, target):
+
+    def narrow(i, target):
+        loads[i].wait()
+        source = moves[i][1]
+
         @pl.loop(0, source.shape[0] // 16)
-        def _(i):
-            at = span(i, 16)
+        def _(k):
+            at = span(k, 16)
             target[at] = source[at].astype(BF16)
 
-    meet(rows=True, weights=True, core=True, spread_in=True)
+    def hand(i, source, target):
+        return remote(source, target, xsent.at[i], xcame.at[i], dp=1 - dp)
+
+    hand_act = hand(0, act_turned.at[span(1 - dp, half_units)], act_other)
+    hand_rows = hand(1, turned.at[span(1 - dp, half_width)], turned_other)
+    hand_back = hand(2, back, back_other)
+    hand_hidden = hand(3, hidden, hidden_other)
+    hand_mix = hand(4, mix_turned.at[span(1 - dp, half_heads)], mix_other)
+    hand_new = hand(5, back, back_other)
+    hand_xs = hand(6, turned.at[span(1 - dp, half_width)], turned_other)
+    hand_joined = hand(7, joined, joined_other)
+
+    def turn_rows(j):
+        values = rows[:, span(j, 256)].T
+        turned[span(j, 128), :] = values[:128]
+        turned[span(2 * tiles + j, 128), :] = values[128:]
+
+    def two(target, at, wide, own, own_at, right, other, right_other):
+        target[at, wide] = (
+            dot(own[own_at, :], right[:, wide]) + dot(other[at, :], right_other[:, wide])
+        ).astype(BF16)
+
+    meet(rows=True, cols=True, core=True, spread_in=True, spread_out=True)
     spread_x.start()
-    loads[0].wait()
-    narrow(heads32, heads16)
+    narrow(0, bring_heads.place)
     bring_heads.start_y()
     bring_heads.start_z()
-    loads[1].wait()
-    narrow(merge32, merge16)
+    narrow(1, bring_merge.place)
     bring_merge.start_y()
     bring_merge.start_z()
-    loads[2].wait()
-    narrow(reduce32, reduce16)
-    loads[3].wait()
-    narrow(expand32, expand16)
+    for i in range(4):
+        narrow(2 + i, bring_reduce.place.at[pl.ds(i * quarter, quarter)])
+    for i in range(2):
+        narrow(6 + i, bring_expand.place.at[:, pl.ds(i * units, units)])
     spread_x.wait()
     gather_x.start()
     bring_heads.relay()
@@ -726,34 +781,41 @@
     bring_heads.relay_near()
     bring_merge.relay()
     gather_x.relay_again()
+    bring_merge.relay_own()
     bring_heads.hand_over()
+    bring_merge.relay_near()
     bring_expand.start_z()
     bring_reduce.start_z()
+    docs[...], starts = documents(lengths, docs.shape, 0)
+    doc_row[...], _ = documents(lengths, doc_row.shape, 1)
+    lane = lax.broadcasted_iota(jnp.int32, docs.shape, 1)
+    frequency = jnp.exp((lane % (HD // 2)).astype(F32) * (-2.0 / HD * math.log(THETA)))
+    angles = (lax.broadcasted_iota(jnp.int32, docs.shape, 0) - starts).astype(F32) * frequency
+    cosine[...] = jnp.cos(angles)
+    sine[...] = jnp.where(lane < HD // 2, -1.0, 1.0) * jnp.sin(angles)
     gather_x.wait()
     bring_heads.wait()
     puts[0].start()
-    puts[1].start()
 
     for i in range(2):
         raw[:, i * head_width : (i + 1) * head_width] = dot(
-            xs[...], heads[:, i * head_width : (i + 1) * head_width]
+            back[...], heads[:, i * head_width : (i + 1) * head_width]
         )
 
     @pl.loop(0, tokens // 64)
     def _(i):
         at = span(i, 64)
         squares = raw[at] * raw[at]
-        sums.put(
+        first_sums.put(
             at,
             jnp.sum(squares[:, :head_width], axis=1, keepdims=True),
             jnp.sum(squares[:, head_width:], axis=1, keepdims=True),
         )
 
-    sums.start()
-    qkv[:, 2 * head_width :] = dot(xs[...], heads[:, 2 * head_width :]).astype(BF16)
-    bring_merge.relay_own()
-    bring_merge.relay_near()
-    sums.end()
+    first_sums.start()
+    qkv[:, 2 * head_width :] = dot(back[...], heads[:, 2 * head_width :]).astype(BF16)
+    bring_merge.hand_over()
+    first_sums.end()
     spread_g.start()
 
     @pl.loop(0, tokens // 64)
@@ -766,9 +828,8 @@
             hat = raw[at, some] * rate[:, j : j + 1]
             qkv[at, some] = turn(hat * gain[...], cosine[at], sine[at]).astype(BF16)
 
-    puts[3].start()
-    puts[4].start()
-    puts[7].start()
+    puts[1].start()
+    puts[2].start()
     for b in range(tokens // QUERY_BLOCK):
         start, count = key_span(b)
         query_at = pl.ds(b * QUERY_BLOCK, QUERY_BLOCK)
@@ -791,148 +852,47 @@
                 probs[h, b, :, count:] = jnp.zeros((QUERY_BLOCK, probs.shape[3] - count), BF16)
             mix[query_at, h * HD : (h + 1) * HD] = (dot(shares, qkv[key_at, value]) * live).astype(BF16)
 
-    puts[5].start()
-    puts[6].start()
     bring_expand.relay()
     bring_reduce.relay()
-    bring_merge.hand_over()
     bring_merge.wait()
-    puts[2].start()
 
     def merge_part(j):
         at = span(j, 256)
         part[:, at] = dot(mix[...], merge[:, at]).astype(BF16)
 
-    n = width // 512
     pl.loop(n, 2 * n)(merge_part)
-    scatter.start_right()
+    scatter[0].start_right()
     pl.loop(0, n)(merge_part)
-    scatter.start_left()
+    scatter[0].start_left()
     bring_expand.relay_own()
     bring_reduce.relay_own()
-    scatter.middle()
+    scatter[0].middle()
     bring_expand.relay_near()
     bring_reduce.relay_near()
-    scatter.end()
+    scatter[0].end()
 
     @pl.loop(0, share // 16)
     def _(i):
         at = span(i, 16)
-        total = scatter.total[at]
+        total = scatter[0].total[at]
         merged[at] = total
         mine = pl.ds(pl.multiple_of(row * share + i * 16, 16), 16)
-        result = xs[mine, :].astype(F32) + total * mean_rate(total) * gain_merge[...]
+        result = back[mine, :].astype(F32) + total * mean_rate(total) * gain_merge[...]
         residual[at] = result
         rows[mine, :] = result.astype(BF16)
 
-    gather.start()
-    gather.relay()
+    row_gather.start()
+    row_gather.relay()
     bring_expand.hand_over()
-    gather.relay_again()
+    row_gather.relay_again()
     bring_reduce.hand_over()
-    gather.wait()
-    puts[8].start()
-    scatter.finish()
-    spread_g.wait()
+    row_gather.wait()
+    scatter[0].finish()
     bring_expand.wait()
-    bring_reduce.wait()
     for copy in puts:
         copy.wait()
-
-
-def rest_kernel(
-    rows_in, expand_in, reduce_in, heads_in, merge_in, xs_in, raw_in, qkv_in, probs_in, mix_in, rates_in,
-    residual, g, merged, cosine, sine, docs, gain_query, gain_key, gain_merge, gain_reduce,
-    out, input_grad, gains_grad, heads_grad, merge_grad, expand_grad, reduce_grad,
-    rows, turned, expand, reduce, heads, merge, gate, up, act, act_turned, part, back, hidden, probs, mix, mix_turned,
-    rates, stats, grad_mix, done, final, grad_resid, sums, grad_gate,
-    gains, gain_row, gain_col, gain_core, gain_sum, act_other, turned_other, hidden_other, back_other, mix_other,
-    joined_other, free, load, late, osent, ocame, isent, icame, nsent, ncame, xsent, xcame,
-    g1sent, g1came, g2sent, g2came, *refs,
-):
-    dp, row, col = here()
-    share, width = residual.shape
-    tokens, units = act.shape
-    head_width = mix.shape[1]
-    tiles = units // 256
-    n = width // 512
-    scatter = [Scatter(part, *refs[:6], *refs[6 + 2 * i : 8 + 2 * i]) for i in range(3)]
-    token_sums = TokenSums(stats, *refs[12:16])
-    half_units, half_width, half_heads = units // 2, width // 2, head_width // 2
-    reduce_part, merge_part = reduce.at[pl.ds(0, half_units)], merge.at[pl.ds(0, half_heads)]
-    expand_part, heads_part = expand.at[pl.ds(0, half_width)], heads.at[pl.ds(0, half_width)]
-    reduce_sum = GradSum("wide", reduce_part, reduce_grad, *refs[16:21])
-    expand_sum = GradSum("tall", expand_part, expand_grad, *refs[21:26])
-    merge_sum = GradSum("wide", merge_part, merge_grad, *refs[26:31])
-    heads_sum = GradSum("tall", heads_part, heads_grad, *refs[31:36])
-    gather = Gather(back, share, width // 2, g1sent, g1came)
-    last_gather = Gather(back, share, width // 2, g2sent, g2came)
-    spread = Spread(False, lambda k: cols(done, k, 256), lambda k: rows_of(out, k, 64), osent, ocame)
-    spread_grad = Spread(False, lambda k: cols(final, k, 256), lambda k: rows_of(input_grad, k, 64), isent, icame)
-    row_gains = [
-        remote(gains, gain_row.at[row], nsent.at[d - 1], ncame.at[d - 1], row=row_peer(row, d))
-        for d in range(1, 8)
-    ]
-    col_gains = [
-        remote(gain_sum.at[0], gain_col.at[col], nsent.at[6 + d], ncame.at[6 + d], col=(col + d) % 8)
-        for d in range(1, 8)
-    ]
-    core_gains = remote(gain_sum.at[1], gain_core, nsent.at[14], ncame.at[14], dp=1 - dp)
-
-    raw, qkv, new_rows = up.at[:, : 2 * head_width], act.at[:, : 3 * head_width], back
-    heads_change = gate.at[:, : 3 * head_width]
-    joined = hidden.at[:, : 3 * head_width]
-    get_rows = pltpu.make_async_copy(rows_in, rows, load.at[0])
-    get_reduce = pltpu.make_async_copy(reduce_in, reduce, load.at[1])
-
-    def get_expand(j):
-        at = span(j, 256)
-        return pltpu.make_async_copy(expand_in.at[:, at], expand.at[:, at], load.at[2 + j])
-
-    early = [
-        pltpu.make_async_copy(source, target, late.at[i])
-        for i, (source, target) in enumerate(
-            ((heads_in, heads), (merge_in, merge), (probs_in, probs), (mix_in, mix), (rates_in, rates))
-        )
-    ]
-    get_raw = pltpu.make_async_copy(raw_in, raw, late.at[5])
-    get_qkv = pltpu.make_async_copy(qkv_in, qkv, late.at[6])
-    get_xs = pltpu.make_async_copy(xs_in, rows, late.at[7])
-
-    def hand(i, source, target):
-        return remote(source, target, xsent.at[i], xcame.at[i], dp=1 - dp)
-
-    hand_act = hand(0, act_turned.at[span(1 - dp, half_units)], act_other)
-    hand_rows = hand(1, turned.at[span(1 - dp, half_width)], turned_other)
-    hand_back = hand(2, back, back_other)
-    hand_hidden = hand(3, hidden, hidden_other)
-    hand_mix = hand(4, mix_turned.at[span(1 - dp, half_heads)], mix_other)
-    hand_new = hand(5, back, back_other)
-    hand_xs = hand(6, turned.at[span(1 - dp, half_width)], turned_other)
-    hand_joined = hand(7, joined, joined_other)
-
-    def turn_rows(j):
-        values = rows[:, span(j, 256)].T
-        turned[span(j, 128), :] = values[:128]
-        turned[span(2 * tiles + j, 128), :] = values[128:]
-
-    def two(target, at, wide, own, own_at, right, other, right_other):
-        target[at, wide] = (
-            dot(own[own_at, :], right[:, wide]) + dot(other[at, :], right_other[:, wide])
-        ).astype(BF16)
-
-    get_rows.start()
-    for j in range(tiles):
-        get_expand(j).start()
-        get_expand(tiles + j).start()
-    get_reduce.start()
-    meet(rows=True, cols=True, core=True, spread_out=True)
-    get_rows.wait()
-
     @pl.loop(0, tiles)
     def _(j):
-        get_expand(j).wait()
-        get_expand(tiles + j).wait()
         at = span(j, 256)
         gate[:, at] = dot(rows[...], expand[:, at])
         up[:, at] = dot(rows[...], expand[:, span(tiles + j, 256)])
@@ -943,16 +903,16 @@
             x = gate[some, at]
             act[some, at] = (x * jax.nn.sigmoid(x) * up[some, at]).astype(BF16)
 
-    get_reduce.wait()
+    bring_reduce.wait()
 
     def reduced(j):
         at = span(j, 256)
         part[:, at] = dot(act[...], reduce[:, at]).astype(BF16)
 
     pl.loop(n, 2 * n)(reduced)
-    scatter[0].start_right()
+    scatter[1].start_right()
     pl.loop(0, n)(reduced)
-    scatter[0].start_left()
+    scatter[1].start_left()
 
     @pl.loop(0, tiles)
     def _(j):
@@ -960,19 +920,18 @@
         act_turned[at, :] = act[:, at].T
 
     hand_act.start()
-    for copy in early:
-        copy.start()
     get_qkv.start()
 
-    scatter[0].middle()
-    scatter[0].end()
+    spread_g.wait()
+    scatter[1].middle()
+    scatter[1].end()
     sums[...] = jnp.zeros_like(sums)
 
     @pl.loop(0, share // 16)
     def _(i):
         at = span(i, 16)
         grad = g[at].astype(F32)
-        hat, change = back_of(grad, scatter[0].total[at], gain_reduce[...])
+        hat, change = back_of(grad, scatter[1].total[at], gain_reduce[...])
         back[pl.ds(pl.multiple_of(row * share + i * 16, 16), 16), :] = change.astype(BF16)
         done[at] = (residual[at] + hat * gain_reduce[...]).astype(BF16)
         product = grad * hat
@@ -981,7 +940,7 @@
     gather.start()
     gains[...] = jnp.zeros_like(gains)
     gains[3:4] = jnp.sum(sums[...], axis=0, keepdims=True)
-    scatter[0].finish()
+    scatter[1].finish()
     gather.relay()
 
     pl.loop(0, 2 * tiles)(turn_rows)
@@ -1013,9 +972,9 @@
         part[:, at] = dot_flipped(hidden[...], expand[at, :]).astype(BF16)
 
     pl.loop(n, 2 * n)(branch)
-    scatter[1].start_right()
+    scatter[2].start_right()
     pl.loop(0, n)(branch)
-    scatter[1].start_left()
+    scatter[2].start_left()
 
     hand_act.wait()
     hand_back.wait()
@@ -1028,7 +987,7 @@
 
     pl.semaphore_signal(free.at[0], inc=1, device_id={"dp": 1 - dp}, device_id_type=MESH)
     reduce_sum.start()
-    scatter[1].middle()
+    scatter[2].middle()
     hand_rows.wait()
     hand_hidden.wait()
 
@@ -1040,13 +999,13 @@
     pl.semaphore_signal(free.at[1], inc=1, device_id={"dp": 1 - dp}, device_id_type=MESH)
     expand_sum.start()
     reduce_sum.over_z()
-    scatter[1].end()
+    scatter[2].end()
     sums[...] = jnp.zeros_like(sums)
 
     @pl.loop(0, share // 16)
     def _(i):
         at = span(i, 16)
-        grad = g[at].astype(F32) + scatter[1].total[at]
+        grad = g[at].astype(F32) + scatter[2].total[at]
         grad_resid[at] = grad
         hat, change = back_of(grad, merged[at], gain_merge[...])
         new_rows[pl.ds(pl.multiple_of(row * share + i * 16, 16), 16), :] = change.astype(BF16)
@@ -1061,14 +1020,12 @@
     hand_xs.start()
     last_gather.relay()
     last_gather.relay_again()
-    for copy in early:
-        copy.wait()
     get_raw.wait()
     get_qkv.wait()
     mix_turned[...] = mix[...].T
     hand_mix.start()
     expand_sum.over_z()
-    scatter[1].finish()
+    scatter[2].finish()
     last_gather.wait()
     pl.semaphore_wait(free.at[0], 1)
     hand_new.start()
@@ -1155,9 +1112,9 @@
         part[:, at] = dot_flipped(joined[...], heads[at, :]).astype(BF16)
 
     pl.loop(n, 2 * n)(input_part)
-    scatter[2].start_right()
+    scatter[3].start_right()
     pl.loop(0, n)(input_part)
-    scatter[2].start_left()
+    scatter[3].start_left()
 
     hand_xs.wait()
     hand_joined.wait()
@@ -1171,10 +1128,10 @@
     expand_sum.over_y()
     merge_sum.over_z()
     reduce_sum.end()
-    scatter[2].middle()
+    scatter[3].middle()
     heads_sum.over_z()
-    scatter[2].end()
-    final[...] = (grad_resid[...] + scatter[2].total[...]).astype(BF16)
+    scatter[3].end()
+    final[...] = (grad_resid[...] + scatter[3].total[...]).astype(BF16)
     spread_grad.start()
     for copy in col_gains:
         copy.wait()
@@ -1190,7 +1147,7 @@
     heads_sum.end()
     core_gains.wait()
     gains_grad[...] = gain_sum[1] + gain_core[...]
-    scatter[2].finish()
+    scatter[3].finish()
     spread.wait()
     spread_grad.wait()
     for grad in (reduce_sum, expand_sum, merge_sum, heads_sum):
@@ -1217,7 +1174,6 @@
     gains_first,
     gains_second,
 ):
-    row_at = lax.axis_index("row")
     col_width = block_input.shape[1]
     model_width = col_width * lax.axis_size("col")
     head_width = merge_weight.shape[0]
@@ -1225,77 +1181,12 @@
     seq_len = block_input.shape[0] * lax.axis_size("row") // lax.axis_size("col")
     share = seq_len // lax.axis_size("row")
     head_count = head_width // HD
-    doc_ids, places, live_rows = positions(doc_lengths[0], seq_len)
-    gain_query = lax.dynamic_slice_in_dim(norm_gains[0], row_at * head_width, head_width)
-    gain_key = lax.dynamic_slice_in_dim(norm_gains[1], row_at * head_width, head_width)
-    gain_merge, gain_reduce = norm_gains[2:3], norm_gains[3:4]
     rows_shape = struct((seq_len, model_width), BF16)
-    mine_f32 = struct((share, model_width), F32)
-    half_dim = HD // 2
-    frequency = THETA ** (-2.0 * jnp.arange(half_dim, dtype=F32) / HD)
-    angles = places.astype(F32)[:, None] * frequency[None, :]
-    cosine, sine = jnp.cos(angles), jnp.sin(angles)
-    cosine = jnp.concatenate([cosine, cosine], axis=1)
-    sine = jnp.concatenate([-sine, sine], axis=1)
-    docs = jnp.broadcast_to(doc_ids.astype(F32)[:, None], (seq_len, 128))
-    doc_row = jnp.broadcast_to(doc_ids.astype(F32)[None, :], (8, seq_len))
     blocks = seq_len // QUERY_BLOCK
 
-    (
-        input_rows, cot_share, heads_low, merge_low, expand_low, reduce_low, raw, qkv, probs, mixture_low, rates,
-        merged, residual, residual_rows,
-    ) = call(
-        attend_kernel, "attend", 1,
-        [
-            rows_shape,
-            struct((share, model_width), BF16),
-            struct((model_width, 3 * head_width), BF16),
-            struct((head_width, model_width), BF16),
-            struct((model_width, 2 * unit_width), BF16),
-            struct((unit_width, model_width), BF16),
-            struct((seq_len, 2 * head_width), F32),
-            struct((seq_len, 3 * head_width), BF16),
-            struct((head_count, blocks, QUERY_BLOCK, WINDOW + QUERY_BLOCK), BF16),
-            struct((seq_len, head_width), BF16),
-            struct((seq_len, 128), F32),
-            mine_f32,
-            mine_f32,
-            rows_shape,
-        ],
-        [
-            block_input, cotangent, heads_weight, merge_weight, expand_weight, reduce_weight, cosine, sine, docs,
-            doc_row, gain_query[None], gain_key[None], gain_merge,
-        ],
-        [ANY] * 6 + [VMEM] * 7,
-        [ANY] * 11 + [VMEM] * 2 + [ANY],
-        [
-            pltpu.VMEM((seq_len, model_width), BF16),
-            pltpu.VMEM(heads_weight.shape, F32),
-            pltpu.VMEM(merge_weight.shape, F32),
-            pltpu.VMEM(expand_weight.shape, F32),
-            pltpu.VMEM(reduce_weight.shape, F32),
-            pltpu.VMEM(heads_weight.shape, BF16),
-            pltpu.VMEM(merge_weight.shape, BF16),
-            pltpu.VMEM(expand_weight.shape, BF16),
-            pltpu.VMEM(reduce_weight.shape, BF16),
-            pltpu.VMEM((model_width, 3 * head_width), BF16),
-            pltpu.VMEM((head_width, model_width), BF16),
-            pltpu.VMEM((seq_len, 2 * head_width), F32),
-            pltpu.VMEM((seq_len, 3 * head_width), BF16),
-            pltpu.VMEM((head_count, blocks, QUERY_BLOCK, WINDOW + QUERY_BLOCK), BF16),
-            pltpu.VMEM((seq_len, head_width), BF16),
-            pltpu.VMEM((seq_len, 128), F32),
-            pltpu.VMEM((seq_len, model_width), BF16),
-            pltpu.VMEM((seq_len, model_width), BF16),
-            DMA((4,)), DMA((9,)), DMA((8,)), DMA((8,)), DMA((8,)), DMA((8,)),
-        ]
-        + gather_scratch() + gather_scratch()
-        + scatter_scratch(share, model_width) + sums_scratch(seq_len)
-        + bring_scratch() + bring_scratch() + bring_scratch() + bring_scratch(),
-    )
     gain_shape = (4, model_width)
     block_output, input_grad, gains_grad, heads_grad, merge_grad, expand_grad, reduce_grad = call(
-        rest_kernel, "rest", 2,
+        layer_kernel, "layer", 1,
         [
             struct(block_input.shape, BF16),
             struct(block_input.shape, BF16),
@@ -1304,13 +1195,15 @@
             struct(merge_weight.shape, BF16),
             struct(expand_weight.shape, BF16),
             struct(reduce_weight.shape, BF16),
+            rows_shape,
+            struct((seq_len, 2 * head_width), F32),
+            struct((seq_len, 3 * head_width), BF16),
         ],
         [
-            residual_rows, expand_low, reduce_low, heads_low, merge_low, input_rows, raw, qkv, probs, mixture_low, rates,
-            residual, cot_share, merged, cosine, sine, docs, gain_query[None], gain_key[None], gain_merge, gain_reduce,
+            block_input, cotangent, heads_weight, merge_weight, expand_weight, reduce_weight, doc_lengths, norm_gains,
         ],
-        [ANY] * 11 + [VMEM] * 10,
-        [ANY] * 2 + [VMEM] + [ANY] * 4,
+        [ANY] * 6 + [pl.BlockSpec(memory_space=pltpu.SMEM), VMEM],
+        [ANY] * 2 + [VMEM] + [ANY] * 7,
         [
             pltpu.VMEM((seq_len, model_width), BF16),
             pltpu.VMEM((model_width, seq_len), BF16),
@@ -1334,6 +1227,9 @@
             pltpu.VMEM((share, model_width), BF16),
             pltpu.VMEM((share, model_width), BF16),
             pltpu.VMEM((share, model_width), F32),
+            pltpu.VMEM((share, model_width), F32),
+            pltpu.VMEM((share, model_width), F32),
+            pltpu.VMEM((share, model_width), BF16),
             pltpu.VMEM((8, model_width), F32),
             pltpu.VMEM((seq_len, 256), F32),
             pltpu.VMEM(gain_shape, F32),
@@ -1347,15 +1243,21 @@
             pltpu.VMEM((seq_len, model_width), BF16),
             pltpu.VMEM((head_width // 2, seq_len), BF16),
             pltpu.VMEM((seq_len, 3 * head_width), BF16),
+            pltpu.VMEM((seq_len, HD), F32),
+            pltpu.VMEM((8, seq_len), F32),
+            pltpu.VMEM((seq_len, HD), F32),
+            pltpu.VMEM((seq_len, HD), F32),
             pltpu.SemaphoreType.REGULAR((2,)),
-            DMA((10,)), DMA((8,)), DMA((8,)), DMA((8,)), DMA((8,)), DMA((8,)), DMA((15,)), DMA((15,)), DMA((8,)), DMA((8,)),
+            DMA((8,)), DMA((3,)), DMA((3,)), DMA((8,)), DMA((8,)), DMA((8,)), DMA((8,)), DMA((15,)), DMA((15,)),
+            DMA((8,)), DMA((8,)), DMA((8,)), DMA((8,)), DMA((8,)), DMA((8,)),
         ]
-        + gather_scratch() + gather_scratch()
-        + scatter_scratch(share, model_width) + [DMA((14,))] * 4
-        + sums_scratch(seq_len)
+        + gather_scratch() * 4
+        + scatter_scratch(share, model_width) + [DMA((14,))] * 6
+        + sums_scratch(seq_len) * 2
         + grad_sum_scratch(reduce_weight.shape) + grad_sum_scratch(expand_weight.shape)
-        + grad_sum_scratch(merge_weight.shape) + grad_sum_scratch(heads_weight.shape),
-    )
+        + grad_sum_scratch(merge_weight.shape) + grad_sum_scratch(heads_weight.shape)
+        + bring_scratch() * 4,
+    )[:7]
     heads_grad, merge_grad, expand_grad, reduce_grad = (
         heads_grad.astype(F32), merge_grad.astype(F32), expand_grad.astype(F32), reduce_grad.astype(F32)
     )

time: 296 us -> 271 us (0.916)
  Pallas kernels: 263 us -> 249 us
  local copies, waits for them, and re-layouts: 8.27 us -> 1.78 us
  other arithmetic: 18.2 us -> 15 us
    pallas_call x2 -> x1, Pallas kernels: 263 us -> 249 us  [call(): pl.pallas_call(kernel, name=name, out_shape=outs, in_specs=in_specs, out_...]
    convert_element_type x1, other arithmetic: 4.62 us -> 7.91 us  [on_device(): expand_fresh.astype(jnp.bfloat16)]
where the time goes in v6:
time: 271 us; the launch traced here: 267 us
  Pallas kernels  249 us (92%)
  other arithmetic  15 us (6%)
    pallas_call x1, Pallas kernels, call(): pl.pallas_call(kernel, name=name, out_shape=outs, in_specs=in_specs, out_...  249 us
    convert_element_type x1, other arithmetic, on_device(): expand_fresh.astype(jnp.bfloat16)  7.91 us

profile of v6, /device:TPU:9, one launch (start us, length us, event | category | flops | bytes accessed | tf_op | source)
XLA Modules:
  0.0 266.7 jit_solution(6095029741440046891)
XLA Ops:
  0.7 249.1 %layer.1 = (bf16[512,256]{1,0:T(8,128)(2,1)}, bf16[512,256]{1,0:T(8,128)(2,1)}, f32[4,2048]{1,0:T(4,128)}, bf16[256,768]{1,0:T(8,128)(2,1)}, bf16[256,256]{1,0:T...) custom-call(bf16[512,256]{1,0:T(8,128)(2,1)} %x.1, ...), custom_call_target="tpu_custom_call" | custom-call | tf_op jit(solution)/shard_map/layer/pallas_call | solution.py:176
  249.8 0.0 copy-start
  249.8 0.0 copy-start.3
  249.8 0.0 copy-start.4
  249.8 0.0 copy-start.7
  249.8 7.9 %fusion.8 = (bf16[256,2048]{1,0:T(8,128)(2,1)}, f32[256,2048]{1,0:T(8,128)}, f32[256,2048]{1,0:T(8,128)}, f32[256,2048]{1,0:T(8,128)}, f32[256,2048]{1,0:T(8,128)}) fusion(f32[256,2048]{1,0:T(8,128)} %expand_in.1, f32[256,2048]{1,0:T(8,128)} %param.29, f32[256,2048]{1,0:T(8,128)} %param.28, bf16[256,2048]{1,0:T(8,128)(2,1)} %get-tuple-element.37), kind=kLoop, calls=%fused_computation.21 | loop fusion | flops 8388608 | bytes 16777216 | tf_op jit(solution)/shard_map/convert_element_type | solution.py:1296
  257.7 0.0 copy-done
  257.7 0.0 copy-done.3
  257.7 0.0 copy-done.4
  257.7 0.0 copy-start.1
  257.8 0.0 copy-start.5
  257.8 0.0 copy-start.6
  257.8 0.0 copy-start.8
  257.8 2.5 fusion.6
  260.3 0.0 copy-done.1
  260.3 0.0 copy-done.6
  260.3 0.4 copy-done.8
  260.7 2.0 fusion.12
  262.8 1.1 fusion.10
  263.8 0.0 copy-done.15
  263.8 0.7 multiply_subtract_fusion.4
  264.5 0.8 convert_element_type.27
  265.4 0.7 copy.46
  266.1 0.6 copy.47
  (21 shorter events, 0.0 us)
Async XLA Ops:
  249.8 8.0 %copy-start = (f32[1024,256]{1,0:T(8,128)S(1)}, f32[1024,256]{1,0:T(8,128)}, u32[]{:S(2)}) copy-start(f32[1024,256]{1,0:T(8,128)} %reduce_in.1) | copy-start | bytes 3145732
  249.8 7.9 %copy-start.3 = (f32[1024,256]{1,0:T(8,128)S(1)}, f32[1024,256]{1,0:T(8,128)}, u32[]{:S(2)}) copy-start(f32[1024,256]{1,0:T(8,128)} %param.32) | copy-start | bytes 3145732
  249.8 7.9 %copy-start.4 = (f32[1024,256]{1,0:T(8,128)S(1)}, f32[1024,256]{1,0:T(8,128)}, u32[]{:S(2)}) copy-start(f32[1024,256]{1,0:T(8,128)} %param.31) | copy-start | bytes 3145732
  249.8 7.9 %copy-start.7 = (bf16[1024,256]{1,0:T(8,128)(2,1)S(1)}, bf16[1024,256]{1,0:T(8,128)(2,1)}, u32[]{:S(2)}) copy-start(bf16[1024,256]{1,0:T(8,128)(2,1)} %get-tuple-element.38) | copy-start | bytes 1572868
  257.7 2.6 copy-start.1
  257.8 2.5 copy-start.5
  257.8 2.5 copy-start.6
  257.8 2.9 %copy-start.8 = (bf16[256,768]{1,0:T(8,128)(2,1)S(1)}, bf16[256,768]{1,0:T(8,128)(2,1)}, u32[]{:S(2)}) copy-start(bf16[256,768]{1,0:T(8,128)(2,1)} %get-tuple-element.35) | copy-start | bytes 1179652
  260.7 2.0 copy-start.2
  260.7 2.0 copy-start.11
  260.7 2.0 copy-start.12
  260.7 2.1 copy-start.14
  262.7 1.1 copy-start.13
  262.7 1.1 copy-start.15
  262.7 1.1 copy-start.16
  262.7 1.1 copy-start.17
  262.7 1.8 copy-start.9
  262.7 2.6 copy-start.10

commit v7 on v6

--- a/solution.py
+++ b/solution.py
@@ -22,6 +22,7 @@
 ADAM_EPS = 1e-08
 
 BF16 = jnp.bfloat16
+SCATTER_LEFT, GATHER_LEFT, INPUT_LEFT = 8, 9, 16
 F32 = jnp.float32
 MESH = pl.DeviceIdType.MESH
 ANY = pl.BlockSpec(memory_space=pl.ANY)
@@ -207,11 +208,13 @@
 
 
 class Scatter:
-    def __init__(self, part, total, from_y, from_x, last_y, last_x, stage, sent, arrived):
+    def __init__(self, part, total, from_y, from_x, last_y, last_x, stage_y, stage_x, sent, arrived):
         dp, row, col = here()
         self.row, self.part, self.total = row, part, total
-        self.from_y, self.from_x, self.last_y, self.last_x, self.stage = from_y, from_x, last_y, last_x, stage
-        self.count, self.half = total.shape[0], total.shape[1] // 2
+        self.from_y, self.from_x, self.last_y, self.last_x = from_y, from_x, last_y, last_x
+        self.stage_y, self.stage_x = stage_y, stage_x
+        self.count, self.left = total.shape[0], from_x.shape[3]
+        self.sides = (pl.ds(0, self.left), pl.ds(self.left, total.shape[1] - self.left))
         number = iter(range(14))
 
         def copy(source, target, dx, dy):
@@ -224,13 +227,11 @@
             for dy in (1, 0)
             for dx in (1, 3, 2)
         }
-        self.x_last = {dx: copy(stage.at[dx], last_x.at[dx - 1], dx, 0) for dx in (1, 3, 2)}
-        self.y_last = copy(stage.at[0], last_y, 0, 1)
+        self.x_last = {dx: copy(stage_x.at[dx - 1], last_x.at[dx - 1], dx, 0) for dx in (1, 3, 2)}
+        self.y_last = copy(stage_y, last_y, 0, 1)
 
     def block(self, dx, dy, side):
-        return self.part.at[
-            span(near_row(self.row, dx, dy), self.count), pl.ds(side * self.half, self.half)
-        ]
+        return self.part.at[span(near_row(self.row, dx, dy), self.count), self.sides[side]]
 
     def start_right(self):
         for copy in self.y_first.values():
@@ -251,7 +252,7 @@
             own = self.block(dx, 0, 1)
 
             def add(at):
-                self.stage[dx, at] = (own[at].astype(F32) + self.from_y[dx, at].astype(F32)).astype(BF16)
+                self.stage_x[dx - 1, at] = (own[at].astype(F32) + self.from_y[dx, at].astype(F32)).astype(BF16)
 
             self.chunks(add)
             self.x_last[dx].start()
@@ -263,7 +264,7 @@
             total = other[at].astype(F32)
             for k in range(3):
                 total = total + self.from_x[1, k, at].astype(F32)
-            self.stage[0, at] = total.astype(BF16)
+            self.stage_y[at] = total.astype(BF16)
 
         self.chunks(add)
         self.y_last.start()
@@ -280,11 +281,11 @@
             total = left[at].astype(F32) + self.last_y[at].astype(F32)
             for k in range(3):
                 total = total + self.from_x[0, k, at].astype(F32)
-            self.total[at, : self.half] = total
+            self.total[at, self.sides[0]] = total
             total = right[at].astype(F32) + self.from_y[0, at].astype(F32)
             for k in range(3):
                 total = total + self.last_x[k, at].astype(F32)
-            self.total[at, self.half :] = total
+            self.total[at, self.sides[1]] = total
 
         self.chunks(add)
 
@@ -296,14 +297,16 @@
 
 
 def scatter_scratch(share, width):
-    half = width // 2
+    left = SCATTER_LEFT * width // 16
+    right = width - left
     return [
         pltpu.VMEM((share, width), F32),
-        pltpu.VMEM((4, share, half), BF16),
-        pltpu.VMEM((2, 3, share, half), BF16),
-        pltpu.VMEM((share, half), BF16),
-        pltpu.VMEM((3, share, half), BF16),
-        pltpu.VMEM((4, share, half), BF16),
+        pltpu.VMEM((4, share, right), BF16),
+        pltpu.VMEM((2, 3, share, left), BF16),
+        pltpu.VMEM((share, left), BF16),
+        pltpu.VMEM((3, share, right), BF16),
+        pltpu.VMEM((share, left), BF16),
+        pltpu.VMEM((3, share, right), BF16),
         DMA((14,)),
         DMA((14,)),
     ]
@@ -324,19 +327,20 @@
             return remote(ref, ref, sent.at[i], arrived.at[i], row=near_row(row, dx, dy))
 
         part = share // 2
+        steps = (1, 3, 2)
+        two = steps[:2]
         self.y_left = copy(0, 0, 0, 0, 1)
-        self.x_left = [copy(0, 0, 0, dx, 0) for dx in (1, 3)]
-        self.x_other = [copy(0, 1, 0, dx, 0) for dx in (1, 3)]
-        steps = list(enumerate((1, 3)))
-        self.on_left = [copy(4 - dx, 0, 0, dx, 0, i * part, part) for i, dx in steps]
-        self.on_other = [copy(4 - dx, 1, 0, dx, 0, i * part, part) for i, dx in steps]
-        self.y_right, self.x_right, self.on_right, self.y_near, self.y_far = [], [], [], [], []
+        self.x_left = [copy(0, 0, 0, dx, 0) for dx in two]
+        self.on_left = [copy(4 - dx, 0, 0, dx, 0, i * part, part) for i, dx in enumerate(two)]
+        self.y_right, self.x_right, self.y_near, self.on_other = [], [], [], []
         if right:
+            self.x_other = [copy(0, 1, 0, dx, 0) for dx in steps]
             self.y_right = [copy(0, 0, 1, 0, 1)]
-            self.x_right = [copy(0, 0, 1, dx, 0) for dx in (1, 3)]
-            self.on_right = [copy(4 - dx, 0, 1, dx, 0, i * part, part) for i, dx in steps]
-            self.y_near = [copy(4 - dx, 0, 1, 0, 1) for dx in (1, 3)]
-            self.y_far = [copy(2, 0, 1, 0, 1, i * part, part) for i in range(2)]
+            self.x_right = [copy(0, 0, 1, dx, 0) for dx in steps]
+            self.y_near = [copy(4 - dx, 0, 1, 0, 1) for dx in steps]
+        else:
+            self.x_other = [copy(0, 1, 0, dx, 0) for dx in two]
+            self.on_other = [copy(4 - dx, 1, 0, dx, 0, i * part, part) for i, dx in enumerate(two)]
 
     def start(self):
         for copy in (self.y_left, *self.x_right, *self.y_right, *self.x_left):
@@ -348,25 +352,21 @@
             copy.start()
         for i, came in enumerate(self.x_right):
             came.wait_recv()
-            self.on_right[i].start()
             self.y_near[i].start()
 
     def relay_again(self):
         for i in range(2):
             self.x_left[i].wait_recv()
             self.on_left[i].start()
-        for i, came in enumerate(self.on_right):
-            came.wait_recv()
-            self.y_far[i].start()
-        for i in range(2):
+        for i, copy in enumerate(self.on_other):
             self.x_other[i].wait_recv()
-            self.on_other[i].start()
+            copy.start()
 
     def wait(self):
-        for copy in (*self.y_right, *self.on_left, *self.on_other, *self.y_near, *self.y_far):
+        for copy in (*self.y_right, *self.x_other[len(self.on_other) :], *self.on_left, *self.on_other, *self.y_near):
             copy.wait_recv()
         for copy in (self.y_left, *self.x_left, *self.x_other, *self.on_left, *self.on_other, *self.y_right,
-                     *self.x_right, *self.on_right, *self.y_near, *self.y_far):
+                     *self.x_right, *self.y_near):
             copy.wait_send()
 
 
@@ -652,41 +652,119 @@
     return start, (b + 1) * QUERY_BLOCK - start
 
 
+UPDATE_STEPS = 4
+
+
+def update_kernel(*refs):
+    ins, outs = refs[:22], refs[22:]
+    outs[0][...] = ins[0][...]
+    outs[1][...] = ins[1][...].astype(F32)
+    for i in range(4):
+        gradient, weight, first_mom, second_mom = (ref[...] for ref in ins[2 + 4 * i : 6 + 4 * i])
+        gradient = gradient.astype(F32)
+        mean, square, fresh = adamw(weight, gradient, first_mom, second_mom, LR, DECAY)
+        for ref, value in zip(outs[2 + 5 * i : 7 + 5 * i], (gradient, mean, square, fresh, fresh), strict=True):
+            ref[...] = value.astype(ref.dtype)
+
+    @pl.when(pl.program_id(0) == 0)
+    def _():
+        gradient, weight, first_mom, second_mom = (ref[...] for ref in ins[18:])
+        mean, square, fresh = adamw(weight, gradient, first_mom, second_mom, LR_GAIN, 0.0)
+        for ref, value in zip(outs[22:], (gradient, mean, square, fresh), strict=True):
+            ref[...] = value
+
+
+def update(block_output, input_grad, *groups):
+    def part(shape):
+        return pl.BlockSpec((shape[0] // UPDATE_STEPS, shape[1]), lambda i: (i, 0))
+
+    ins, outs, in_specs, out_specs = [block_output, input_grad], [], [], []
+    outs += [struct(block_output.shape, BF16), struct(input_grad.shape, F32)]
+    in_specs += [part(block_output.shape)] * 2
+    out_specs += [part(block_output.shape)] * 2
+    for group in groups[:4]:
+        shape = group[0].shape
+        ins += group
+        in_specs += [part(shape)] * 4
+        outs += [struct(shape, F32)] * 4 + [struct(shape, BF16)]
+        out_specs += [part(shape)] * 5
+    whole = pl.BlockSpec(groups[4][0].shape, lambda i: (0, 0))
+    ins += groups[4]
+    in_specs += [whole] * 4
+    outs += [struct(groups[4][0].shape, F32)] * 4
+    out_specs += [whole] * 4
+    return tuple(
+        pl.pallas_call(
+            update_kernel,
+            name="update",
+            grid=(UPDATE_STEPS,),
+            out_shape=outs,
+            in_specs=in_specs,
+            out_specs=out_specs,
+            compiler_params=pltpu.CompilerParams(vmem_limit_bytes=62 * 2**20),
+        )(*ins)
+    )
+
+
 def layer_kernel(
     x, g_in, heads_in, merge_in, expand_in, reduce_in, lengths, gain_all,
     out, input_grad, gains_grad, heads_grad, merge_grad, expand_grad, reduce_grad, xs_keep, raw_keep, qkv_keep,
     rows, turned, expand, reduce, heads, merge, gate, up, act, act_turned, part, back, hidden, probs, mix, mix_turned,
     rates, stats, grad_mix, done, final, grad_resid, merged, residual, g, sums, grad_gate,
     gains, gain_row, gain_col, gain_core, gain_sum, act_other, turned_other, hidden_other, back_other, mix_other,
-    joined_other, docs, doc_row, cosine, sine, free, load, keep, late, osent, ocame, isent, icame, nsent, ncame, xsent, xcame,
-    asent, acame, bsent, bcame, g1sent, g1came, g2sent, g2came, g3sent, g3came, g4sent, g4came, *refs,
+    joined_other, values_part, docs, doc_row, cosine, sine, free, load, keep, late, osent, ocame, isent, icame, nsent, ncame, xsent, xcame,
+    asent, acame, bsent, bcame, g1sent, g1came, g2sent, g2came, g3sent, g3came, g4sent, g4came, g5sent, g5came, g6sent, g6came, *refs,
 ):
     dp, row, col = here()
     share, width = residual.shape
     tokens, units = act.shape
     head_width = mix.shape[1]
     tiles = units // 256
-    n = width // 512
+    n, first_right = width // 512, SCATTER_LEFT * width // 16 // 256
     gain_query, gain_key = (gain_all.at[i : i + 1, span(row, head_width)] for i in range(2))
     gain_merge, gain_reduce = (gain_all.at[i : i + 1] for i in range(2, 4))
-    scatter = [Scatter(part, *refs[:6], *refs[6 + 2 * i : 8 + 2 * i]) for i in range(4)]
-    first_sums = TokenSums(rates, *refs[14:18])
-    token_sums = TokenSums(stats, *refs[18:22])
+    batch, half_share = tokens // 2, share // 2
+
+    def scatter_of(i, m=None):
+        sems = refs[7 + 2 * i : 9 + 2 * i]
+        if m is None:
+            return Scatter(part, *refs[:7], *sems)
+        at = pl.ds(m * half_share, half_share)
+        total, from_y, from_x, last_y, last_x, stage_y, stage_x = refs[:7]
+        return Scatter(
+            part.at[pl.ds(m * batch, batch)], total.at[at], from_y.at[:, at], from_x.at[:, :, at], last_y.at[at],
+            last_x.at[:, at], stage_y.at[at], stage_x.at[:, at], *sems,
+        )
+
+    merge_scatter, input_scatter = scatter_of(0), scatter_of(5)
+    reduced_scatter = [scatter_of(1 + m, m) for m in range(2)]
+    branch_scatter = [scatter_of(3 + m, m) for m in range(2)]
+    first_sums = TokenSums(rates, *refs[19:23])
+    token_sums = TokenSums(stats, *refs[23:27])
     half_units, half_width, half_heads = units // 2, width // 2, head_width // 2
     reduce_part, merge_part_ref = reduce.at[pl.ds(0, half_units)], merge.at[pl.ds(0, half_heads)]
     expand_part, heads_part = expand.at[pl.ds(0, half_width)], heads.at[pl.ds(0, half_width)]
-    reduce_sum = GradSum("wide", reduce_part, reduce_grad, *refs[22:27])
-    expand_sum = GradSum("tall", expand_part, expand_grad, *refs[27:32])
-    merge_sum = GradSum("wide", merge_part_ref, merge_grad, *refs[32:37])
-    heads_sum = GradSum("tall", heads_part, heads_grad, *refs[37:42])
-    bring_heads = Bring("tall", heads_in.shape, heads, *refs[42:44])
-    bring_merge = Bring("wide", merge_in.shape, merge, *refs[44:46])
-    bring_reduce = Bring("wide", reduce_in.shape, reduce, *refs[46:48])
-    bring_expand = Bring("tall", expand_in.shape, expand, *refs[48:50])
-    gather_x = Gather(back, share, width, g1sent, g1came)
-    row_gather = Gather(rows, share, width // 2, g2sent, g2came)
-    gather = Gather(back, share, width // 2, g3sent, g3came)
-    last_gather = Gather(back, share, width // 2, g4sent, g4came)
+    reduce_sum = GradSum("wide", reduce_part, reduce_grad, *refs[27:32])
+    expand_sum = GradSum("tall", expand_part, expand_grad, *refs[32:37])
+    merge_sum = GradSum("wide", merge_part_ref, merge_grad, *refs[37:42])
+    values_at, others_at = pl.ds(2 * head_width, head_width), pl.ds(0, 2 * head_width)
+    values_sum = GradSum("tall", values_part, heads_grad.at[:, values_at], *refs[42:47])
+    heads_sum = GradSum("tall", heads_part.at[:, others_at], heads_grad.at[:, others_at], *refs[47:52])
+    bring_heads = Bring("tall", heads_in.shape, heads, *refs[52:54])
+    bring_merge = Bring("wide", merge_in.shape, merge, *refs[54:56])
+    bring_reduce = Bring("wide", reduce_in.shape, reduce, *refs[56:58])
+    bring_expand = Bring("tall", expand_in.shape, expand, *refs[58:60])
+    gather_x = Gather(back, share, INPUT_LEFT * width // 16, g1sent, g1came)
+    left = GATHER_LEFT * width // 16
+    row_gather = [
+        Gather(rows.at[pl.ds(m * batch, batch)], half_share, left, *sems)
+        for m, sems in enumerate(((g2sent, g2came), (g3sent, g3came)))
+    ]
+    gather = [
+        Gather(back.at[pl.ds(m * batch, batch)], half_share, left, *sems)
+        for m, sems in enumerate(((g4sent, g4came), (g5sent, g5came)))
+    ]
+    last_gather = Gather(back, share, left, g6sent, g6came)
     spread_x = SpreadIn(
         lambda k: rows_of(x, k, share), lambda k, c: back.at[span(k, share), span(c, 256)], asent, acame
     )
@@ -747,7 +825,8 @@
     hand_mix = hand(4, mix_turned.at[span(1 - dp, half_heads)], mix_other)
     hand_new = hand(5, back, back_other)
     hand_xs = hand(6, turned.at[span(1 - dp, half_width)], turned_other)
-    hand_joined = hand(7, joined, joined_other)
+    hand_joined = hand(7, joined.at[:, others_at], joined_other.at[:, others_at])
+    hand_values = hand(8, joined.at[:, values_at], joined_other.at[:, values_at])
 
     def turn_rows(j):
         values = rows[:, span(j, 256)].T
@@ -815,6 +894,8 @@
     first_sums.start()
     qkv[:, 2 * head_width :] = dot(back[...], heads[:, 2 * head_width :]).astype(BF16)
     bring_merge.hand_over()
+    bring_expand.relay()
+    bring_reduce.relay()
     first_sums.end()
     spread_g.start()
 
@@ -852,67 +933,132 @@
                 probs[h, b, :, count:] = jnp.zeros((QUERY_BLOCK, probs.shape[3] - count), BF16)
             mix[query_at, h * HD : (h + 1) * HD] = (dot(shares, qkv[key_at, value]) * live).astype(BF16)
 
-    bring_expand.relay()
-    bring_reduce.relay()
     bring_merge.wait()
 
     def merge_part(j):
         at = span(j, 256)
         part[:, at] = dot(mix[...], merge[:, at]).astype(BF16)
 
-    pl.loop(n, 2 * n)(merge_part)
-    scatter[0].start_right()
-    pl.loop(0, n)(merge_part)
-    scatter[0].start_left()
+    pl.loop(first_right, 2 * n)(merge_part)
+    merge_scatter.start_right()
+    pl.loop(0, first_right)(merge_part)
+    merge_scatter.start_left()
     bring_expand.relay_own()
     bring_reduce.relay_own()
-    scatter[0].middle()
+    merge_scatter.middle()
     bring_expand.relay_near()
     bring_reduce.relay_near()
-    scatter[0].end()
+    merge_scatter.end()
+
+    def place(i):
+        per = half_share // 16
+        return pl.ds(pl.multiple_of(i // per * batch + row * half_share + i % per * 16, 16), 16)
 
     @pl.loop(0, share // 16)
     def _(i):
         at = span(i, 16)
-        total = scatter[0].total[at]
+        total = merge_scatter.total[at]
         merged[at] = total
         mine = pl.ds(pl.multiple_of(row * share + i * 16, 16), 16)
         result = back[mine, :].astype(F32) + total * mean_rate(total) * gain_merge[...]
         residual[at] = result
-        rows[mine, :] = result.astype(BF16)
-
-    row_gather.start()
-    row_gather.relay()
+        rows[place(i), :] = result.astype(BF16)
+
+    row_gather[0].start()
+    row_gather[0].relay()
+    row_gather[1].start()
     bring_expand.hand_over()
-    row_gather.relay_again()
+    row_gather[0].relay_again()
+    row_gather[1].relay()
     bring_reduce.hand_over()
-    row_gather.wait()
-    scatter[0].finish()
+    row_gather[0].wait()
+    row_gather[1].relay_again()
+    merge_scatter.finish()
     bring_expand.wait()
     for copy in puts:
         copy.wait()
-    @pl.loop(0, tiles)
-    def _(j):
-        at = span(j, 256)
-        gate[:, at] = dot(rows[...], expand[:, at])
-        up[:, at] = dot(rows[...], expand[:, span(tiles + j, 256)])
-
-        @pl.loop(0, tokens // 64)
+
+    def rows_in(m):
+        return pl.ds(m * batch, batch)
+
+    def gated(m):
+        mine = rows_in(m)
+
+        @pl.loop(0, tiles)
+        def _(j):
+            at = span(j, 256)
+            gate[mine, at] = dot(rows[mine, :], expand[:, at])
+            up[mine, at] = dot(rows[mine, :], expand[:, span(tiles + j, 256)])
+
+            @pl.loop(m * (batch // 64), (m + 1) * (batch // 64))
+            def _(i):
+                some = span(i, 64)
+                x = gate[some, at]
+                act[some, at] = (x * jax.nn.sigmoid(x) * up[some, at]).astype(BF16)
+
+    def reduced(m):
+        mine = rows_in(m)
+
+        def product(j):
+            at = span(j, 256)
+            part[mine, at] = dot(act[mine, :], reduce[:, at]).astype(BF16)
+
+        pl.loop(first_right, 2 * n)(product)
+        reduced_scatter[m].start_right()
+        pl.loop(0, first_right)(product)
+        reduced_scatter[m].start_left()
+
+    def output_norm(m):
+        @pl.loop(m * (half_share // 16), (m + 1) * (half_share // 16))
         def _(i):
-            some = span(i, 64)
-            x = gate[some, at]
-            act[some, at] = (x * jax.nn.sigmoid(x) * up[some, at]).astype(BF16)
-
+            at = span(i, 16)
+            grad = g[at].astype(F32)
+            hat, change = back_of(grad, merge_scatter.total[at], gain_reduce[...])
+            back[place(i), :] = change.astype(BF16)
+            done[at] = (residual[at] + hat * gain_reduce[...]).astype(BF16)
+            product = grad * hat
+            sums[...] += product[:8] + product[8:]
+
+    def activity_gradient(m):
+        mine = rows_in(m)
+
+        @pl.loop(0, tiles)
+        def _(j):
+            at, up_at = span(j, 256), span(tiles + j, 256)
+            grad_gate[mine, :] = dot_flipped(back[mine, :], reduce[at, :])
+
+            @pl.loop(m * (batch // 64), (m + 1) * (batch // 64))
+            def _(i):
+                some = span(i, 64)
+                x, change = gate[some, at], grad_gate[some]
+                s = jax.nn.sigmoid(x)
+                hidden[some, at] = (change * up[some, at] * s * (1.0 + x * (1.0 - s))).astype(BF16)
+                hidden[some, up_at] = (change * (x * s)).astype(BF16)
+
+    def branch(m):
+        mine = rows_in(m)
+
+        def product(j):
+            at = span(j, 256)
+            part[mine, at] = dot_flipped(hidden[mine, :], expand[at, :]).astype(BF16)
+
+        pl.loop(first_right, 2 * n)(product)
+        branch_scatter[m].start_right()
+        pl.loop(0, first_right)(product)
+        branch_scatter[m].start_left()
+
+    gated(0)
     bring_reduce.wait()
-
-    def reduced(j):
-        at = span(j, 256)
-        part[:, at] = dot(act[...], reduce[:, at]).astype(BF16)
-
-    pl.loop(n, 2 * n)(reduced)
-    scatter[1].start_right()
-    pl.loop(0, n)(reduced)
-    scatter[1].start_left()
+    reduced(0)
+    row_gather[1].wait()
+    gated(1)
+    reduced_scatter[0].middle()
+    reduced(1)
+    spread_g.wait()
+    sums[...] = jnp.zeros_like(sums)
+    reduced_scatter[0].end()
+    output_norm(0)
+    gather[0].start()
 
     @pl.loop(0, tiles)
     def _(j):
@@ -921,61 +1067,32 @@
 
     hand_act.start()
     get_qkv.start()
-
-    spread_g.wait()
-    scatter[1].middle()
-    scatter[1].end()
-    sums[...] = jnp.zeros_like(sums)
-
-    @pl.loop(0, share // 16)
-    def _(i):
-        at = span(i, 16)
-        grad = g[at].astype(F32)
-        hat, change = back_of(grad, scatter[1].total[at], gain_reduce[...])
-        back[pl.ds(pl.multiple_of(row * share + i * 16, 16), 16), :] = change.astype(BF16)
-        done[at] = (residual[at] + hat * gain_reduce[...]).astype(BF16)
-        product = grad * hat
-        sums[...] += product[:8] + product[8:]
-
-    gather.start()
+    reduced_scatter[1].middle()
+    gather[0].relay()
+    reduced_scatter[1].end()
+    output_norm(1)
+    gather[1].start()
+    gather[0].relay_again()
     gains[...] = jnp.zeros_like(gains)
     gains[3:4] = jnp.sum(sums[...], axis=0, keepdims=True)
-    scatter[1].finish()
-    gather.relay()
-
+    for m in range(2):
+        reduced_scatter[m].finish()
     pl.loop(0, 2 * tiles)(turn_rows)
     hand_rows.start()
     get_xs.start()
-    gather.relay_again()
-    gather.wait()
+    gather[0].wait()
+    gather[1].relay()
+    activity_gradient(0)
+    gather[1].relay_again()
+    branch(0)
+    gather[1].wait()
     hand_back.start()
-    spread.start()
-
-    @pl.loop(0, tiles)
-    def _(j):
-        at, up_at = span(j, 256), span(tiles + j, 256)
-        grad_gate[...] = dot_flipped(back[...], reduce[at, :])
-
-        @pl.loop(0, tokens // 64)
-        def _(i):
-            some = span(i, 64)
-            x, change = gate[some, at], grad_gate[some]
-            s = jax.nn.sigmoid(x)
-            hidden[some, at] = (change * up[some, at] * s * (1.0 + x * (1.0 - s))).astype(BF16)
-            hidden[some, up_at] = (change * (x * s)).astype(BF16)
-
+    activity_gradient(1)
     hand_hidden.start()
     get_raw.start()
-
-    def branch(j):
-        at = span(j, 256)
-        part[:, at] = dot_flipped(hidden[...], expand[at, :]).astype(BF16)
-
-    pl.loop(n, 2 * n)(branch)
-    scatter[2].start_right()
-    pl.loop(0, n)(branch)
-    scatter[2].start_left()
-
+    branch_scatter[0].middle()
+    branch(1)
+    spread.start()
     hand_act.wait()
     hand_back.wait()
     halves = [pl.ds(side * (width // 2), width // 2) for side in range(2)]
@@ -987,7 +1104,8 @@
 
     pl.semaphore_signal(free.at[0], inc=1, device_id={"dp": 1 - dp}, device_id_type=MESH)
     reduce_sum.start()
-    scatter[2].middle()
+    branch_scatter[0].end()
+    branch_scatter[1].middle()
     hand_rows.wait()
     hand_hidden.wait()
 
@@ -999,13 +1117,13 @@
     pl.semaphore_signal(free.at[1], inc=1, device_id={"dp": 1 - dp}, device_id_type=MESH)
     expand_sum.start()
     reduce_sum.over_z()
-    scatter[2].end()
+    branch_scatter[1].end()
     sums[...] = jnp.zeros_like(sums)
 
     @pl.loop(0, share // 16)
     def _(i):
         at = span(i, 16)
-        grad = g[at].astype(F32) + scatter[2].total[at]
+        grad = g[at].astype(F32) + merge_scatter.total[at]
         grad_resid[at] = grad
         hat, change = back_of(grad, merged[at], gain_merge[...])
         new_rows[pl.ds(pl.multiple_of(row * share + i * 16, 16), 16), :] = change.astype(BF16)
@@ -1016,8 +1134,6 @@
     gains[2:3] = jnp.sum(sums[...], axis=0, keepdims=True)
     get_xs.wait()
     pl.loop(0, 2 * tiles)(turn_rows)
-    pl.semaphore_wait(free.at[1], 1)
-    hand_xs.start()
     last_gather.relay()
     last_gather.relay_again()
     get_raw.wait()
@@ -1025,7 +1141,10 @@
     mix_turned[...] = mix[...].T
     hand_mix.start()
     expand_sum.over_z()
-    scatter[2].finish()
+    pl.semaphore_wait(free.at[1], 1)
+    hand_xs.start()
+    for m in range(2):
+        branch_scatter[m].finish()
     last_gather.wait()
     pl.semaphore_wait(free.at[0], 1)
     hand_new.start()
@@ -1051,6 +1170,8 @@
             heads_change[key_at, key] += dot(grad_scores.T, qkv[query_at, query]) * HD**-0.5
             heads_change[key_at, value] += dot(shares.T, change)
 
+    joined[:, 2 * head_width :] = heads_change[:, 2 * head_width :].astype(BF16)
+    hand_values.start()
     reduce_sum.over_y()
     sums[...] = jnp.zeros_like(sums)
 
@@ -1082,7 +1203,17 @@
             dot(mix_turned[mine, :], back[:, wide]) + dot(mix_other[...], back_other[:, wide])
         ).astype(BF16)
     merge_sum.start()
-    joined[:, 2 * head_width :] = heads_change[:, 2 * head_width :].astype(BF16)
+    hand_values.wait()
+    hand_xs.wait()
+
+    @pl.loop(0, tiles)
+    def _(j):
+        two(
+            values_part, span(j, 256), pl.ds(0, head_width), turned, span(dp * tiles + j, 256), joined.at[:, values_at],
+            turned_other, joined_other.at[:, values_at],
+        )
+
+    values_sum.start()
     token_sums.end()
 
     @pl.loop(0, tokens // 64)
@@ -1096,6 +1227,21 @@
             joined[at, some] = (rate * (heads_change[at, some] - hat * dots[:, j : j + 1])).astype(BF16)
 
     hand_joined.start()
+    def input_part(j):
+        at = span(j, 256)
+        part[:, at] = dot_flipped(joined[...], heads[at, :]).astype(BF16)
+
+    pl.loop(first_right, 2 * n)(input_part)
+    input_scatter.start_right()
+    pl.loop(0, first_right)(input_part)
+    input_scatter.start_left()
+    hand_joined.wait()
+
+    @pl.loop(0, tiles)
+    def _(j):
+        two(heads, span(j, 256), others_at, turned, span(dp * tiles + j, 256), joined, turned_other, joined_other)
+
+    heads_sum.start()
     for copy in row_gains:
         copy.wait()
     gain_row[row] = gains[...]
@@ -1106,33 +1252,18 @@
     gain_col[col] = total
     for copy in col_gains:
         copy.start()
-
-    def input_part(j):
-        at = span(j, 256)
-        part[:, at] = dot_flipped(joined[...], heads[at, :]).astype(BF16)
-
-    pl.loop(n, 2 * n)(input_part)
-    scatter[3].start_right()
-    pl.loop(0, n)(input_part)
-    scatter[3].start_left()
-
-    hand_xs.wait()
-    hand_joined.wait()
-    everything = pl.ds(0, 3 * head_width)
-
-    @pl.loop(0, tiles)
-    def _(j):
-        two(heads, span(j, 256), everything, turned, span(dp * tiles + j, 256), joined, turned_other, joined_other)
-
-    heads_sum.start()
+    values_sum.over_z()
+    input_scatter.middle()
+    merge_sum.over_z()
+    heads_sum.over_z()
+    reduce_sum.end()
     expand_sum.over_y()
-    merge_sum.over_z()
-    reduce_sum.end()
-    scatter[3].middle()
-    heads_sum.over_z()
-    scatter[3].end()
-    final[...] = (grad_resid[...] + scatter[3].total[...]).astype(BF16)
+    input_scatter.end()
+    final[...] = (grad_resid[...] + input_scatter.total[...]).astype(BF16)
     spread_grad.start()
+    values_sum.over_y()
+    merge_sum.over_y()
+    heads_sum.over_y()
     for copy in col_gains:
         copy.wait()
     total = gain_col[0]
@@ -1140,17 +1271,16 @@
         total = total + gain_col[k]
     gain_sum[1] = total
     core_gains.start()
-    merge_sum.over_y()
-    heads_sum.over_y()
     expand_sum.end()
+    values_sum.end()
     merge_sum.end()
     heads_sum.end()
     core_gains.wait()
     gains_grad[...] = gain_sum[1] + gain_core[...]
-    scatter[3].finish()
+    input_scatter.finish()
     spread.wait()
     spread_grad.wait()
-    for grad in (reduce_sum, expand_sum, merge_sum, heads_sum):
+    for grad in (reduce_sum, expand_sum, values_sum, merge_sum, heads_sum):
         grad.wait()
 
 
@@ -1243,66 +1373,32 @@
             pltpu.VMEM((seq_len, model_width), BF16),
             pltpu.VMEM((head_width // 2, seq_len), BF16),
             pltpu.VMEM((seq_len, 3 * head_width), BF16),
+            pltpu.VMEM((model_width // 2, head_width), BF16),
             pltpu.VMEM((seq_len, HD), F32),
             pltpu.VMEM((8, seq_len), F32),
             pltpu.VMEM((seq_len, HD), F32),
             pltpu.VMEM((seq_len, HD), F32),
             pltpu.SemaphoreType.REGULAR((2,)),
             DMA((8,)), DMA((3,)), DMA((3,)), DMA((8,)), DMA((8,)), DMA((8,)), DMA((8,)), DMA((15,)), DMA((15,)),
-            DMA((8,)), DMA((8,)), DMA((8,)), DMA((8,)), DMA((8,)), DMA((8,)),
+            DMA((9,)), DMA((9,)), DMA((8,)), DMA((8,)), DMA((8,)), DMA((8,)),
         ]
-        + gather_scratch() * 4
-        + scatter_scratch(share, model_width) + [DMA((14,))] * 6
+        + gather_scratch() * 6
+        + scatter_scratch(share, model_width) + [DMA((14,))] * 10
         + sums_scratch(seq_len) * 2
         + grad_sum_scratch(reduce_weight.shape) + grad_sum_scratch(expand_weight.shape)
-        + grad_sum_scratch(merge_weight.shape) + grad_sum_scratch(heads_weight.shape)
+        + grad_sum_scratch(merge_weight.shape)
+        + grad_sum_scratch((heads_weight.shape[0], head_width))
+        + grad_sum_scratch((heads_weight.shape[0], 2 * head_width))
         + bring_scratch() * 4,
     )[:7]
-    heads_grad, merge_grad, expand_grad, reduce_grad = (
-        heads_grad.astype(F32), merge_grad.astype(F32), expand_grad.astype(F32), reduce_grad.astype(F32)
-    )
-    heads_mean, heads_square, heads_fresh = adamw(
-        heads_weight, heads_grad, heads_first, heads_second, LR, DECAY
-    )
-    merge_mean, merge_square, merge_fresh = adamw(
-        merge_weight, merge_grad, merge_first, merge_second, LR, DECAY
-    )
-    expand_mean, expand_square, expand_fresh = adamw(
-        expand_weight, expand_grad, expand_first, expand_second, LR, DECAY
-    )
-    reduce_mean, reduce_square, reduce_fresh = adamw(
-        reduce_weight, reduce_grad, reduce_first, reduce_second, LR, DECAY
-    )
-    gains_mean, gains_square, gains_fresh = adamw(
-        norm_gains, gains_grad, gains_first, gains_second, LR_GAIN, 0.0
-    )
-    return (
+    return update(
         block_output,
-        input_grad.astype(F32),
-        heads_grad,
-        heads_mean,
-        heads_square,
-        heads_fresh,
-        heads_fresh.astype(jnp.bfloat16),
-        merge_grad,
-        merge_mean,
-        merge_square,
-        merge_fresh,
-        merge_fresh.astype(jnp.bfloat16),
-        expand_grad,
-        expand_mean,
-        expand_square,
-        expand_fresh,
-        expand_fresh.astype(jnp.bfloat16),
-        reduce_grad,
-        reduce_mean,
-        reduce_square,
-        reduce_fresh,
-        reduce_fresh.astype(jnp.bfloat16),
-        gains_grad,
-        gains_mean,
-        gains_square,
-        gains_fresh,
+        input_grad,
+        (heads_grad, heads_weight, heads_first, heads_second),
+        (merge_grad, merge_weight, merge_first, merge_second),
+        (expand_grad, expand_weight, expand_first, expand_second),
+        (reduce_grad, reduce_weight, reduce_first, reduce_second),
+        (gains_grad, norm_gains, gains_first, gains_second),
     )
 
 

time: 271 us -> 263 us (0.970); the launches traced: 267 us -> 262 us
  other arithmetic: 15 us -> 0 us
  Pallas kernels: 249 us -> 261 us
    convert_element_type x5 -> x0, other arithmetic: 14.3 us -> none  [the longest x1 7.91 us: on_device(): expand_fresh.astype(jnp.bfloat16)]
    pallas_call x0 -> x1, Pallas kernels: none -> 13.7 us  [update(): pl.pallas_call(update_kernel, name='update', grid=(UPDATE_STEPS,), out_sh...]
where the time goes in v7:
time: 263 us; the launch traced here: 262 us
  Pallas kernels  261 us (99%)
    pallas_call x1, Pallas kernels, call(): pl.pallas_call(kernel, name=name, out_shape=outs, in_specs=in_specs, out_...  248 us
    pallas_call x1, Pallas kernels, update(): pl.pallas_call(update_kernel, name='update', grid=(UPDATE_STEPS,), out_sh...  13.7 us

profile of v7, /device:TPU:9, one launch (start us, length us, event | category | flops | bytes accessed | tf_op | source)
XLA Modules:
  0.0 262.2 jit_solution(12628135212326617244)
XLA Ops:
  0.7 247.7 %layer.1 = (bf16[512,256]{1,0:T(8,128)(2,1)}, bf16[512,256]{1,0:T(8,128)(2,1)}, f32[4,2048]{1,0:T(4,128)}, bf16[256,768]{1,0:T(8,128)(2,1)}, bf16[256,256]{1,0:T...) custom-call(bf16[512,256]{1,0:T(8,128)(2,1)} %x.1, ...), custom_call_target="tpu_custom_call" | custom-call | tf_op jit(solution)/shard_map/layer/pallas_call | solution.py:177
  248.4 13.7 %update.1 = (bf16[512,256]{1,0:T(8,128)(2,1)}, f32[512,256]{1,0:T(8,128)}, f32[256,768]{1,0:T(8,128)}, f32[256,768]{1,0:T(8,128)}, f32[256,768]{1,0:T(8,128)}, /...) custom-call(bf16[512,256]{1,0:T(8,128)(2,1)} %get-tuple-element.33.r, ...), custom_call_target="tpu_custom_call" | custom-call | tf_op jit(solution)/shard_map/update/pallas_call | solution.py:697

commit v8 on v7

--- a/solution.py
+++ b/solution.py
@@ -118,40 +118,46 @@
     pl.semaphore_wait(barrier, count)
 
 
-class Spread:
-    def __init__(self, inward, source, target, sent, arrived):
+class Exchange:
+    def __init__(self, first, second, source, middle, target, sent, arrived):
         dp, row, col = here()
-        self.row, self.col, self.inward = row, col, inward
+        a, b = (row, col) if first == "row" else (col, row)
+        self.keep = pltpu.make_async_copy(source(a), middle.at[a], sent.at[7])
         self.copies = []
-        for k in range(8):
-            to_row, to_col = (k, row) if inward else (col, k)
-            mine = (row == to_row) & (col == to_col)
-            copy = remote(
-                source(k),
-                target(col if inward else row),
-                sent.at[k],
-                arrived.at[col if inward else row],
-                row=to_row,
-                col=to_col,
+        for d in range(1, 8):
+            k = (a + d) % 8
+            self.copies.append(remote(source(k), middle.at[a], sent.at[d - 1], arrived.at[d - 1], **{first: k}))
+        self.passed = []
+        for j in range(8):
+            self.passed.append(
+                (
+                    b == j,
+                    remote(middle.at[j], target(b), sent.at[8 + j], arrived.at[7 + b], **{second: j}),
+                    remote(middle.at[j], target(j), sent.at[8 + j], arrived.at[7 + j], **{second: j}),
+                    pltpu.make_async_copy(middle.at[j], target(b), sent.at[8 + j]),
+                )
             )
-            waiter = remote(source(k), target(k), sent.at[k], arrived.at[k], row=to_row, col=to_col)
-            local = pltpu.make_async_copy(
-                source(k), target(col if inward else row), sent.at[k]
-            )
-            self.copies.append((mine, copy, waiter, local))
 
     def start(self):
-        for mine, copy, _, local in self.copies:
+        self.keep.start()
+        for copy in self.copies:
+            copy.start()
+
+    def relay(self):
+        self.keep.wait()
+        for copy in self.copies:
+            copy.wait_recv()
+        for mine, copy, _, local in self.passed:
             pl.when(jnp.logical_not(mine))(copy.start)
             pl.when(mine)(local.start)
 
     def wait(self):
-        for k, (mine, copy, waiter, local) in enumerate(self.copies):
-            from_row, from_col = (self.col, k) if self.inward else (k, self.row)
-            me = (from_row == self.row) & (from_col == self.col)
-            pl.when(jnp.logical_not(me))(waiter.wait_recv)
+        for mine, copy, came, local in self.passed:
+            pl.when(jnp.logical_not(mine))(came.wait_recv)
             pl.when(jnp.logical_not(mine))(copy.wait_send)
             pl.when(mine)(local.wait)
+        for copy in self.copies:
+            copy.wait_send()
 
 
 def half_of(kind, ref, c, h):
@@ -712,7 +718,7 @@
     rows, turned, expand, reduce, heads, merge, gate, up, act, act_turned, part, back, hidden, probs, mix, mix_turned,
     rates, stats, grad_mix, done, final, grad_resid, merged, residual, g, sums, grad_gate,
     gains, gain_row, gain_col, gain_core, gain_sum, act_other, turned_other, hidden_other, back_other, mix_other,
-    joined_other, values_part, docs, doc_row, cosine, sine, free, load, keep, late, osent, ocame, isent, icame, nsent, ncame, xsent, xcame,
+    joined_other, values_part, exchanged, docs, doc_row, cosine, sine, free, load, keep, late, osent, ocame, isent, icame, nsent, ncame, xsent, xcame,
     asent, acame, bsent, bcame, g1sent, g1came, g2sent, g2came, g3sent, g3came, g4sent, g4came, g5sent, g5came, g6sent, g6came, *refs,
 ):
     dp, row, col = here()
@@ -768,9 +774,15 @@
     spread_x = SpreadIn(
         lambda k: rows_of(x, k, share), lambda k, c: back.at[span(k, share), span(c, 256)], asent, acame
     )
-    spread_g = SpreadIn(lambda k: rows_of(g_in, k, share), lambda k, c: g.at[:, span(c, 256)], bsent, bcame)
-    spread = Spread(False, lambda k: cols(done, k, 256), lambda k: rows_of(out, k, 64), osent, ocame)
-    spread_grad = Spread(False, lambda k: cols(final, k, 256), lambda k: rows_of(input_grad, k, 64), isent, icame)
+    spread_g = Exchange(
+        "row", "col", lambda k: rows_of(g_in, k, share), exchanged.at[0], lambda k: g.at[:, span(k, 256)], bsent, bcame
+    )
+    spread = Exchange(
+        "col", "row", lambda k: cols(done, k, 256), exchanged.at[1], lambda k: rows_of(out, k, 64), osent, ocame
+    )
+    spread_grad = Exchange(
+        "col", "row", lambda k: cols(final, k, 256), exchanged.at[2], lambda k: rows_of(input_grad, k, 64), isent, icame
+    )
     row_gains = [
         remote(gains, gain_row.at[row], nsent.at[d - 1], ncame.at[d - 1], row=row_peer(row, d))
         for d in range(1, 8)
@@ -838,7 +850,7 @@
             dot(own[own_at, :], right[:, wide]) + dot(other[at, :], right_other[:, wide])
         ).astype(BF16)
 
-    meet(rows=True, cols=True, core=True, spread_in=True, spread_out=True)
+    meet(rows=True, cols=True, core=True, spread_in=True)
     spread_x.start()
     narrow(0, bring_heads.place)
     bring_heads.start_y()
@@ -897,7 +909,6 @@
     bring_expand.relay()
     bring_reduce.relay()
     first_sums.end()
-    spread_g.start()
 
     @pl.loop(0, tokens // 64)
     def _(i):
@@ -972,6 +983,7 @@
     row_gather[1].relay()
     bring_reduce.hand_over()
     row_gather[0].wait()
+    spread_g.start()
     row_gather[1].relay_again()
     merge_scatter.finish()
     bring_expand.wait()
@@ -1049,6 +1061,7 @@
 
     gated(0)
     bring_reduce.wait()
+    spread_g.relay()
     reduced(0)
     row_gather[1].wait()
     gated(1)
@@ -1072,6 +1085,7 @@
     reduced_scatter[1].end()
     output_norm(1)
     gather[1].start()
+    spread.start()
     gather[0].relay_again()
     gains[...] = jnp.zeros_like(gains)
     gains[3:4] = jnp.sum(sums[...], axis=0, keepdims=True)
@@ -1092,30 +1106,43 @@
     get_raw.start()
     branch_scatter[0].middle()
     branch(1)
-    spread.start()
     hand_act.wait()
     hand_back.wait()
-    halves = [pl.ds(side * (width // 2), width // 2) for side in range(2)]
-
-    @pl.loop(0, tiles // 2)
+    quarter_width = width // 4
+    z_far = (col // 2 + 2) % 4
+
+    def reduce_tile(k):
+        two(
+            reduce, pl.ds(0, half_units), span(k, quarter_width), act_turned, span(dp, half_units), back, act_other,
+            back_other,
+        )
+
+    reduce_tile(z_far)
+    reduce_sum.start()
+
+    @pl.loop(1, 4)
     def _(j):
-        for wide in halves:
-            two(reduce, span(j, 256), wide, act_turned, span(dp * (tiles // 2) + j, 256), back, act_other, back_other)
+        reduce_tile((z_far + j) % 4)
 
     pl.semaphore_signal(free.at[0], inc=1, device_id={"dp": 1 - dp}, device_id_type=MESH)
-    reduce_sum.start()
     branch_scatter[0].end()
     branch_scatter[1].middle()
     hand_rows.wait()
     hand_hidden.wait()
-
-    @pl.loop(0, tiles)
+    halves = [pl.ds(side * (width // 2), width // 2) for side in range(2)]
+
+    def expand_tile(k):
+        for wide in halves:
+            two(expand, span(k, 256), wide, turned, span(dp * tiles + k, 256), hidden, turned_other, hidden_other)
+
+    expand_tile(z_far)
+    expand_sum.start()
+
+    @pl.loop(1, 4)
     def _(j):
-        for wide in halves:
-            two(expand, span(j, 256), wide, turned, span(dp * tiles + j, 256), hidden, turned_other, hidden_other)
+        expand_tile((z_far + j) % 4)
 
     pl.semaphore_signal(free.at[1], inc=1, device_id={"dp": 1 - dp}, device_id_type=MESH)
-    expand_sum.start()
     reduce_sum.over_z()
     branch_scatter[1].end()
     sums[...] = jnp.zeros_like(sums)
@@ -1149,6 +1176,7 @@
     pl.semaphore_wait(free.at[0], 1)
     hand_new.start()
 
+    spread.relay()
     live = (docs[:, 0:1] < 5.0).astype(F32)
     grad_mix[...] = (dot_flipped(new_rows[...], merge[...]) * live).astype(BF16)
     heads_change[:, head_width:] = jnp.zeros((tokens, 2 * head_width), F32)
@@ -1237,11 +1265,16 @@
     input_scatter.start_left()
     hand_joined.wait()
 
-    @pl.loop(0, tiles)
+    def heads_tile(k):
+        two(heads, span(k, 256), others_at, turned, span(dp * tiles + k, 256), joined, turned_other, joined_other)
+
+    heads_tile(z_far)
+    heads_sum.start()
+
+    @pl.loop(1, 4)
     def _(j):
-        two(heads, span(j, 256), others_at, turned, span(dp * tiles + j, 256), joined, turned_other, joined_other)
-
-    heads_sum.start()
+        heads_tile((z_far + j) % 4)
+
     for copy in row_gains:
         copy.wait()
     gain_row[row] = gains[...]
@@ -1252,8 +1285,8 @@
     gain_col[col] = total
     for copy in col_gains:
         copy.start()
+    input_scatter.middle()
     values_sum.over_z()
-    input_scatter.middle()
     merge_sum.over_z()
     heads_sum.over_z()
     reduce_sum.end()
@@ -1271,6 +1304,7 @@
         total = total + gain_col[k]
     gain_sum[1] = total
     core_gains.start()
+    spread_grad.relay()
     expand_sum.end()
     values_sum.end()
     merge_sum.end()
@@ -1374,13 +1408,14 @@
             pltpu.VMEM((head_width // 2, seq_len), BF16),
             pltpu.VMEM((seq_len, 3 * head_width), BF16),
             pltpu.VMEM((model_width // 2, head_width), BF16),
+            pltpu.VMEM((3, 8, share, block_input.shape[1]), BF16),
             pltpu.VMEM((seq_len, HD), F32),
             pltpu.VMEM((8, seq_len), F32),
             pltpu.VMEM((seq_len, HD), F32),
             pltpu.VMEM((seq_len, HD), F32),
             pltpu.SemaphoreType.REGULAR((2,)),
-            DMA((8,)), DMA((3,)), DMA((3,)), DMA((8,)), DMA((8,)), DMA((8,)), DMA((8,)), DMA((15,)), DMA((15,)),
-            DMA((9,)), DMA((9,)), DMA((8,)), DMA((8,)), DMA((8,)), DMA((8,)),
+            DMA((8,)), DMA((3,)), DMA((3,)), DMA((16,)), DMA((15,)), DMA((16,)), DMA((15,)), DMA((15,)), DMA((15,)),
+            DMA((9,)), DMA((9,)), DMA((8,)), DMA((8,)), DMA((16,)), DMA((15,)),
         ]
         + gather_scratch() * 6
         + scatter_scratch(share, model_width) + [DMA((14,))] * 10

time: 263 us -> 249 us (0.947)
  Pallas kernels: 261 us -> 246 us
    pallas_call x1, Pallas kernels: 248 us -> 233 us  [call(): pl.pallas_call(kernel, name=name, out_shape=outs, in_specs=in_specs, out_...]
where the time goes in v8:
time: 249 us; the launch traced here: 247 us
  Pallas kernels  246 us (99%)
    pallas_call x1, Pallas kernels, call(): pl.pallas_call(kernel, name=name, out_shape=outs, in_specs=in_specs, out_...  233 us
    pallas_call x1, Pallas kernels, update(): pl.pallas_call(update_kernel, name='update', grid=(UPDATE_STEPS,), out_sh...  13.7 us

profile of v8, /device:TPU:9, one launch (start us, length us, event | category | flops | bytes accessed | tf_op | source)
XLA Modules:
  0.0 247.2 jit_solution(11911777122078001221)
XLA Ops:
  0.7 232.7 %layer.1 = (bf16[512,256]{1,0:T(8,128)(2,1)}, bf16[512,256]{1,0:T(8,128)(2,1)}, f32[4,2048]{1,0:T(4,128)}, bf16[256,768]{1,0:T(8,128)(2,1)}, bf16[256,256]{1,0:T...) custom-call(bf16[512,256]{1,0:T(8,128)(2,1)} %x.1, ...), custom_call_target="tpu_custom_call" | custom-call | tf_op jit(solution)/shard_map/layer/pallas_call | solution.py:183
  233.4 13.7 %update.1 = (bf16[512,256]{1,0:T(8,128)(2,1)}, f32[512,256]{1,0:T(8,128)}, f32[256,768]{1,0:T(8,128)}, f32[256,768]{1,0:T(8,128)}, f32[256,768]{1,0:T(8,128)}, /...) custom-call(bf16[512,256]{1,0:T(8,128)(2,1)} %get-tuple-element.33.r, ...), custom_call_target="tpu_custom_call" | custom-call | tf_op jit(solution)/shard_map/update/pallas_call | solution.py:703

commit v9 on v8

--- a/solution.py
+++ b/solution.py
@@ -22,7 +22,7 @@
 ADAM_EPS = 1e-08
 
 BF16 = jnp.bfloat16
-SCATTER_LEFT, GATHER_LEFT, INPUT_LEFT = 8, 9, 16
+SCATTER_LEFT, GATHER_LEFT, INPUT_LEFT = 8, 8, 16
 F32 = jnp.float32
 MESH = pl.DeviceIdType.MESH
 ANY = pl.BlockSpec(memory_space=pl.ANY)

time: 249 us -> 249 us (level)
  no operation moved by 1% of the time
where the time goes in v9:
time: 249 us; the launch traced here: 246 us
  Pallas kernels  245 us (98%)
    pallas_call x1, Pallas kernels, call(): pl.pallas_call(kernel, name=name, out_shape=outs, in_specs=in_specs, out_...  232 us
    pallas_call x1, Pallas kernels, update(): pl.pallas_call(update_kernel, name='update', grid=(UPDATE_STEPS,), out_sh...  13.7 us

profile of v9, /device:TPU:9, one launch (start us, length us, event | category | flops | bytes accessed | tf_op | source)
XLA Modules:
  0.0 246.2 jit_solution(12703570507718170037)
XLA Ops:
  0.7 231.7 %layer.1 = (bf16[512,256]{1,0:T(8,128)(2,1)}, bf16[512,256]{1,0:T(8,128)(2,1)}, f32[4,2048]{1,0:T(4,128)}, bf16[256,768]{1,0:T(8,128)(2,1)}, bf16[256,256]{1,0:T...) custom-call(bf16[512,256]{1,0:T(8,128)(2,1)} %x.1, ...), custom_call_target="tpu_custom_call" | custom-call | tf_op jit(solution)/shard_map/layer/pallas_call | solution.py:183
  232.3 13.7 %update.1 = (bf16[512,256]{1,0:T(8,128)(2,1)}, f32[512,256]{1,0:T(8,128)}, f32[256,768]{1,0:T(8,128)}, f32[256,768]{1,0:T(8,128)}, f32[256,768]{1,0:T(8,128)}, /...) custom-call(bf16[512,256]{1,0:T(8,128)(2,1)} %get-tuple-element.33.r, ...), custom_call_target="tpu_custom_call" | custom-call | tf_op jit(solution)/shard_map/update/pallas_call | solution.py:703
